TPU v7x, 32 devices: a whole 2x2x4 slice. The times are simulated.
32 devices in a mesh: groups: 2 (over x), row: 16 (over z, y, core).
Axes of the slice: x: 2, y: 2, z: 4, core: 2. Of those that a mesh axis runs over, the one named last changes fastest.
Arguments:
- orbitals: bfloat16 [4096, 512], P(('groups', 'row')), parts along dimension 0, may hold values from -1.296875 to 1.296875
- basis: bfloat16 [4096, 1024], P(('groups', 'row')), parts along dimension 0, may hold values from -0.1875 to 0.1875
- kernel: bfloat16 [4096, 2048], P(('groups', 'row')), parts along dimension 0, may hold values from -6 to 6
Outputs:
- exchange_matrix: float32 [2048, 1024], P('groups', 'row'), parts along dimension 0
There are 2 independent parts, one for each index of `groups`. A program takes and returns all parts, laid end to end along the dimension named above; each array names one. Nothing has to cross between parts.
All inputs are finite; a program needn't handle non-finite values.
Results may differ from a plain program's by a relative error of at most 0.0041.
Values may be sent and summed in bfloat16 or wider, within the bound.
No kernel may reach another device: no remote copies, remote signals or barrier semaphores. Data moves between devices by JAX's collectives and lax.ppermute only.
A program may use at most 128 MiB of HBM per device.

v0:
```python
import jax
import jax.numpy as jnp
from jax import lax
from jax.sharding import PartitionSpec as P


def shards(orbitals, basis, kernel):
    density = lax.dot_general(
        orbitals,
        lax.all_gather(orbitals, "row", axis=0, tiled=True),
        (((1,), (1,)), ((), ())),
        preferred_element_type=jnp.float32,
    )
    weighted = (density * kernel.astype(jnp.float32)).astype(jnp.bfloat16)
    whole_basis = lax.all_gather(basis, "row", axis=0, tiled=True)
    applied = jnp.dot(weighted, whole_basis, preferred_element_type=jnp.float32).astype(
        jnp.bfloat16
    )
    received = lax.all_to_all(applied, "row", split_axis=1, concat_axis=0, tiled=True)
    exchange_matrix = lax.dot_general(
        whole_basis, received, (((0,), (0,)), ((), ())), preferred_element_type=jnp.float32
    )
    return exchange_matrix


def solution(mesh):
    return jax.shard_map(
        shards,
        mesh=mesh,
        in_specs=(
            P(("groups", "row"), None),
            P(("groups", "row"), None),
            P(("groups", "row"), None),
        ),
        out_specs=P("groups", "row"),
        check_vma=False,
    )
```

profile of v0, /device:TPU:0, one launch (start us, length us, event | category | flops | bytes accessed | tf_op | source)
XLA Modules:
  0.0 133.5 jit_solution(10812226006285130068)
XLA Ops:
  6.5 0.0 all-gather.3.cloned.1.call-start
  6.5 0.7 all-gather.3.cloned.1.call-update
  7.3 0.0 all-gather.5.cloned.1.call-start
  7.3 0.7 all-gather.5.cloned.1.call-update
  8.0 45.6 %all-gather.3.cloned.1.call-done = bf16[2048,512]{1,0:T(8,128)(2,1)} async-done(((bf16[128,512]{1,0:T(8,128)(2,1)}), bf16[2048,512]{1,0:T(8,128)(2,1)}) %all-gather.3.cloned.1.call-update) | async-done | bytes 2097168 | tf_op jit(solution)/shard_map/all_gather | solution.py:10
  53.7 51.7 %all-gather.5.cloned.1.call-done = bf16[2048,1024]{1,0:T(8,128)(2,1)} async-done(((bf16[128,1024]{1,0:T(8,128)(2,1)}), bf16[2048,1024]{1,0:T(8,128)(2,1)}) %all-gather.5.cloned.1.call-update) | async-done | bytes 4194320 | tf_op jit(solution)/shard_map/all_gather | solution.py:15
  105.3 4.4 %convolution_convert_fusion = bf16[128,1024]{1,0:T(8,128)(2,1)S(1)} fusion(bf16[2048,1024]{1,0:T(8,128)(2,1)} %all-gather.5.cloned.1.call-done, bf16[128,512]{1,0:T(8,128)(2,1)} %param.3, bf16[2048,512]{1,0:T(8,128)(2,1)} %all-gather.3.cloned.1.call-done, bf16[128,2048]{1,0:T(8,128)(2,1)} %param.5), kind=kOutput, calls=%fused_computation.2 | convolution fusion | flops 806223872 | bytes 7208960 | tf_op jit(solution)/shard_map/dot_general | solution.py:16
  109.7 0.2 copy.4
  109.9 13.0 %all_to_all.19 = bf16[128,16,64]{0,2,1:T(8,128)(2,1)S(1)} all-to-all(bf16[128,16,64]{0,2,1:T(8,128)(2,1)S(1)} %bitcast.15), channel_id=1, replica_groups=mesh['groups'=2,'row'=16] {'row'}, dimensions={1} | all-to-all | bytes 524288 | tf_op jit(solution)/shard_map/all_to_all | solution.py:19
  123.0 3.7 %convolution_bitcast_fusion = f32[1024,64]{0,1:T(8,128)} fusion(bf16[2048,1024]{1,0:T(8,128)(2,1)} %all-gather.5.cloned.1.call-done, bf16[128,16,64]{0,2,1:T(8,128)(2,1)S(1)} %all_to_all.19), kind=kOutput, calls=%fused_computation.3 | convolution fusion | flops 268435456 | bytes 4718592 | tf_op jit(solution)/shard_map/dot_general | solution.py:20
Async XLA Ops:
  6.5 47.1 %all-gather.3.cloned.1.call-start = ((), (), s32[]{:S(2)}) async-start(), calls=%async_computation.1 | async-start | bytes 2228224 | tf_op jit(solution)/shard_map/all_gather | solution.py:10
  7.3 98.1 %all-gather.5.cloned.1.call-start = ((), (), s32[]{:S(2)}) async-start(), calls=%async_computation.2 | async-start | bytes 4456448 | tf_op jit(solution)/shard_map/all_gather | solution.py:15
Sparse Core Ops, SparseCore 0:
  9.5 44.0 all-gather.2
  55.8 49.4 all-gather.4
where the time goes:
time: 134 us
  waiting for transfers between devices  98.7 us (74%)
  between operations  13.4 us (10%)
  blocking collectives  13 us (10%)
  matrix products  8.14 us (6%)
    all_gather x1, waiting for transfers between devices, shards(): whole_basis = lax.all_gather(basis, 'row', axis=0, tiled=True)  51.7 us
    all_gather x1, waiting for transfers between devices, shards(): lax.all_gather(orbitals, 'row', axis=0, tiled=True)  45.6 us
    all_to_all x1, blocking collectives, shards(): lax.all_to_all(applied, 'row', split_axis=1, concat_axis=0, tiled=True)  13 us
    dot_general x1, matrix products, shards(): jnp.dot(weighted, whole_basis, preferred_element_type=jnp.float32)  4.41 us
    dot_general x1, matrix products, shards(): lax.dot_general(whole_basis, received, (((0,), (0,)), ((), ())), preferre...  3.73 us
  transfers between devices with their start and end apart: 2, of which 2 were waited for; matrix products, arithmetic and copies ran while one was open for 0% of the time, Pallas kernels for 0%

commit v1 on v0

v1 whole, which is shorter than its diff:
```python
import functools

import jax
import jax.numpy as jnp
from jax import lax
from jax.experimental import pallas as pl
from jax.experimental.pallas import tpu as pltpu
from jax.sharding import PartitionSpec as P

QUAD = 4
F32, BF16 = jnp.float32, jnp.bfloat16


def dot(a, b, ca, cb):
    return lax.dot_general(a, b, (((ca,), (cb,)), ((), ())), preferred_element_type=F32)


def call(body, out_shape, args, flops, scalars=1, scratch=()):
    size = sum(a.size * a.dtype.itemsize for a in args) + sum(
        o.size * o.dtype.itemsize for o in out_shape
    )
    held = size + sum(s.shape[0] * s.shape[1] * 4 for s in scratch)
    in_specs = [pl.BlockSpec(memory_space=pltpu.SMEM)] * scalars
    in_specs += [pl.BlockSpec(memory_space=pltpu.VMEM)] * (len(args) - scalars)
    return pl.pallas_call(
        body,
        out_shape=list(out_shape),
        in_specs=in_specs,
        out_specs=[pl.BlockSpec(memory_space=pltpu.VMEM)] * len(out_shape),
        scratch_shapes=list(scratch),
        cost_estimate=pl.CostEstimate(flops=flops, bytes_accessed=size, transcendentals=0),
        compiler_params=pltpu.CompilerParams(vmem_limit_bytes=held + (16 << 20)),
    )(*args)


def pick_kernel(width, me_ref, b0, b1, b2, b3, x_ref):
    place = me_ref[0] % QUAD
    columns, share = b0.shape[1], x_ref.shape[1]
    k = lax.broadcasted_iota(jnp.int32, (columns, share), 0)
    m = lax.broadcasted_iota(jnp.int32, (columns, share), 1)
    chosen = (m // width) * (QUAD * width) + place * width + m % width
    picker = (k == chosen).astype(F32).astype(BF16)
    rows = b0.shape[0]
    for r, b in enumerate((b0, b1, b2, b3)):
        x_ref[r * rows : (r + 1) * rows, :] = dot(b[...], picker, 1, 0).astype(BF16)


def main_kernel(order, width, me_ref, *refs):
    nz = len(order)
    o, k, b = refs[0:4], refs[4:8], refs[8:12]
    x = refs[12 : 12 + nz]
    own_ref, outs, total = refs[12 + nz], refs[13 + nz : 12 + 2 * nz], refs[12 + 2 * nz]
    rows = k[0].shape[0]
    me = me_ref[0]
    zi, place = me // QUAD, me % QUAD
    o_rows = jnp.concatenate([r[0:rows, :] for r in o], axis=0)
    acc = None
    for i, m in enumerate(order):
        for pair in (0, 2):
            o_cols = jnp.concatenate([o[pair + c][i * rows : (i + 1) * rows, :] for c in (0, 1)], axis=0)
            density = dot(o_rows, o_cols, 1, 1)
            at = [
                pl.multiple_of(((zi ^ m) * QUAD + (place ^ (pair + c))) * rows, rows) for c in (0, 1)
            ]
            k_block = jnp.concatenate(
                [jnp.concatenate([kr[:, pl.ds(a, rows)] for a in at], axis=1) for kr in k], axis=0
            )
            weighted = (density * k_block.astype(F32)).astype(BF16)
            term = dot(weighted, x[i][pair * rows : (pair + 2) * rows, :], 1, 0)
            acc = term if acc is None else acc + term
    applied = acc.astype(BF16)
    b_all = jnp.concatenate([r[...] for r in b], axis=0)
    total[...] = dot(applied, b_all, 0, 0)
    for m in range(nz):
        part = total[pl.ds(pl.multiple_of((zi ^ m) * width, width), width), :]
        if m == 0:
            own_ref[...] = part
        else:
            outs[m - 1][...] = part.astype(BF16)


def shards(n, orbitals, basis, kernel):
    nz = n // QUAD
    me = lax.axis_index("row")
    where = jnp.full((1,), me, jnp.int32)
    rows, columns = basis.shape
    width = columns // n

    def swap(a, bit):
        return lax.ppermute(a, "row", [(i, i ^ bit) for i in range(n)])

    def along_z(a):
        held, order, step = [a], [0], nz // 2
        while step:
            held = held + [swap(h, QUAD * step) for h in held]
            order = order + [m + step for m in order]
            step //= 2
        return held, order

    b_y, b_c = swap(basis, 2), swap(basis, 1)
    b_yc = swap(b_y, 1)
    bs = (basis, b_c, b_y, b_yc)
    (x,) = call(
        functools.partial(pick_kernel, width),
        [jax.ShapeDtypeStruct((QUAD * rows, columns // QUAD), BF16)],
        (where, *bs),
        2 * QUAD * rows * columns * columns // QUAD,
    )
    xs, order = along_z(x)
    k_y, k_c = swap(kernel, 2), swap(kernel, 1)
    k_yc = swap(k_y, 1)
    held, _ = along_z(orbitals)
    o = jnp.concatenate(held, axis=0)
    o_y, o_c = swap(o, 2), swap(o, 1)
    o_yc = swap(o_y, 1)

    points = n * rows
    flops = 2 * QUAD * rows * (points * orbitals.shape[1] + points * columns // QUAD + columns * columns // QUAD)
    parts = call(
        functools.partial(main_kernel, tuple(order), width),
        [jax.ShapeDtypeStruct((width, columns), F32 if m == 0 else BF16) for m in range(nz)],
        (where, o, o_c, o_y, o_yc, kernel, k_c, k_y, k_yc, *bs, *xs),
        flops,
        scratch=(pltpu.VMEM((columns // QUAD, columns), F32),),
    )
    total = parts[0]
    for m in range(1, nz):
        total = total + swap(parts[m], QUAD * m).astype(F32)
    return total.T


def solution(mesh):
    rows = P(("groups", "row"), None)
    return jax.shard_map(
        functools.partial(shards, mesh.shape["row"]),
        mesh=mesh,
        in_specs=(rows, rows, rows),
        out_specs=P("groups", "row"),
        check_vma=False,
    )
```

time: 134 us -> 67.8 us (0.51)
  waiting for transfers between devices: 98.7 us -> 42 us
  starting transfers between devices: 0.04 us -> 19.9 us
  between operations: 13.4 us -> 0.07 us
  blocking collectives: 13 us -> 0 us
  matrix products: 8.14 us -> 0 us
  Pallas kernels: 0 us -> 3.95 us
    all_gather x2 -> x0, waiting for transfers between devices: 97.3 us -> none  [the longest x1 51.7 us: shards(): whole_basis = lax.all_gather(basis, 'row', axis=0, tiled=True)]
    ppermute x0 -> x18, waiting for transfers between devices: none -> 42 us  [swap(): return lax.ppermute(a, 'row', [(i, i ^ bit) for i in range(n)])]
    ppermute x0 -> x18, starting transfers between devices: none -> 19.9 us  [swap(): return lax.ppermute(a, 'row', [(i, i ^ bit) for i in range(n)])]
    all_to_all x1 -> x0, blocking collectives: 13 us -> none  [shards(): lax.all_to_all(applied, 'row', split_axis=1, concat_axis=0, tiled=True)]
    dot_general x2 -> x0, matrix products: 8.14 us -> none  [the longest x1 4.41 us: shards(): jnp.dot(weighted, whole_basis, preferred_element_type=jnp.float32)]
    pallas_call x0 -> x2, Pallas kernels: none -> 3.95 us  [call(): pl.pallas_call(body, out_shape=list(out_shape), in_specs=in_specs, out_sp...]
    unnamed x2 -> x0, waiting for transfers between devices: 1.41 us -> none
  transfers between devices with their start and end apart: 2 -> 18, of which waited for: 2 -> 10; matrix products, arithmetic and copies ran while one was open for 0% -> 1% of each run, Pallas kernels for 0% -> 1%
where the time goes in v1:
time: 67.8 us; the launch traced here: 67.6 us
  waiting for transfers between devices  42 us (62%)
  starting transfers between devices  19.9 us (29%)
  Pallas kernels  3.95 us (6%)
  local copies, waits for them, and re-layouts  0.95 us (1%)
  other arithmetic  0.76 us (1%)
    ppermute x18, waiting for transfers between devices, swap(): return lax.ppermute(a, 'row', [(i, i ^ bit) for i in range(n)])  42 us
    ppermute x18, starting transfers between devices, swap(): return lax.ppermute(a, 'row', [(i, i ^ bit) for i in range(n)])  19.9 us
    pallas_call x2, Pallas kernels, call(): pl.pallas_call(body, out_shape=list(out_shape), in_specs=in_specs, out_sp...  3.95 us
  transfers between devices with their start and end apart: 18, of which 10 were waited for; matrix products, arithmetic and copies ran while one was open for 1% of the time, Pallas kernels for 1%

profile of v1, /device:TPU:0, one launch (start us, length us, event | category | flops | bytes accessed | tf_op | source)
XLA Modules:
  0.0 67.6 jit_solution(11756498856166704014)
XLA Ops:
  0.0 4.0 %collective-permute-start = (bf16[128,512]{1,0:T(8,128)(2,1)}, bf16[128,512]{1,0:T(8,128)(2,1)S(1)}, u32[]{:S(2)}, u32[]{:S(2)}) collective-permute-start(bf16[128,512]{1,0:T(8,128)(2,1)} %param.3), channel_id=1, source_target_pairs={{0,8},{1,9},{2,10},{3,11},{4,12},{5,13},{6,14},{7,15},{8,0},{9,1},... | collective-permute-start | bytes 393224 | tf_op jit(solution)/shard_map/ppermute | solution.py:90
  4.0 1.6 %collective-permute-start.1 = (bf16[128,512]{1,0:T(8,128)(2,1)}, bf16[128,512]{1,0:T(8,128)(2,1)S(1)}, u32[]{:S(2)}, u32[]{:S(2)}) collective-permute-start(bf16[128,512]{1,0:T(8,128)(2,1)} %param.3), channel_id=1, source_target_pairs={{0,4},{1,5},{2,6},{3,7},{4,0},{5,1},{6,2},{7,3},{8,12},{9,13},{10,... | collective-permute-start | bytes 393224 | tf_op jit(solution)/shard_map/ppermute | solution.py:90
  5.6 1.5 %collective-permute-start.10 = (bf16[128,1024]{1,0:T(8,128)(2,1)}, bf16[128,1024]{1,0:T(8,128)(2,1)S(1)}, u32[]{:S(2)}, u32[]{:S(2)}) collective-permute-start(bf16[128,1024]{1,0:T(8,128)(2,1)} %refs_8_.1), channel_id=1, source_target_pairs={{0,2},{1,3},{2,0},{3,1},{4,6},{5,7},{6,4},{7,5},{8,10},{9,11},{10,... | collective-permute-start | bytes 786440 | tf_op jit(solution)/shard_map/ppermute | solution.py:90
  7.1 0.5 collective-permute-start.7
  7.6 0.9 %constant_dynamic-update-slice_fusion.3 = bf16[512,512]{1,0:T(8,128)(2,1)S(1)} fusion(bf16[128,512]{1,0:T(8,128)(2,1)} %param.3), kind=kLoop, calls=%fused_computation.4 | loop fusion | bytes 262144
  8.6 2.1 %collective-permute-done = bf16[128,512]{1,0:T(8,128)(2,1)S(1)} collective-permute-done((bf16[128,512]{1,0:T(8,128)(2,1)}, bf16[128,512]{1,0:T(8,128)(2,1)S(1)}, u32[]{:S(2)}, u32[]{:S(2)}) %collective-permute-start) | collective-permute-done | bytes 131104 | tf_op jit(solution)/shard_map/ppermute | solution.py:90
  10.7 0.7 %collective-permute-start.2 = (bf16[128,512]{1,0:T(8,128)(2,1)S(1)}, bf16[128,512]{1,0:T(8,128)(2,1)S(1)}, u32[]{:S(2)}, u32[]{:S(2)}) collective-permute-start(bf16[128,512]{1,0:T(8,128)(2,1)S(1)} %collective-permute-done), channel_id=1, source_target_pairs={{0,4},{1,5},{2,6},{3,7},{4,0},{5,1},{6,2},{7,3},{8,12},{9,13},{10,... | collective-permute-start | bytes 393224 | tf_op jit(solution)/shard_map/ppermute | solution.py:90
  11.4 4.2 %collective-permute-done.2 = bf16[128,512]{1,0:T(8,128)(2,1)S(1)} collective-permute-done((bf16[128,512]{1,0:T(8,128)(2,1)S(1)}, bf16[128,512]{1,0:T(8,128)(2,1)S(1)}, u32[]{:S(2)}, u32[]{:S(2)}) %collective-permute-start.2) | collective-permute-done | bytes 131104 | tf_op jit(solution)/shard_map/ppermute | solution.py:90
  15.6 1.6 %collective-permute-start.4 = (bf16[512,512]{1,0:T(8,128)(2,1)S(1)}, bf16[512,512]{1,0:T(8,128)(2,1)S(1)}, u32[]{:S(2)}, u32[]{:S(2)}) collective-permute-start(bf16[512,512]{1,0:T(8,128)(2,1)S(1)} %constant_dynamic-update-slice_fusion.refs_0_), channel_id=1, source_target_pairs={{0,2},{1,3},{2,0},{3,1},{4,6},{5,7},{6,4},{7,5},{8,10},{9,11},{10,... | collective-permute-start | bytes 1572872 | tf_op jit(solution)/shard_map/ppermute | solution.py:90
  17.3 0.5 collective-permute-start.11
  17.9 0.9 %collective-permute-done.9.b1.refs_9_ = bf16[128,1024]{1,0:T(8,128)(2,1)S(1)} collective-permute-done((bf16[128,1024]{1,0:T(8,128)(2,1)S(1)}, bf16[128,1024]{1,0:T(8,128)(2,1)S(1)}, u32[]{:S(2)}, u32[]{:S(2)}) %collective-permute-start.9) | collective-permute-done | bytes 262176 | tf_op jit(solution)/shard_map/ppermute | solution.py:90
  19.2 0.5 shard_map.37.refs_12_
  19.7 2.7 %collective-permute-start.12 = (bf16[512,256]{1,0:T(8,128)(2,1)S(1)}, bf16[512,256]{1,0:T(8,128)(2,1)S(1)}, u32[]{:S(2)}, u32[]{:S(2)}) collective-permute-start(bf16[512,256]{1,0:T(8,128)(2,1)S(1)} %shard_map.37.refs_12_), channel_id=1, source_target_pairs={{0,8},{1,9},{2,10},{3,11},{4,12},{5,13},{6,14},{7,15},{8,0},{9,1},... | collective-permute-start | bytes 786440 | tf_op jit(solution)/shard_map/ppermute | solution.py:90
  22.4 3.9 %collective-permute-done.7.refs_6_ = bf16[128,2048]{1,0:T(8,128)(2,1)S(1)} collective-permute-done((bf16[128,2048]{1,0:T(8,128)(2,1)}, bf16[128,2048]{1,0:T(8,128)(2,1)S(1)}, u32[]{:S(2)}, u32[]{:S(2)}) %collective-permute-start.7) | collective-permute-done | bytes 524320 | tf_op jit(solution)/shard_map/ppermute | solution.py:90
  26.3 9.5 %collective-permute-done.4.refs_2_ = bf16[512,512]{1,0:T(8,128)(2,1)S(1)} collective-permute-done((bf16[512,512]{1,0:T(8,128)(2,1)S(1)}, bf16[512,512]{1,0:T(8,128)(2,1)S(1)}, u32[]{:S(2)}, u32[]{:S(2)}) %collective-permute-start.4) | collective-permute-done | bytes 524320 | tf_op jit(solution)/shard_map/ppermute | solution.py:90
  36.2 1.6 %collective-permute-start.14 = (bf16[512,256]{1,0:T(8,128)(2,1)S(1)}, bf16[512,256]{1,0:T(8,128)(2,1)S(1)}, u32[]{:S(2)}, u32[]{:S(2)}) collective-permute-start(bf16[512,256]{1,0:T(8,128)(2,1)S(1)} %collective-permute-done.12.refs_13_), channel_id=1, source_target_pairs={{0,4},{1,5},{2,6},{3,7},{4,0},{5,1},{6,2},{7,3},{8,12},{9,13},{10,... | collective-permute-start | bytes 786440 | tf_op jit(solution)/shard_map/ppermute | solution.py:90
  37.8 7.1 %collective-permute-done.13.refs_14_ = bf16[512,256]{1,0:T(8,128)(2,1)S(1)} collective-permute-done((bf16[512,256]{1,0:T(8,128)(2,1)S(1)}, bf16[512,256]{1,0:T(8,128)(2,1)S(1)}, u32[]{:S(2)}, u32[]{:S(2)}) %collective-permute-start.13) | collective-permute-done | bytes 262176 | tf_op jit(solution)/shard_map/ppermute | solution.py:90
  44.9 5.2 %collective-permute-done.14.refs_15_ = bf16[512,256]{1,0:T(8,128)(2,1)S(1)} collective-permute-done((bf16[512,256]{1,0:T(8,128)(2,1)S(1)}, bf16[512,256]{1,0:T(8,128)(2,1)S(1)}, u32[]{:S(2)}, u32[]{:S(2)}) %collective-permute-start.14) | collective-permute-done | bytes 262176 | tf_op jit(solution)/shard_map/ppermute | solution.py:90
  50.1 3.5 %shard_map.38 = (f32[64,1024]{1,0:T(8,128)S(1)}, bf16[64,1024]{1,0:T(8,128)(2,1)S(1)}, bf16[64,1024]{1,0:T(8,128)(2,1)S(1)}, bf16[64,1024]{1,0:T(8,128)(2,1)S(1)}) custom-call(s32[1]{0:T(128)} %bitcast.me_ref, bf16[512,512]{1,0:T(8,128)(2,1)S(1)} %constant_dynamic-update-slice_fusion.refs_0_, bf16[512,512]{1,0:T(8,128)(2,1)S(1)} %collective-permute-done.3.refs_1_, ...), custom_call_target="tpu_custom_call" | custom-call | flops 1879048192 | bytes 6946820 | tf_op jit(solution)/shard_map/pallas_call | solution.py:25
  53.6 0.5 collective-permute-start.15
  54.5 3.6 %collective-permute-start.17 = (bf16[64,1024]{1,0:T(8,128)(2,1)S(1)}, bf16[64,1024]{1,0:T(8,128)(2,1)S(1)}, u32[]{:S(2)}, u32[]{:S(2)}) collective-permute-start(bf16[64,1024]{1,0:T(8,128)(2,1)S(1)} %get-tuple-element.12), channel_id=1, source_target_pairs={{0,12},{1,13},{2,14},{3,15},{4,8},{5,9},{6,10},{7,11},{8,4},{9,5},... | collective-permute-start | bytes 393224 | tf_op jit(solution)/shard_map/ppermute | solution.py:90
  58.1 2.3 %collective-permute-done.15 = bf16[64,1024]{1,0:T(8,128)(2,1)S(1)} collective-permute-done((bf16[64,1024]{1,0:T(8,128)(2,1)S(1)}, bf16[64,1024]{1,0:T(8,128)(2,1)S(1)}, u32[]{:S(2)}, u32[]{:S(2)}) %collective-permute-start.15) | collective-permute-done | bytes 131104 | tf_op jit(solution)/shard_map/ppermute | solution.py:90
  60.4 6.5 %collective-permute-done.16 = bf16[64,1024]{1,0:T(8,128)(2,1)S(1)} collective-permute-done((bf16[64,1024]{1,0:T(8,128)(2,1)S(1)}, bf16[64,1024]{1,0:T(8,128)(2,1)S(1)}, u32[]{:S(2)}, u32[]{:S(2)}) %collective-permute-start.16) | collective-permute-done | bytes 131104 | tf_op jit(solution)/shard_map/ppermute | solution.py:90
  66.8 0.8 %add_bitcast_fusion = f32[1024,64]{0,1:T(8,128)} fusion(bf16[64,1024]{1,0:T(8,128)(2,1)S(1)} %collective-permute-done.17, bf16[64,1024]{1,0:T(8,128)(2,1)S(1)} %collective-permute-done.16, f32[64,1024]{1,0:T(8,128)S(1)} %get-tuple-element.9, bf16[64,1024]{1,0:T(8,128)(2,1)S(1)} %collective-permute-done.15), kind=kLoop, calls=%fused_computation | loop fusion | flops 393216 | bytes 917504 | tf_op jit(solution)/shard_map/transpose | solution.py:129
  (23 shorter events, 1.3 us)
Async XLA Ops:
  0.0 17.8 %copy-start.1 = (bf16[128,2048]{1,0:T(8,128)(2,1)S(1)}, bf16[128,2048]{1,0:T(8,128)(2,1)}, u32[]{:S(2)}) copy-start(bf16[128,2048]{1,0:T(8,128)(2,1)} %refs_4_.1) | copy-start | bytes 1572868
  0.0 10.7 %collective-permute-start = (bf16[128,512]{1,0:T(8,128)(2,1)}, bf16[128,512]{1,0:T(8,128)(2,1)S(1)}, u32[]{:S(2)}, u32[]{:S(2)}) collective-permute-start(bf16[128,512]{1,0:T(8,128)(2,1)} %param.3), channel_id=1, source_target_pairs={{0,8},{1,9},{2,10},{3,11},{4,12},{5,13},{6,14},{7,15},{8,0},{9,1},... | collective-permute-start | bytes 393224 | tf_op jit(solution)/shard_map/ppermute | solution.py:90
  4.0 7.4 %collective-permute-start.1 = (bf16[128,512]{1,0:T(8,128)(2,1)}, bf16[128,512]{1,0:T(8,128)(2,1)S(1)}, u32[]{:S(2)}, u32[]{:S(2)}) collective-permute-start(bf16[128,512]{1,0:T(8,128)(2,1)} %param.3), channel_id=1, source_target_pairs={{0,4},{1,5},{2,6},{3,7},{4,0},{5,1},{6,2},{7,3},{8,12},{9,13},{10,... | collective-permute-start | bytes 393224 | tf_op jit(solution)/shard_map/ppermute | solution.py:90
  5.6 11.7 %collective-permute-start.10 = (bf16[128,1024]{1,0:T(8,128)(2,1)}, bf16[128,1024]{1,0:T(8,128)(2,1)S(1)}, u32[]{:S(2)}, u32[]{:S(2)}) collective-permute-start(bf16[128,1024]{1,0:T(8,128)(2,1)} %refs_8_.1), channel_id=1, source_target_pairs={{0,2},{1,3},{2,0},{3,1},{4,6},{5,7},{6,4},{7,5},{8,10},{9,11},{10,... | collective-permute-start | bytes 786440 | tf_op jit(solution)/shard_map/ppermute | solution.py:90
  7.1 19.2 %collective-permute-start.7 = (bf16[128,2048]{1,0:T(8,128)(2,1)}, bf16[128,2048]{1,0:T(8,128)(2,1)S(1)}, u32[]{:S(2)}, u32[]{:S(2)}) collective-permute-start(bf16[128,2048]{1,0:T(8,128)(2,1)} %refs_4_.1), channel_id=1, source_target_pairs={{0,2},{1,3},{2,0},{3,1},{4,6},{5,7},{6,4},{7,5},{8,10},{9,11},{10,... | collective-permute-start | bytes 1572872 | tf_op jit(solution)/shard_map/ppermute | solution.py:90
  10.7 5.0 %collective-permute-start.2 = (bf16[128,512]{1,0:T(8,128)(2,1)S(1)}, bf16[128,512]{1,0:T(8,128)(2,1)S(1)}, u32[]{:S(2)}, u32[]{:S(2)}) collective-permute-start(bf16[128,512]{1,0:T(8,128)(2,1)S(1)} %collective-permute-done), channel_id=1, source_target_pairs={{0,4},{1,5},{2,6},{3,7},{4,0},{5,1},{6,2},{7,3},{8,12},{9,13},{10,... | collective-permute-start | bytes 393224 | tf_op jit(solution)/shard_map/ppermute | solution.py:90
  11.4 5.9 %copy-start = (bf16[128,1024]{1,0:T(8,128)(2,1)S(1)}, bf16[128,1024]{1,0:T(8,128)(2,1)}, u32[]{:S(2)}) copy-start(bf16[128,1024]{1,0:T(8,128)(2,1)} %refs_8_.1) | copy-start | bytes 786436
  15.6 20.1 %collective-permute-start.4 = (bf16[512,512]{1,0:T(8,128)(2,1)S(1)}, bf16[512,512]{1,0:T(8,128)(2,1)S(1)}, u32[]{:S(2)}, u32[]{:S(2)}) collective-permute-start(bf16[512,512]{1,0:T(8,128)(2,1)S(1)} %constant_dynamic-update-slice_fusion.refs_0_), channel_id=1, source_target_pairs={{0,2},{1,3},{2,0},{3,1},{4,6},{5,7},{6,4},{7,5},{8,10},{9,11},{10,... | collective-permute-start | bytes 1572872 | tf_op jit(solution)/shard_map/ppermute | solution.py:90
  17.3 1.5 %collective-permute-start.9 = (bf16[128,1024]{1,0:T(8,128)(2,1)S(1)}, bf16[128,1024]{1,0:T(8,128)(2,1)S(1)}, u32[]{:S(2)}, u32[]{:S(2)}) collective-permute-start(bf16[128,1024]{1,0:T(8,128)(2,1)S(1)} %copy-done), channel_id=1, source_target_pairs={{0,1},{1,0},{2,3},{3,2},{4,5},{5,4},{6,7},{7,6},{8,9},{9,8},{10,11... | collective-permute-start | bytes 786440 | tf_op jit(solution)/shard_map/ppermute | solution.py:90
  17.3 1.9 %collective-permute-start.11 = (bf16[128,1024]{1,0:T(8,128)(2,1)S(1)}, bf16[128,1024]{1,0:T(8,128)(2,1)S(1)}, u32[]{:S(2)}, u32[]{:S(2)}) collective-permute-start(bf16[128,1024]{1,0:T(8,128)(2,1)S(1)} %collective-permute-done.10.b2.refs_10_), channel_id=1, source_target_pairs={{0,1},{1,0},{2,3},{3,2},{4,5},{5,4},{6,7},{7,6},{8,9},{9,8},{10,11... | collective-permute-start | bytes 786440 | tf_op jit(solution)/shard_map/ppermute | solution.py:90
  17.8 18.0 %collective-permute-start.6 = (bf16[128,2048]{1,0:T(8,128)(2,1)S(1)}, bf16[128,2048]{1,0:T(8,128)(2,1)}, u32[]{:S(2)}, u32[]{:S(2)}) collective-permute-start(bf16[128,2048]{1,0:T(8,128)(2,1)S(1)} %copy-done.1), channel_id=1, source_target_pairs={{0,1},{1,0},{2,3},{3,2},{4,5},{5,4},{6,7},{7,6},{8,9},{9,8},{10,11... | collective-permute-start | bytes 1572872 | tf_op jit(solution)/shard_map/ppermute | solution.py:90
  18.8 26.1 %collective-permute-start.3 = (bf16[512,512]{1,0:T(8,128)(2,1)S(1)}, bf16[512,512]{1,0:T(8,128)(2,1)S(1)}, u32[]{:S(2)}, u32[]{:S(2)}) collective-permute-start(bf16[512,512]{1,0:T(8,128)(2,1)S(1)} %constant_dynamic-update-slice_fusion.refs_0_), channel_id=1, source_target_pairs={{0,1},{1,0},{2,3},{3,2},{4,5},{5,4},{6,7},{7,6},{8,9},{9,8},{10,11... | collective-permute-start | bytes 1572872 | tf_op jit(solution)/shard_map/ppermute | solution.py:90
  19.7 16.6 %collective-permute-start.12 = (bf16[512,256]{1,0:T(8,128)(2,1)S(1)}, bf16[512,256]{1,0:T(8,128)(2,1)S(1)}, u32[]{:S(2)}, u32[]{:S(2)}) collective-permute-start(bf16[512,256]{1,0:T(8,128)(2,1)S(1)} %shard_map.37.refs_12_), channel_id=1, source_target_pairs={{0,8},{1,9},{2,10},{3,11},{4,12},{5,13},{6,14},{7,15},{8,0},{9,1},... | collective-permute-start | bytes 786440 | tf_op jit(solution)/shard_map/ppermute | solution.py:90
  26.3 23.8 %collective-permute-start.8 = (bf16[128,2048]{1,0:T(8,128)(2,1)S(1)}, bf16[128,2048]{1,0:T(8,128)(2,1)S(1)}, u32[]{:S(2)}, u32[]{:S(2)}) collective-permute-start(bf16[128,2048]{1,0:T(8,128)(2,1)S(1)} %collective-permute-done.7.refs_6_), channel_id=1, source_target_pairs={{0,1},{1,0},{2,3},{3,2},{4,5},{5,4},{6,7},{7,6},{8,9},{9,8},{10,11... | collective-permute-start | bytes 1572872 | tf_op jit(solution)/shard_map/ppermute | solution.py:90
  35.8 14.3 %collective-permute-start.5 = (bf16[512,512]{1,0:T(8,128)(2,1)S(1)}, bf16[512,512]{1,0:T(8,128)(2,1)S(1)}, u32[]{:S(2)}, u32[]{:S(2)}) collective-permute-start(bf16[512,512]{1,0:T(8,128)(2,1)S(1)} %collective-permute-done.4.refs_2_), channel_id=1, source_target_pairs={{0,1},{1,0},{2,3},{3,2},{4,5},{5,4},{6,7},{7,6},{8,9},{9,8},{10,11... | collective-permute-start | bytes 1572872 | tf_op jit(solution)/shard_map/ppermute | solution.py:90
  35.8 9.1 %collective-permute-start.13 = (bf16[512,256]{1,0:T(8,128)(2,1)S(1)}, bf16[512,256]{1,0:T(8,128)(2,1)S(1)}, u32[]{:S(2)}, u32[]{:S(2)}) collective-permute-start(bf16[512,256]{1,0:T(8,128)(2,1)S(1)} %shard_map.37.refs_12_), channel_id=1, source_target_pairs={{0,4},{1,5},{2,6},{3,7},{4,0},{5,1},{6,2},{7,3},{8,12},{9,13},{10,... | collective-permute-start | bytes 786440 | tf_op jit(solution)/shard_map/ppermute | solution.py:90
  36.2 13.9 %collective-permute-start.14 = (bf16[512,256]{1,0:T(8,128)(2,1)S(1)}, bf16[512,256]{1,0:T(8,128)(2,1)S(1)}, u32[]{:S(2)}, u32[]{:S(2)}) collective-permute-start(bf16[512,256]{1,0:T(8,128)(2,1)S(1)} %collective-permute-done.12.refs_13_), channel_id=1, source_target_pairs={{0,4},{1,5},{2,6},{3,7},{4,0},{5,1},{6,2},{7,3},{8,12},{9,13},{10,... | collective-permute-start | bytes 786440 | tf_op jit(solution)/shard_map/ppermute | solution.py:90
  53.6 6.7 %collective-permute-start.15 = (bf16[64,1024]{1,0:T(8,128)(2,1)S(1)}, bf16[64,1024]{1,0:T(8,128)(2,1)S(1)}, u32[]{:S(2)}, u32[]{:S(2)}) collective-permute-start(bf16[64,1024]{1,0:T(8,128)(2,1)S(1)} %get-tuple-element.10), channel_id=1, source_target_pairs={{0,4},{1,5},{2,6},{3,7},{4,0},{5,1},{6,2},{7,3},{8,12},{9,13},{10,... | collective-permute-start | bytes 393224 | tf_op jit(solution)/shard_map/ppermute | solution.py:90
  54.1 12.7 %collective-permute-start.16 = (bf16[64,1024]{1,0:T(8,128)(2,1)S(1)}, bf16[64,1024]{1,0:T(8,128)(2,1)S(1)}, u32[]{:S(2)}, u32[]{:S(2)}) collective-permute-start(bf16[64,1024]{1,0:T(8,128)(2,1)S(1)} %get-tuple-element.11), channel_id=1, source_target_pairs={{0,8},{1,9},{2,10},{3,11},{4,12},{5,13},{6,14},{7,15},{8,0},{9,1},... | collective-permute-start | bytes 393224 | tf_op jit(solution)/shard_map/ppermute | solution.py:90
  54.5 12.4 %collective-permute-start.17 = (bf16[64,1024]{1,0:T(8,128)(2,1)S(1)}, bf16[64,1024]{1,0:T(8,128)(2,1)S(1)}, u32[]{:S(2)}, u32[]{:S(2)}) collective-permute-start(bf16[64,1024]{1,0:T(8,128)(2,1)S(1)} %get-tuple-element.12), channel_id=1, source_target_pairs={{0,12},{1,13},{2,14},{3,15},{4,8},{5,9},{6,10},{7,11},{8,4},{9,5},... | collective-permute-start | bytes 393224 | tf_op jit(solution)/shard_map/ppermute | solution.py:90

commit v2 on v0

v2 whole, which is shorter than its diff:
```python
import functools

import jax
import jax.numpy as jnp
from jax import lax
from jax.experimental import pallas as pl
from jax.experimental.pallas import tpu as pltpu
from jax.sharding import PartitionSpec as P

QUAD = 4
F32, BF16 = jnp.float32, jnp.bfloat16


def dot(a, b, ca, cb):
    return lax.dot_general(a, b, (((ca,), (cb,)), ((), ())), preferred_element_type=F32)


def call(body, outs, where, args, flops, scratch=()):
    size = sum(a.size * a.dtype.itemsize for a in (*args, *outs))
    held = size + sum(s.shape[0] * s.shape[1] * 4 for s in scratch)
    vmem = pl.BlockSpec(memory_space=pltpu.VMEM)
    return pl.pallas_call(
        body,
        out_shape=list(outs),
        in_specs=[pl.BlockSpec(memory_space=pltpu.SMEM)] + [vmem] * len(args),
        out_specs=[vmem] * len(outs),
        scratch_shapes=list(scratch),
        cost_estimate=pl.CostEstimate(flops=flops, bytes_accessed=size, transcendentals=0),
        compiler_params=pltpu.CompilerParams(vmem_limit_bytes=held + (16 << 20)),
    )(where, *args)


def part_kernel(me_ref, k_ref, keep_ref, send_ref):
    core, block = me_ref[0] % 2, k_ref.shape[0]
    for j in range(keep_ref.shape[1] // block):
        for ref, c in ((keep_ref, core), (send_ref, 1 - core)):
            at = pl.multiple_of((2 * j + c) * block, block)
            ref[:, j * block : (j + 1) * block] = k_ref[:, pl.ds(at, block)]


def pick_kernel(width, me_ref, own_ref, y_ref, x_ref):
    place = me_ref[0] % QUAD
    rows, columns = own_ref.shape
    share = columns // QUAD
    k = lax.broadcasted_iota(jnp.int32, (columns, share), 0)
    m = lax.broadcasted_iota(jnp.int32, (columns, share), 1)
    for c in (0, 1):
        chosen = (m // width) * (QUAD * width) + (place ^ c) * width + m % width
        picker = (k == chosen).astype(F32).astype(BF16)
        for s, b in enumerate((own_ref, y_ref)):
            x_ref[s * rows : (s + 1) * rows, c * share : (c + 1) * share] = dot(b[...], picker, 1, 0).astype(BF16)


def apply_kernel(order, me_ref, near, far, near_y, far_y, oc_ref, oyc_ref, *refs):
    nz = len(order)
    k, x, (keep_ref, send_ref) = refs[0:4], refs[4 : 4 + nz], refs[4 + nz :]
    rows = k[0].shape[0]
    zi, y = me_ref[0] // QUAD, (me_ref[0] // 2) % 2
    o_rows = jnp.concatenate([r[0:rows, :] for r in (near, oc_ref, near_y, oyc_ref)], axis=0)
    acc = None
    for i, m in enumerate(order):
        held, at = ((near, near_y), i * rows) if i * rows < near.shape[0] else ((far, far_y), i * rows - near.shape[0])
        o_cols = jnp.concatenate([r[at : at + rows, :] for r in held], axis=0)
        density = dot(o_rows, o_cols, 1, 1)
        at = [pl.multiple_of((2 * (zi ^ m) + (y ^ s)) * rows, rows) for s in (0, 1)]
        k_block = jnp.concatenate(
            [jnp.concatenate([kr[:, pl.ds(a, rows)] for a in at], axis=1) for kr in k], axis=0
        )
        weighted = (density * k_block.astype(F32)).astype(BF16)
        term = dot(weighted, x[i][...], 1, 0)
        acc = term if acc is None else acc + term
    share = acc.shape[1] // 2
    keep_ref[...] = acc[:, :share]
    for r in range(QUAD):
        send_ref[(r ^ 1) * rows : ((r ^ 1) + 1) * rows, :] = acc[r * rows : (r + 1) * rows, share:]


def project_kernel(width, me_ref, keep_ref, came_ref, b0, b1, b2, b3, *refs):
    own_ref, outs, total = refs[0], refs[1:-1], refs[-1]
    zi = me_ref[0] // QUAD
    applied = (keep_ref[...] + came_ref[...]).astype(BF16)
    b_all = jnp.concatenate([r[...] for r in (b0, b1, b2, b3)], axis=0)
    total[...] = dot(applied, b_all, 0, 0)
    for m in range(len(outs) + 1):
        part = total[pl.ds(pl.multiple_of((zi ^ m) * width, width), width), :]
        if m == 0:
            own_ref[...] = part
        else:
            outs[m - 1][...] = part.astype(BF16)


def shards(n, orbitals, basis, kernel):
    nz = n // QUAD
    where = jnp.full((1,), lax.axis_index("row"), jnp.int32)
    rows, columns = basis.shape
    width, share, points = columns // n, columns // QUAD, n * rows

    def swap(a, bit):
        return lax.ppermute(a, "row", [(i, i ^ bit) for i in range(n)])

    def after(a, *earlier):
        return lax.optimization_barrier((a, *earlier))[0]

    order, step = [0], nz // 2
    while step:
        order, step = order + [m + step for m in order], step // 2

    def first_hops(a):
        return {m: swap(a, QUAD * m) for m in order if m and m & (m - 1) == 0}

    def other_hops(a, hops):
        held = {0: a, **hops}
        for m in order:
            if m not in held:
                low = m & -m
                held[m] = swap(held[m ^ low], QUAD * low)
        return [held[m] for m in order]

    barrier = lax.optimization_barrier
    half = jax.ShapeDtypeStruct((rows, points // 2), BF16)
    k_keep, k_send = call(part_kernel, (half, half), where, (kernel,), 0)
    b_y, k_c = swap(basis, 2), swap(k_send, 1)
    o_hops = first_hops(orbitals)
    b_y, k_c, k_keep = barrier((b_y, k_c, k_keep))
    (x,) = call(
        functools.partial(pick_kernel, width),
        (jax.ShapeDtypeStruct((2 * rows, 2 * share), BF16),),
        where,
        (basis, b_y),
        8 * rows * columns * share,
    )
    near = jnp.concatenate([orbitals, *o_hops.values()], axis=0)
    k_y, near_y = swap(k_keep, 2), swap(near, 2)
    o_c, b_c = swap(orbitals, 1), swap(basis, 1)
    x_hops = first_hops(x)
    far = jnp.concatenate([a for m, a in zip(order, other_hops(orbitals, o_hops)) if m and m not in o_hops], axis=0)
    far, k_y, near_y, o_c, b_c, *x_first = barrier((far, k_y, near_y, o_c, b_c, *x_hops.values()))
    k_yc, far_y = swap(k_c, 2), swap(far, 2)
    xs = other_hops(x, dict(zip(x_hops, x_first)))
    o_yc, b_yc = swap(near_y[:rows], 1), swap(b_y, 1)
    places = [0, *o_hops, *(m for m in order if m and m not in o_hops)]
    xs = [xs[order.index(m)] for m in places]
    block = jax.ShapeDtypeStruct((QUAD * rows, share), F32)
    keep, send = call(
        functools.partial(apply_kernel, tuple(places)),
        (block, block),
        where,
        (near, far, near_y, far_y, o_c, o_yc, k_keep, k_c, k_y, k_yc, *xs),
        QUAD * rows * points * (orbitals.shape[1] + 2 * share),
    )
    parts = call(
        functools.partial(project_kernel, width),
        [jax.ShapeDtypeStruct((width, columns), BF16 if m else F32) for m in range(nz)],
        where,
        (keep, swap(send, 1), basis, b_c, b_y, b_yc),
        2 * QUAD * rows * share * columns,
        scratch=(pltpu.VMEM((share, columns), F32),),
    )
    total = parts[0]
    for m in range(1, nz):
        total = total + swap(parts[m], QUAD * m).astype(F32)
    return total.T


def solution(mesh):
    rows = P(("groups", "row"), None)
    return jax.shard_map(
        functools.partial(shards, mesh.shape["row"]),
        mesh=mesh,
        in_specs=(rows, rows, rows),
        out_specs=P("groups", "row"),
        check_vma=False,
    )
```

time: 134 us -> 57.5 us (0.43)
  waiting for transfers between devices: 98.7 us -> 31.6 us
  starting transfers between devices: 0.04 us -> 20.7 us
  between operations: 13.4 us -> 0.09 us
  blocking collectives: 13 us -> 0 us
  matrix products: 8.14 us -> 0 us
  Pallas kernels: 0 us -> 2.69 us
  local copies, waits for them, and re-layouts: 0.17 us -> 1.55 us
    all_gather x2 -> x0, waiting for transfers between devices: 97.3 us -> none  [the longest x1 51.7 us: shards(): whole_basis = lax.all_gather(basis, 'row', axis=0, tiled=True)]
    ppermute x0 -> x20, waiting for transfers between devices: none -> 31.6 us  [swap(): return lax.ppermute(a, 'row', [(i, i ^ bit) for i in range(n)])]
    ppermute x0 -> x20, starting transfers between devices: none -> 20.7 us  [swap(): return lax.ppermute(a, 'row', [(i, i ^ bit) for i in range(n)])]
    all_to_all x1 -> x0, blocking collectives: 13 us -> none  [shards(): lax.all_to_all(applied, 'row', split_axis=1, concat_axis=0, tiled=True)]
    dot_general x2 -> x0, matrix products: 8.14 us -> none  [the longest x1 4.41 us: shards(): jnp.dot(weighted, whole_basis, preferred_element_type=jnp.float32)]
    pallas_call x0 -> x4, Pallas kernels: none -> 2.69 us  [call(): pl.pallas_call(body, out_shape=list(outs), in_specs=[pl.BlockSpec(memory_...]
    unnamed x0 -> x8, local copies, waits for them, and re-layouts: none -> 1.53 us
    unnamed x2 -> x0, waiting for transfers between devices: 1.41 us -> none
  transfers between devices with their start and end apart: 2 -> 20, of which waited for: 2 -> 13; matrix products, arithmetic and copies ran while one was open for 0% -> 0% of each run, Pallas kernels for 0% -> 1%
where the time goes in v2:
time: 57.5 us; the launch traced here: 57.3 us
  waiting for transfers between devices  31.6 us (55%)
  starting transfers between devices  20.7 us (36%)
  Pallas kernels  2.69 us (5%)
  local copies, waits for them, and re-layouts  1.55 us (3%)
  other arithmetic  0.76 us (1%)
    ppermute x20, waiting for transfers between devices, swap(): return lax.ppermute(a, 'row', [(i, i ^ bit) for i in range(n)])  31.6 us
    ppermute x20, starting transfers between devices, swap(): return lax.ppermute(a, 'row', [(i, i ^ bit) for i in range(n)])  20.7 us
    pallas_call x4, Pallas kernels, call(): pl.pallas_call(body, out_shape=list(outs), in_specs=[pl.BlockSpec(memory_...  2.69 us
    unnamed x8, local copies, waits for them, and re-layouts  1.53 us
  transfers between devices with their start and end apart: 20, of which 13 were waited for; matrix products, arithmetic and copies ran while one was open for 0% of the time, Pallas kernels for 1%

profile of v2, /device:TPU:0, one launch (start us, length us, event | category | flops | bytes accessed | tf_op | source)
XLA Modules:
  0.0 57.3 jit_solution(12919207055662870672)
XLA Ops:
  0.0 4.0 %collective-permute-start = (bf16[128,512]{1,0:T(8,128)(2,1)}, bf16[128,512]{1,0:T(8,128)(2,1)S(1)}, u32[]{:S(2)}, u32[]{:S(2)}) collective-permute-start(bf16[128,512]{1,0:T(8,128)(2,1)} %param.3), channel_id=1, source_target_pairs={{0,8},{1,9},{2,10},{3,11},{4,12},{5,13},{6,14},{7,15},{8,0},{9,1},... | collective-permute-start | bytes 393224 | tf_op jit(solution)/shard_map/ppermute | solution.py:99
  4.0 1.6 %collective-permute-start.1 = (bf16[128,512]{1,0:T(8,128)(2,1)}, bf16[128,512]{1,0:T(8,128)(2,1)S(1)}, u32[]{:S(2)}, u32[]{:S(2)}) collective-permute-start(bf16[128,512]{1,0:T(8,128)(2,1)} %param.3), channel_id=1, source_target_pairs={{0,4},{1,5},{2,6},{3,7},{4,0},{5,1},{6,2},{7,3},{8,12},{9,13},{10,... | collective-permute-start | bytes 393224 | tf_op jit(solution)/shard_map/ppermute | solution.py:99
  5.6 1.5 %collective-permute-start.3 = (bf16[128,1024]{1,0:T(8,128)(2,1)}, bf16[128,1024]{1,0:T(8,128)(2,1)S(1)}, u32[]{:S(2)}, u32[]{:S(2)}) collective-permute-start(bf16[128,1024]{1,0:T(8,128)(2,1)} %b0.1), channel_id=1, source_target_pairs={{0,2},{1,3},{2,0},{3,1},{4,6},{5,7},{6,4},{7,5},{8,10},{9,11},{10,... | collective-permute-start | bytes 786440 | tf_op jit(solution)/shard_map/ppermute | solution.py:99
  7.1 1.0 %copy-done = bf16[128,2048]{1,0:T(8,128)(2,1)S(1)} copy-done((bf16[128,2048]{1,0:T(8,128)(2,1)S(1)}, bf16[128,2048]{1,0:T(8,128)(2,1)}, u32[]{:S(2)}) %copy-start) | copy-done | bytes 524312
  9.1 1.5 %collective-permute-done = bf16[128,512]{1,0:T(8,128)(2,1)S(1)} collective-permute-done((bf16[128,512]{1,0:T(8,128)(2,1)}, bf16[128,512]{1,0:T(8,128)(2,1)S(1)}, u32[]{:S(2)}, u32[]{:S(2)}) %collective-permute-start) | collective-permute-done | bytes 131104 | tf_op jit(solution)/shard_map/ppermute | solution.py:99
  10.9 1.6 %collective-permute-start.6 = (bf16[384,512]{1,0:T(8,128)(2,1)S(1)}, bf16[384,512]{1,0:T(8,128)(2,1)S(1)}, u32[]{:S(2)}, u32[]{:S(2)}) collective-permute-start(bf16[384,512]{1,0:T(8,128)(2,1)S(1)} %constant_dynamic-update-slice_fusion.near), channel_id=1, source_target_pairs={{0,2},{1,3},{2,0},{3,1},{4,6},{5,7},{6,4},{7,5},{8,10},{9,11},{10,... | collective-permute-start | bytes 1179656 | tf_op jit(solution)/shard_map/ppermute | solution.py:99
  12.5 1.4 %collective-permute-start.2 = (bf16[128,512]{1,0:T(8,128)(2,1)S(1)}, bf16[128,512]{1,0:T(8,128)(2,1)S(1)}, u32[]{:S(2)}, u32[]{:S(2)}) collective-permute-start(bf16[128,512]{1,0:T(8,128)(2,1)S(1)} %collective-permute-done), channel_id=1, source_target_pairs={{0,4},{1,5},{2,6},{3,7},{4,0},{5,1},{6,2},{7,3},{8,12},{9,13},{10,... | collective-permute-start | bytes 393224 | tf_op jit(solution)/shard_map/ppermute | solution.py:99
  13.9 1.0 %collective-permute-done.3.y_ref.b2 = bf16[128,1024]{1,0:T(8,128)(2,1)S(1)} collective-permute-done((bf16[128,1024]{1,0:T(8,128)(2,1)}, bf16[128,1024]{1,0:T(8,128)(2,1)S(1)}, u32[]{:S(2)}, u32[]{:S(2)}) %collective-permute-start.3) | collective-permute-done | bytes 262176 | tf_op jit(solution)/shard_map/ppermute | solution.py:99
  15.9 1.0 %collective-permute-start.9 = (bf16[256,512]{1,0:T(8,128)(2,1)S(1)}, bf16[256,512]{1,0:T(8,128)(2,1)S(1)}, u32[]{:S(2)}, u32[]{:S(2)}) collective-permute-start(bf16[256,512]{1,0:T(8,128)(2,1)S(1)} %shard_map.38.refs_4_), channel_id=1, source_target_pairs={{0,8},{1,9},{2,10},{3,11},{4,12},{5,13},{6,14},{7,15},{8,0},{9,1},... | collective-permute-start | bytes 786440 | tf_op jit(solution)/shard_map/ppermute | solution.py:99
  16.9 0.6 collective-permute-done.2.far
  17.9 1.6 %collective-permute-start.13 = (bf16[128,1024]{1,0:T(8,128)(2,1)S(1)}, bf16[128,1024]{1,0:T(8,128)(2,1)S(1)}, u32[]{:S(2)}, u32[]{:S(2)}) collective-permute-start(bf16[128,1024]{1,0:T(8,128)(2,1)S(1)} %collective-permute-done.4.refs_1_), channel_id=1, source_target_pairs={{0,2},{1,3},{2,0},{3,1},{4,6},{5,7},{6,4},{7,5},{8,10},{9,11},{10,... | collective-permute-start | bytes 786440 | tf_op jit(solution)/shard_map/ppermute | solution.py:99
  19.5 3.8 %collective-permute-done.6.near_y = bf16[384,512]{1,0:T(8,128)(2,1)S(1)} collective-permute-done((bf16[384,512]{1,0:T(8,128)(2,1)S(1)}, bf16[384,512]{1,0:T(8,128)(2,1)S(1)}, u32[]{:S(2)}, u32[]{:S(2)}) %collective-permute-start.6) | collective-permute-done | bytes 393248 | tf_op jit(solution)/shard_map/ppermute | solution.py:99
  23.4 6.2 %collective-permute-done.10.refs_6_ = bf16[256,512]{1,0:T(8,128)(2,1)S(1)} collective-permute-done((bf16[256,512]{1,0:T(8,128)(2,1)S(1)}, bf16[256,512]{1,0:T(8,128)(2,1)S(1)}, u32[]{:S(2)}, u32[]{:S(2)}) %collective-permute-start.10) | collective-permute-done | bytes 262176 | tf_op jit(solution)/shard_map/ppermute | solution.py:99
  29.6 1.3 %collective-permute-done.9.refs_5_ = bf16[256,512]{1,0:T(8,128)(2,1)S(1)} collective-permute-done((bf16[256,512]{1,0:T(8,128)(2,1)S(1)}, bf16[256,512]{1,0:T(8,128)(2,1)S(1)}, u32[]{:S(2)}, u32[]{:S(2)}) %collective-permute-start.9) | collective-permute-done | bytes 262176 | tf_op jit(solution)/shard_map/ppermute | solution.py:99
  31.4 1.2 %collective-permute-start.11 = (bf16[128,512]{1,0:T(8,128)(2,1)S(1)}, bf16[128,512]{1,0:T(8,128)(2,1)S(1)}, u32[]{:S(2)}, u32[]{:S(2)}) collective-permute-start(bf16[128,512]{1,0:T(8,128)(2,1)S(1)} %collective-permute-done.2.far), channel_id=1, source_target_pairs={{0,2},{1,3},{2,0},{3,1},{4,6},{5,7},{6,4},{7,5},{8,10},{9,11},{10,... | collective-permute-start | bytes 393224 | tf_op jit(solution)/shard_map/ppermute | solution.py:99
  32.6 1.6 %collective-permute-done.13.refs_3_ = bf16[128,1024]{1,0:T(8,128)(2,1)S(1)} collective-permute-done((bf16[128,1024]{1,0:T(8,128)(2,1)S(1)}, bf16[128,1024]{1,0:T(8,128)(2,1)S(1)}, u32[]{:S(2)}, u32[]{:S(2)}) %collective-permute-start.13) | collective-permute-done | bytes 262176 | tf_op jit(solution)/shard_map/ppermute | solution.py:99
  34.2 3.1 %collective-permute-done.11.far_y = bf16[128,512]{1,0:T(8,128)(2,1)S(1)} collective-permute-done((bf16[128,512]{1,0:T(8,128)(2,1)S(1)}, bf16[128,512]{1,0:T(8,128)(2,1)S(1)}, u32[]{:S(2)}, u32[]{:S(2)}) %collective-permute-start.11) | collective-permute-done | bytes 131104 | tf_op jit(solution)/shard_map/ppermute | solution.py:99
  37.5 1.6 %shard_map.39 = (f32[512,256]{1,0:T(8,128)S(1)}, f32[512,256]{1,0:T(8,128)S(1)}) custom-call(s32[1]{0:T(128)} %bitcast.me_ref, bf16[384,512]{1,0:T(8,128)(2,1)S(1)} %constant_dynamic-update-slice_fusion.near, bf16[128,512]{1,0:T(8,128)(2,1)S(1)} %collective-permute-done.2.far, bf16[384,512]{1,0:T(8,128)(2,1)S(1)} %collective-permute-done.6.near_y, ...), custom_call_target="tpu_custom_call" | custom-call | flops 1073741824 | bytes 4456448 | tf_op jit(solution)/shard_map/pallas_call | solution.py:22
  39.6 1.8 %collective-permute-done.16.b3 = bf16[128,1024]{1,0:T(8,128)(2,1)S(1)} collective-permute-done((bf16[128,1024]{1,0:T(8,128)(2,1)S(1)}, bf16[128,1024]{1,0:T(8,128)(2,1)S(1)}, u32[]{:S(2)}, u32[]{:S(2)}) %collective-permute-start.16) | collective-permute-done | bytes 262176 | tf_op jit(solution)/shard_map/ppermute | solution.py:99
  42.0 1.7 %collective-permute-start.17 = (bf16[64,1024]{1,0:T(8,128)(2,1)S(1)}, bf16[64,1024]{1,0:T(8,128)(2,1)S(1)}, u32[]{:S(2)}, u32[]{:S(2)}) collective-permute-start(bf16[64,1024]{1,0:T(8,128)(2,1)S(1)} %get-tuple-element.38), channel_id=1, source_target_pairs={{0,4},{1,5},{2,6},{3,7},{4,0},{5,1},{6,2},{7,3},{8,12},{9,13},{10,... | collective-permute-start | bytes 393224 | tf_op jit(solution)/shard_map/ppermute | solution.py:99
  43.6 2.3 %collective-permute-start.18 = (bf16[64,1024]{1,0:T(8,128)(2,1)S(1)}, bf16[64,1024]{1,0:T(8,128)(2,1)S(1)}, u32[]{:S(2)}, u32[]{:S(2)}) collective-permute-start(bf16[64,1024]{1,0:T(8,128)(2,1)S(1)} %get-tuple-element.39), channel_id=1, source_target_pairs={{0,8},{1,9},{2,10},{3,11},{4,12},{5,13},{6,14},{7,15},{8,0},{9,1},... | collective-permute-start | bytes 393224 | tf_op jit(solution)/shard_map/ppermute | solution.py:99
  46.4 3.0 %collective-permute-done.17 = bf16[64,1024]{1,0:T(8,128)(2,1)S(1)} collective-permute-done((bf16[64,1024]{1,0:T(8,128)(2,1)S(1)}, bf16[64,1024]{1,0:T(8,128)(2,1)S(1)}, u32[]{:S(2)}, u32[]{:S(2)}) %collective-permute-start.17) | collective-permute-done | bytes 131104 | tf_op jit(solution)/shard_map/ppermute | solution.py:99
  49.4 7.2 %collective-permute-done.18 = bf16[64,1024]{1,0:T(8,128)(2,1)S(1)} collective-permute-done((bf16[64,1024]{1,0:T(8,128)(2,1)S(1)}, bf16[64,1024]{1,0:T(8,128)(2,1)S(1)}, u32[]{:S(2)}, u32[]{:S(2)}) %collective-permute-start.18) | collective-permute-done | bytes 131104 | tf_op jit(solution)/shard_map/ppermute | solution.py:99
  56.6 0.8 %add_bitcast_fusion = f32[1024,64]{0,1:T(8,128)} fusion(bf16[64,1024]{1,0:T(8,128)(2,1)S(1)} %collective-permute-done.19, bf16[64,1024]{1,0:T(8,128)(2,1)S(1)} %collective-permute-done.18, f32[64,1024]{1,0:T(8,128)S(1)} %get-tuple-element.37, bf16[64,1024]{1,0:T(8,128)(2,1)S(1)} %collective-permute-done.17), kind=kLoop, calls=%fused_computation | loop fusion | flops 393216 | bytes 917504 | tf_op jit(solution)/shard_map/transpose | solution.py:162
  (31 shorter events, 4.7 us)
Async XLA Ops:
  0.0 10.7 %collective-permute-start = (bf16[128,512]{1,0:T(8,128)(2,1)}, bf16[128,512]{1,0:T(8,128)(2,1)S(1)}, u32[]{:S(2)}, u32[]{:S(2)}) collective-permute-start(bf16[128,512]{1,0:T(8,128)(2,1)} %param.3), channel_id=1, source_target_pairs={{0,8},{1,9},{2,10},{3,11},{4,12},{5,13},{6,14},{7,15},{8,0},{9,1},... | collective-permute-start | bytes 393224 | tf_op jit(solution)/shard_map/ppermute | solution.py:99
  4.0 6.8 %collective-permute-start.1 = (bf16[128,512]{1,0:T(8,128)(2,1)}, bf16[128,512]{1,0:T(8,128)(2,1)S(1)}, u32[]{:S(2)}, u32[]{:S(2)}) collective-permute-start(bf16[128,512]{1,0:T(8,128)(2,1)} %param.3), channel_id=1, source_target_pairs={{0,4},{1,5},{2,6},{3,7},{4,0},{5,1},{6,2},{7,3},{8,12},{9,13},{10,... | collective-permute-start | bytes 393224 | tf_op jit(solution)/shard_map/ppermute | solution.py:99
  5.6 10.3 %collective-permute-start.7 = (bf16[128,512]{1,0:T(8,128)(2,1)}, bf16[128,512]{1,0:T(8,128)(2,1)S(1)}, u32[]{:S(2)}, u32[]{:S(2)}) collective-permute-start(bf16[128,512]{1,0:T(8,128)(2,1)} %param.3), channel_id=1, source_target_pairs={{0,1},{1,0},{2,3},{3,2},{4,5},{5,4},{6,7},{7,6},{8,9},{9,8},{10,11... | collective-permute-start | bytes 393224 | tf_op jit(solution)/shard_map/ppermute | solution.py:99
  5.6 9.3 %collective-permute-start.3 = (bf16[128,1024]{1,0:T(8,128)(2,1)}, bf16[128,1024]{1,0:T(8,128)(2,1)S(1)}, u32[]{:S(2)}, u32[]{:S(2)}) collective-permute-start(bf16[128,1024]{1,0:T(8,128)(2,1)} %b0.1), channel_id=1, source_target_pairs={{0,2},{1,3},{2,0},{3,1},{4,6},{5,7},{6,4},{7,5},{8,10},{9,11},{10,... | collective-permute-start | bytes 786440 | tf_op jit(solution)/shard_map/ppermute | solution.py:99
  7.1 1.0 %copy-start = (bf16[128,2048]{1,0:T(8,128)(2,1)S(1)}, bf16[128,2048]{1,0:T(8,128)(2,1)}, u32[]{:S(2)}) copy-start(bf16[128,2048]{1,0:T(8,128)(2,1)} %k_ref.1) | copy-start | bytes 1572868
  8.2 0.9 %copy-start.2 = (bf16[128,512]{1,0:T(8,128)(2,1)S(1)}, bf16[128,512]{1,0:T(8,128)(2,1)}, u32[]{:S(2)}) copy-start(bf16[128,512]{1,0:T(8,128)(2,1)} %param.3) | copy-start | bytes 393220
  8.3 6.6 %collective-permute-start.4 = (bf16[128,1024]{1,0:T(8,128)(2,1)S(1)}, bf16[128,1024]{1,0:T(8,128)(2,1)S(1)}, u32[]{:S(2)}, u32[]{:S(2)}) collective-permute-start(bf16[128,1024]{1,0:T(8,128)(2,1)S(1)} %get-tuple-element.23), channel_id=1, source_target_pairs={{0,1},{1,0},{2,3},{3,2},{4,5},{5,4},{6,7},{7,6},{8,9},{9,8},{10,11... | collective-permute-start | bytes 786440 | tf_op jit(solution)/shard_map/ppermute | solution.py:99
  9.1 5.8 %copy-start.1 = (bf16[128,1024]{1,0:T(8,128)(2,1)S(1)}, bf16[128,1024]{1,0:T(8,128)(2,1)}, u32[]{:S(2)}) copy-start(bf16[128,1024]{1,0:T(8,128)(2,1)} %b0.1) | copy-start | bytes 786436
  10.9 12.5 %collective-permute-start.6 = (bf16[384,512]{1,0:T(8,128)(2,1)S(1)}, bf16[384,512]{1,0:T(8,128)(2,1)S(1)}, u32[]{:S(2)}, u32[]{:S(2)}) collective-permute-start(bf16[384,512]{1,0:T(8,128)(2,1)S(1)} %constant_dynamic-update-slice_fusion.near), channel_id=1, source_target_pairs={{0,2},{1,3},{2,0},{3,1},{4,6},{5,7},{6,4},{7,5},{8,10},{9,11},{10,... | collective-permute-start | bytes 1179656 | tf_op jit(solution)/shard_map/ppermute | solution.py:99
  12.5 5.0 %collective-permute-start.2 = (bf16[128,512]{1,0:T(8,128)(2,1)S(1)}, bf16[128,512]{1,0:T(8,128)(2,1)S(1)}, u32[]{:S(2)}, u32[]{:S(2)}) collective-permute-start(bf16[128,512]{1,0:T(8,128)(2,1)S(1)} %collective-permute-done), channel_id=1, source_target_pairs={{0,4},{1,5},{2,6},{3,7},{4,0},{5,1},{6,2},{7,3},{8,12},{9,13},{10,... | collective-permute-start | bytes 393224 | tf_op jit(solution)/shard_map/ppermute | solution.py:99
  14.9 3.0 %collective-permute-start.8 = (bf16[128,1024]{1,0:T(8,128)(2,1)S(1)}, bf16[128,1024]{1,0:T(8,128)(2,1)S(1)}, u32[]{:S(2)}, u32[]{:S(2)}) collective-permute-start(bf16[128,1024]{1,0:T(8,128)(2,1)S(1)} %copy-done.1), channel_id=1, source_target_pairs={{0,1},{1,0},{2,3},{3,2},{4,5},{5,4},{6,7},{7,6},{8,9},{9,8},{10,11... | collective-permute-start | bytes 786440 | tf_op jit(solution)/shard_map/ppermute | solution.py:99
  15.4 14.2 %collective-permute-start.10 = (bf16[256,512]{1,0:T(8,128)(2,1)S(1)}, bf16[256,512]{1,0:T(8,128)(2,1)S(1)}, u32[]{:S(2)}, u32[]{:S(2)}) collective-permute-start(bf16[256,512]{1,0:T(8,128)(2,1)S(1)} %shard_map.38.refs_4_), channel_id=1, source_target_pairs={{0,4},{1,5},{2,6},{3,7},{4,0},{5,1},{6,2},{7,3},{8,12},{9,13},{10,... | collective-permute-start | bytes 786440 | tf_op jit(solution)/shard_map/ppermute | solution.py:99
  15.9 15.0 %collective-permute-start.9 = (bf16[256,512]{1,0:T(8,128)(2,1)S(1)}, bf16[256,512]{1,0:T(8,128)(2,1)S(1)}, u32[]{:S(2)}, u32[]{:S(2)}) collective-permute-start(bf16[256,512]{1,0:T(8,128)(2,1)S(1)} %shard_map.38.refs_4_), channel_id=1, source_target_pairs={{0,8},{1,9},{2,10},{3,11},{4,12},{5,13},{6,14},{7,15},{8,0},{9,1},... | collective-permute-start | bytes 786440 | tf_op jit(solution)/shard_map/ppermute | solution.py:99
  17.5 13.4 %collective-permute-start.5 = (bf16[128,1024]{1,0:T(8,128)(2,1)S(1)}, bf16[128,1024]{1,0:T(8,128)(2,1)S(1)}, u32[]{:S(2)}, u32[]{:S(2)}) collective-permute-start(bf16[128,1024]{1,0:T(8,128)(2,1)S(1)} %get-tuple-element.25.refs_0_), channel_id=1, source_target_pairs={{0,2},{1,3},{2,0},{3,1},{4,6},{5,7},{6,4},{7,5},{8,10},{9,11},{10,... | collective-permute-start | bytes 786440 | tf_op jit(solution)/shard_map/ppermute | solution.py:99
  17.9 16.3 %collective-permute-start.13 = (bf16[128,1024]{1,0:T(8,128)(2,1)S(1)}, bf16[128,1024]{1,0:T(8,128)(2,1)S(1)}, u32[]{:S(2)}, u32[]{:S(2)}) collective-permute-start(bf16[128,1024]{1,0:T(8,128)(2,1)S(1)} %collective-permute-done.4.refs_1_), channel_id=1, source_target_pairs={{0,2},{1,3},{2,0},{3,1},{4,6},{5,7},{6,4},{7,5},{8,10},{9,11},{10,... | collective-permute-start | bytes 786440 | tf_op jit(solution)/shard_map/ppermute | solution.py:99
  30.9 6.6 %collective-permute-start.14 = (bf16[256,512]{1,0:T(8,128)(2,1)S(1)}, bf16[256,512]{1,0:T(8,128)(2,1)S(1)}, u32[]{:S(2)}, u32[]{:S(2)}) collective-permute-start(bf16[256,512]{1,0:T(8,128)(2,1)S(1)} %collective-permute-done.9.refs_5_), channel_id=1, source_target_pairs={{0,4},{1,5},{2,6},{3,7},{4,0},{5,1},{6,2},{7,3},{8,12},{9,13},{10,... | collective-permute-start | bytes 786440 | tf_op jit(solution)/shard_map/ppermute | solution.py:99
  31.3 2.9 %collective-permute-start.12 = (bf16[128,512]{1,0:T(8,128)(2,1)S(1)}, bf16[128,512]{1,0:T(8,128)(2,1)S(1)}, u32[]{:S(2)}, u32[]{:S(2)}) collective-permute-start(bf16[128,512]{1,0:T(8,128)(2,1)S(1)} %slice.3), channel_id=1, source_target_pairs={{0,1},{1,0},{2,3},{3,2},{4,5},{5,4},{6,7},{7,6},{8,9},{9,8},{10,11... | collective-permute-start | bytes 393224 | tf_op jit(solution)/shard_map/ppermute | solution.py:99
  31.4 5.9 %collective-permute-start.11 = (bf16[128,512]{1,0:T(8,128)(2,1)S(1)}, bf16[128,512]{1,0:T(8,128)(2,1)S(1)}, u32[]{:S(2)}, u32[]{:S(2)}) collective-permute-start(bf16[128,512]{1,0:T(8,128)(2,1)S(1)} %collective-permute-done.2.far), channel_id=1, source_target_pairs={{0,2},{1,3},{2,0},{3,1},{4,6},{5,7},{6,4},{7,5},{8,10},{9,11},{10,... | collective-permute-start | bytes 393224 | tf_op jit(solution)/shard_map/ppermute | solution.py:99
  39.1 2.4 %collective-permute-start.15 = (f32[512,256]{1,0:T(8,128)S(1)}, f32[512,256]{1,0:T(8,128)S(1)}, u32[]{:S(2)}, u32[]{:S(2)}) collective-permute-start(f32[512,256]{1,0:T(8,128)S(1)} %get-tuple-element.35), channel_id=1, source_target_pairs={{0,1},{1,0},{2,3},{3,2},{4,5},{5,4},{6,7},{7,6},{8,9},{9,8},{10,11... | collective-permute-start | bytes 1572872 | tf_op jit(solution)/shard_map/ppermute | solution.py:99
  39.1 2.3 %collective-permute-start.16 = (bf16[128,1024]{1,0:T(8,128)(2,1)S(1)}, bf16[128,1024]{1,0:T(8,128)(2,1)S(1)}, u32[]{:S(2)}, u32[]{:S(2)}) collective-permute-start(bf16[128,1024]{1,0:T(8,128)(2,1)S(1)} %collective-permute-done.3.y_ref.b2), channel_id=1, source_target_pairs={{0,1},{1,0},{2,3},{3,2},{4,5},{5,4},{6,7},{7,6},{8,9},{9,8},{10,11... | collective-permute-start | bytes 786440 | tf_op jit(solution)/shard_map/ppermute | solution.py:99
  42.0 7.4 %collective-permute-start.17 = (bf16[64,1024]{1,0:T(8,128)(2,1)S(1)}, bf16[64,1024]{1,0:T(8,128)(2,1)S(1)}, u32[]{:S(2)}, u32[]{:S(2)}) collective-permute-start(bf16[64,1024]{1,0:T(8,128)(2,1)S(1)} %get-tuple-element.38), channel_id=1, source_target_pairs={{0,4},{1,5},{2,6},{3,7},{4,0},{5,1},{6,2},{7,3},{8,12},{9,13},{10,... | collective-permute-start | bytes 393224 | tf_op jit(solution)/shard_map/ppermute | solution.py:99
  43.6 12.9 %collective-permute-start.18 = (bf16[64,1024]{1,0:T(8,128)(2,1)S(1)}, bf16[64,1024]{1,0:T(8,128)(2,1)S(1)}, u32[]{:S(2)}, u32[]{:S(2)}) collective-permute-start(bf16[64,1024]{1,0:T(8,128)(2,1)S(1)} %get-tuple-element.39), channel_id=1, source_target_pairs={{0,8},{1,9},{2,10},{3,11},{4,12},{5,13},{6,14},{7,15},{8,0},{9,1},... | collective-permute-start | bytes 393224 | tf_op jit(solution)/shard_map/ppermute | solution.py:99
  46.0 10.6 %collective-permute-start.19 = (bf16[64,1024]{1,0:T(8,128)(2,1)S(1)}, bf16[64,1024]{1,0:T(8,128)(2,1)S(1)}, u32[]{:S(2)}, u32[]{:S(2)}) collective-permute-start(bf16[64,1024]{1,0:T(8,128)(2,1)S(1)} %get-tuple-element.40), channel_id=1, source_target_pairs={{0,12},{1,13},{2,14},{3,15},{4,8},{5,9},{6,10},{7,11},{8,4},{9,5},... | collective-permute-start | bytes 393224 | tf_op jit(solution)/shard_map/ppermute | solution.py:99

commit v3 on v2

--- a/solution.py
+++ b/solution.py
@@ -72,13 +72,13 @@
     share = acc.shape[1] // 2
     keep_ref[...] = acc[:, :share]
     for r in range(QUAD):
-        send_ref[(r ^ 1) * rows : ((r ^ 1) + 1) * rows, :] = acc[r * rows : (r + 1) * rows, share:]
+        send_ref[(r ^ 1) * rows : ((r ^ 1) + 1) * rows, :] = acc[r * rows : (r + 1) * rows, share:].astype(BF16)
 
 
 def project_kernel(width, me_ref, keep_ref, came_ref, b0, b1, b2, b3, *refs):
     own_ref, outs, total = refs[0], refs[1:-1], refs[-1]
     zi = me_ref[0] // QUAD
-    applied = (keep_ref[...] + came_ref[...]).astype(BF16)
+    applied = (keep_ref[...] + came_ref[...].astype(F32)).astype(BF16)
     b_all = jnp.concatenate([r[...] for r in (b0, b1, b2, b3)], axis=0)
     total[...] = dot(applied, b_all, 0, 0)
     for m in range(len(outs) + 1):
@@ -134,16 +134,18 @@
     o_c, b_c = swap(orbitals, 1), swap(basis, 1)
     x_hops = first_hops(x)
     far = jnp.concatenate([a for m, a in zip(order, other_hops(orbitals, o_hops)) if m and m not in o_hops], axis=0)
-    far, k_y, near_y, o_c, b_c, *x_first = barrier((far, k_y, near_y, o_c, b_c, *x_hops.values()))
+    b_yc = swap(b_y, 1)
+    k_y, near_y, o_c, b_c, b_yc, *x_first = barrier((k_y, near_y, o_c, b_c, b_yc, *x_hops.values()))
     k_yc, far_y = swap(k_c, 2), swap(far, 2)
     xs = other_hops(x, dict(zip(x_hops, x_first)))
-    o_yc, b_yc = swap(near_y[:rows], 1), swap(b_y, 1)
+    o_yc = swap(near_y[:rows], 1)
     places = [0, *o_hops, *(m for m in order if m and m not in o_hops)]
     xs = [xs[order.index(m)] for m in places]
-    block = jax.ShapeDtypeStruct((QUAD * rows, share), F32)
+    kept = jax.ShapeDtypeStruct((QUAD * rows, share), F32)
+    sent = jax.ShapeDtypeStruct((QUAD * rows, share), BF16)
     keep, send = call(
         functools.partial(apply_kernel, tuple(places)),
-        (block, block),
+        (kept, sent),
         where,
         (near, far, near_y, far_y, o_c, o_yc, k_keep, k_c, k_y, k_yc, *xs),
         QUAD * rows * points * (orbitals.shape[1] + 2 * share),
@@ -157,7 +159,7 @@
         scratch=(pltpu.VMEM((share, columns), F32),),
     )
     total = parts[0]
-    for m in range(1, nz):
+    for m in range(nz - 1, 0, -1):
         total = total + swap(parts[m], QUAD * m).astype(F32)
     return total.T
 

time: 57.5 us -> 56.6 us (0.984)
  starting transfers between devices: 20.7 us -> 19.9 us
    ppermute x20, starting transfers between devices: 20.7 us -> 19.9 us  [swap(): return lax.ppermute(a, 'row', [(i, i ^ bit) for i in range(n)])]
  transfers between devices with their start and end apart: 20 -> 20, of which waited for: 13 -> 10; matrix products, arithmetic and copies ran while one was open for 0% -> 0% of each run, Pallas kernels for 1% -> 1%
where the time goes in v3:
time: 56.6 us; the launch traced here: 56.4 us
  waiting for transfers between devices  31.4 us (55%)
  starting transfers between devices  19.9 us (35%)
  Pallas kernels  2.69 us (5%)
  local copies, waits for them, and re-layouts  1.55 us (3%)
  other arithmetic  0.76 us (1%)
    ppermute x20, waiting for transfers between devices, swap(): return lax.ppermute(a, 'row', [(i, i ^ bit) for i in range(n)])  31.4 us
    ppermute x20, starting transfers between devices, swap(): return lax.ppermute(a, 'row', [(i, i ^ bit) for i in range(n)])  19.9 us
    pallas_call x4, Pallas kernels, call(): pl.pallas_call(body, out_shape=list(outs), in_specs=[pl.BlockSpec(memory_...  2.69 us
    unnamed x8, local copies, waits for them, and re-layouts  1.53 us
  transfers between devices with their start and end apart: 20, of which 10 were waited for; matrix products, arithmetic and copies ran while one was open for 0% of the time, Pallas kernels for 1%

profile of v3, /device:TPU:0, one launch (start us, length us, event | category | flops | bytes accessed | tf_op | source)
XLA Modules:
  0.0 56.4 jit_solution(17440500206529142837)
XLA Ops:
  0.0 4.0 %collective-permute-start = (bf16[128,512]{1,0:T(8,128)(2,1)}, bf16[128,512]{1,0:T(8,128)(2,1)S(1)}, u32[]{:S(2)}, u32[]{:S(2)}) collective-permute-start(bf16[128,512]{1,0:T(8,128)(2,1)} %param.3), channel_id=1, source_target_pairs={{0,8},{1,9},{2,10},{3,11},{4,12},{5,13},{6,14},{7,15},{8,0},{9,1},... | collective-permute-start | bytes 393224 | tf_op jit(solution)/shard_map/ppermute | solution.py:99
  4.0 1.6 %collective-permute-start.1 = (bf16[128,512]{1,0:T(8,128)(2,1)}, bf16[128,512]{1,0:T(8,128)(2,1)S(1)}, u32[]{:S(2)}, u32[]{:S(2)}) collective-permute-start(bf16[128,512]{1,0:T(8,128)(2,1)} %param.3), channel_id=1, source_target_pairs={{0,4},{1,5},{2,6},{3,7},{4,0},{5,1},{6,2},{7,3},{8,12},{9,13},{10,... | collective-permute-start | bytes 393224 | tf_op jit(solution)/shard_map/ppermute | solution.py:99
  5.6 1.5 %collective-permute-start.3 = (bf16[128,1024]{1,0:T(8,128)(2,1)}, bf16[128,1024]{1,0:T(8,128)(2,1)S(1)}, u32[]{:S(2)}, u32[]{:S(2)}) collective-permute-start(bf16[128,1024]{1,0:T(8,128)(2,1)} %b0.1), channel_id=1, source_target_pairs={{0,2},{1,3},{2,0},{3,1},{4,6},{5,7},{6,4},{7,5},{8,10},{9,11},{10,... | collective-permute-start | bytes 786440 | tf_op jit(solution)/shard_map/ppermute | solution.py:99
  7.1 1.0 %copy-done = bf16[128,2048]{1,0:T(8,128)(2,1)S(1)} copy-done((bf16[128,2048]{1,0:T(8,128)(2,1)S(1)}, bf16[128,2048]{1,0:T(8,128)(2,1)}, u32[]{:S(2)}) %copy-start) | copy-done | bytes 524312
  9.1 1.5 %collective-permute-done = bf16[128,512]{1,0:T(8,128)(2,1)S(1)} collective-permute-done((bf16[128,512]{1,0:T(8,128)(2,1)}, bf16[128,512]{1,0:T(8,128)(2,1)S(1)}, u32[]{:S(2)}, u32[]{:S(2)}) %collective-permute-start) | collective-permute-done | bytes 131104 | tf_op jit(solution)/shard_map/ppermute | solution.py:99
  10.9 1.6 %collective-permute-start.6 = (bf16[384,512]{1,0:T(8,128)(2,1)S(1)}, bf16[384,512]{1,0:T(8,128)(2,1)S(1)}, u32[]{:S(2)}, u32[]{:S(2)}) collective-permute-start(bf16[384,512]{1,0:T(8,128)(2,1)S(1)} %constant_dynamic-update-slice_fusion.near), channel_id=1, source_target_pairs={{0,2},{1,3},{2,0},{3,1},{4,6},{5,7},{6,4},{7,5},{8,10},{9,11},{10,... | collective-permute-start | bytes 1179656 | tf_op jit(solution)/shard_map/ppermute | solution.py:99
  12.5 2.4 %collective-permute-done.3.y_ref.b2 = bf16[128,1024]{1,0:T(8,128)(2,1)S(1)} collective-permute-done((bf16[128,1024]{1,0:T(8,128)(2,1)}, bf16[128,1024]{1,0:T(8,128)(2,1)S(1)}, u32[]{:S(2)}, u32[]{:S(2)}) %collective-permute-start.3) | collective-permute-done | bytes 262176 | tf_op jit(solution)/shard_map/ppermute | solution.py:99
  15.4 0.5 collective-permute-start.11
  15.9 0.9 %collective-permute-start.10 = (bf16[256,512]{1,0:T(8,128)(2,1)S(1)}, bf16[256,512]{1,0:T(8,128)(2,1)S(1)}, u32[]{:S(2)}, u32[]{:S(2)}) collective-permute-start(bf16[256,512]{1,0:T(8,128)(2,1)S(1)} %shard_map.38.refs_4_), channel_id=1, source_target_pairs={{0,8},{1,9},{2,10},{3,11},{4,12},{5,13},{6,14},{7,15},{8,0},{9,1},... | collective-permute-start | bytes 786440 | tf_op jit(solution)/shard_map/ppermute | solution.py:99
  16.8 0.6 %collective-permute-start.5 = (bf16[128,1024]{1,0:T(8,128)(2,1)S(1)}, bf16[128,1024]{1,0:T(8,128)(2,1)S(1)}, u32[]{:S(2)}, u32[]{:S(2)}) collective-permute-start(bf16[128,1024]{1,0:T(8,128)(2,1)S(1)} %get-tuple-element.25.refs_0_), channel_id=1, source_target_pairs={{0,2},{1,3},{2,0},{3,1},{4,6},{5,7},{6,4},{7,5},{8,10},{9,11},{10,... | collective-permute-start | bytes 786440 | tf_op jit(solution)/shard_map/ppermute | solution.py:99
  17.4 5.9 %collective-permute-done.6.near_y = bf16[384,512]{1,0:T(8,128)(2,1)S(1)} collective-permute-done((bf16[384,512]{1,0:T(8,128)(2,1)S(1)}, bf16[384,512]{1,0:T(8,128)(2,1)S(1)}, u32[]{:S(2)}, u32[]{:S(2)}) %collective-permute-start.6) | collective-permute-done | bytes 393248 | tf_op jit(solution)/shard_map/ppermute | solution.py:99
  23.4 1.1 %collective-permute-start.2 = (bf16[128,512]{1,0:T(8,128)(2,1)S(1)}, bf16[128,512]{1,0:T(8,128)(2,1)S(1)}, u32[]{:S(2)}, u32[]{:S(2)}) collective-permute-start(bf16[128,512]{1,0:T(8,128)(2,1)S(1)} %collective-permute-done), channel_id=1, source_target_pairs={{0,4},{1,5},{2,6},{3,7},{4,0},{5,1},{6,2},{7,3},{8,12},{9,13},{10,... | collective-permute-start | bytes 393224 | tf_op jit(solution)/shard_map/ppermute | solution.py:99
  24.4 5.4 %collective-permute-done.11.refs_6_ = bf16[256,512]{1,0:T(8,128)(2,1)S(1)} collective-permute-done((bf16[256,512]{1,0:T(8,128)(2,1)S(1)}, bf16[256,512]{1,0:T(8,128)(2,1)S(1)}, u32[]{:S(2)}, u32[]{:S(2)}) %collective-permute-start.11) | collective-permute-done | bytes 262176 | tf_op jit(solution)/shard_map/ppermute | solution.py:99
  29.9 1.5 %collective-permute-start.14 = (bf16[128,1024]{1,0:T(8,128)(2,1)S(1)}, bf16[128,1024]{1,0:T(8,128)(2,1)S(1)}, u32[]{:S(2)}, u32[]{:S(2)}) collective-permute-start(bf16[128,1024]{1,0:T(8,128)(2,1)S(1)} %collective-permute-done.4.refs_1_), channel_id=1, source_target_pairs={{0,2},{1,3},{2,0},{3,1},{4,6},{5,7},{6,4},{7,5},{8,10},{9,11},{10,... | collective-permute-start | bytes 786440 | tf_op jit(solution)/shard_map/ppermute | solution.py:99
  31.9 1.5 %collective-permute-start.12 = (bf16[128,512]{1,0:T(8,128)(2,1)S(1)}, bf16[128,512]{1,0:T(8,128)(2,1)S(1)}, u32[]{:S(2)}, u32[]{:S(2)}) collective-permute-start(bf16[128,512]{1,0:T(8,128)(2,1)S(1)} %collective-permute-done.2.far), channel_id=1, source_target_pairs={{0,2},{1,3},{2,0},{3,1},{4,6},{5,7},{6,4},{7,5},{8,10},{9,11},{10,... | collective-permute-start | bytes 393224 | tf_op jit(solution)/shard_map/ppermute | solution.py:99
  33.5 5.0 %collective-permute-done.12.far_y = bf16[128,512]{1,0:T(8,128)(2,1)S(1)} collective-permute-done((bf16[128,512]{1,0:T(8,128)(2,1)S(1)}, bf16[128,512]{1,0:T(8,128)(2,1)S(1)}, u32[]{:S(2)}, u32[]{:S(2)}) %collective-permute-start.12) | collective-permute-done | bytes 131104 | tf_op jit(solution)/shard_map/ppermute | solution.py:99
  38.5 1.6 %shard_map.39 = (f32[512,256]{1,0:T(8,128)S(1)}, bf16[512,256]{1,0:T(8,128)(2,1)S(1)}) custom-call(s32[1]{0:T(128)} %bitcast.me_ref, bf16[384,512]{1,0:T(8,128)(2,1)S(1)} %constant_dynamic-update-slice_fusion.near, bf16[128,512]{1,0:T(8,128)(2,1)S(1)} %collective-permute-done.2.far, bf16[384,512]{1,0:T(8,128)(2,1)S(1)} %collective-permute-done.6.near_y, ...), custom_call_target="tpu_custom_call" | custom-call | flops 1073741824 | bytes 4194304 | tf_op jit(solution)/shard_map/pallas_call | solution.py:22
  40.2 1.5 %collective-permute-done.16.came_ref = bf16[512,256]{1,0:T(8,128)(2,1)S(1)} collective-permute-done((bf16[512,256]{1,0:T(8,128)(2,1)S(1)}, bf16[512,256]{1,0:T(8,128)(2,1)S(1)}, u32[]{:S(2)}, u32[]{:S(2)}) %collective-permute-start.16) | collective-permute-done | bytes 262176 | tf_op jit(solution)/shard_map/ppermute | solution.py:99
  41.7 0.5 shard_map.40
  42.3 2.5 %collective-permute-start.17 = (bf16[64,1024]{1,0:T(8,128)(2,1)S(1)}, bf16[64,1024]{1,0:T(8,128)(2,1)S(1)}, u32[]{:S(2)}, u32[]{:S(2)}) collective-permute-start(bf16[64,1024]{1,0:T(8,128)(2,1)S(1)} %get-tuple-element.38), channel_id=1, source_target_pairs={{0,12},{1,13},{2,14},{3,15},{4,8},{5,9},{6,10},{7,11},{8,4},{9,5},... | collective-permute-start | bytes 393224 | tf_op jit(solution)/shard_map/ppermute | solution.py:99
  44.7 2.0 %collective-permute-start.19 = (bf16[64,1024]{1,0:T(8,128)(2,1)S(1)}, bf16[64,1024]{1,0:T(8,128)(2,1)S(1)}, u32[]{:S(2)}, u32[]{:S(2)}) collective-permute-start(bf16[64,1024]{1,0:T(8,128)(2,1)S(1)} %get-tuple-element.40), channel_id=1, source_target_pairs={{0,4},{1,5},{2,6},{3,7},{4,0},{5,1},{6,2},{7,3},{8,12},{9,13},{10,... | collective-permute-start | bytes 393224 | tf_op jit(solution)/shard_map/ppermute | solution.py:99
  46.7 3.9 %collective-permute-done.17 = bf16[64,1024]{1,0:T(8,128)(2,1)S(1)} collective-permute-done((bf16[64,1024]{1,0:T(8,128)(2,1)S(1)}, bf16[64,1024]{1,0:T(8,128)(2,1)S(1)}, u32[]{:S(2)}, u32[]{:S(2)}) %collective-permute-start.17) | collective-permute-done | bytes 131104 | tf_op jit(solution)/shard_map/ppermute | solution.py:99
  50.6 5.1 %collective-permute-done.18 = bf16[64,1024]{1,0:T(8,128)(2,1)S(1)} collective-permute-done((bf16[64,1024]{1,0:T(8,128)(2,1)S(1)}, bf16[64,1024]{1,0:T(8,128)(2,1)S(1)}, u32[]{:S(2)}, u32[]{:S(2)}) %collective-permute-start.18) | collective-permute-done | bytes 131104 | tf_op jit(solution)/shard_map/ppermute | solution.py:99
  55.7 0.8 %add_bitcast_fusion = f32[1024,64]{0,1:T(8,128)} fusion(bf16[64,1024]{1,0:T(8,128)(2,1)S(1)} %collective-permute-done.19, bf16[64,1024]{1,0:T(8,128)(2,1)S(1)} %collective-permute-done.18, f32[64,1024]{1,0:T(8,128)S(1)} %get-tuple-element.37, bf16[64,1024]{1,0:T(8,128)(2,1)S(1)} %collective-permute-done.17), kind=kLoop, calls=%fused_computation | loop fusion | flops 393216 | bytes 917504 | tf_op jit(solution)/shard_map/transpose | solution.py:164
  (31 shorter events, 2.3 us)
Async XLA Ops:
  0.0 10.7 %collective-permute-start = (bf16[128,512]{1,0:T(8,128)(2,1)}, bf16[128,512]{1,0:T(8,128)(2,1)S(1)}, u32[]{:S(2)}, u32[]{:S(2)}) collective-permute-start(bf16[128,512]{1,0:T(8,128)(2,1)} %param.3), channel_id=1, source_target_pairs={{0,8},{1,9},{2,10},{3,11},{4,12},{5,13},{6,14},{7,15},{8,0},{9,1},... | collective-permute-start | bytes 393224 | tf_op jit(solution)/shard_map/ppermute | solution.py:99
  4.0 6.8 %collective-permute-start.1 = (bf16[128,512]{1,0:T(8,128)(2,1)}, bf16[128,512]{1,0:T(8,128)(2,1)S(1)}, u32[]{:S(2)}, u32[]{:S(2)}) collective-permute-start(bf16[128,512]{1,0:T(8,128)(2,1)} %param.3), channel_id=1, source_target_pairs={{0,4},{1,5},{2,6},{3,7},{4,0},{5,1},{6,2},{7,3},{8,12},{9,13},{10,... | collective-permute-start | bytes 393224 | tf_op jit(solution)/shard_map/ppermute | solution.py:99
  5.6 11.8 %collective-permute-start.8 = (bf16[128,1024]{1,0:T(8,128)(2,1)}, bf16[128,1024]{1,0:T(8,128)(2,1)S(1)}, u32[]{:S(2)}, u32[]{:S(2)}) collective-permute-start(bf16[128,1024]{1,0:T(8,128)(2,1)} %b0.1), channel_id=1, source_target_pairs={{0,1},{1,0},{2,3},{3,2},{4,5},{5,4},{6,7},{7,6},{8,9},{9,8},{10,11... | collective-permute-start | bytes 786440 | tf_op jit(solution)/shard_map/ppermute | solution.py:99
  5.6 9.3 %collective-permute-start.3 = (bf16[128,1024]{1,0:T(8,128)(2,1)}, bf16[128,1024]{1,0:T(8,128)(2,1)S(1)}, u32[]{:S(2)}, u32[]{:S(2)}) collective-permute-start(bf16[128,1024]{1,0:T(8,128)(2,1)} %b0.1), channel_id=1, source_target_pairs={{0,2},{1,3},{2,0},{3,1},{4,6},{5,7},{6,4},{7,5},{8,10},{9,11},{10,... | collective-permute-start | bytes 786440 | tf_op jit(solution)/shard_map/ppermute | solution.py:99
  7.1 1.0 %copy-start = (bf16[128,2048]{1,0:T(8,128)(2,1)S(1)}, bf16[128,2048]{1,0:T(8,128)(2,1)}, u32[]{:S(2)}) copy-start(bf16[128,2048]{1,0:T(8,128)(2,1)} %k_ref.1) | copy-start | bytes 1572868
  8.2 0.9 %copy-start.2 = (bf16[128,512]{1,0:T(8,128)(2,1)S(1)}, bf16[128,512]{1,0:T(8,128)(2,1)}, u32[]{:S(2)}) copy-start(bf16[128,512]{1,0:T(8,128)(2,1)} %param.3) | copy-start | bytes 393220
  8.3 6.6 %collective-permute-start.4 = (bf16[128,1024]{1,0:T(8,128)(2,1)S(1)}, bf16[128,1024]{1,0:T(8,128)(2,1)S(1)}, u32[]{:S(2)}, u32[]{:S(2)}) collective-permute-start(bf16[128,1024]{1,0:T(8,128)(2,1)S(1)} %get-tuple-element.23), channel_id=1, source_target_pairs={{0,1},{1,0},{2,3},{3,2},{4,5},{5,4},{6,7},{7,6},{8,9},{9,8},{10,11... | collective-permute-start | bytes 786440 | tf_op jit(solution)/shard_map/ppermute | solution.py:99
  9.1 5.8 %copy-start.1 = (bf16[128,1024]{1,0:T(8,128)(2,1)S(1)}, bf16[128,1024]{1,0:T(8,128)(2,1)}, u32[]{:S(2)}) copy-start(bf16[128,1024]{1,0:T(8,128)(2,1)} %b0.1) | copy-start | bytes 786436
  10.9 12.5 %collective-permute-start.6 = (bf16[384,512]{1,0:T(8,128)(2,1)S(1)}, bf16[384,512]{1,0:T(8,128)(2,1)S(1)}, u32[]{:S(2)}, u32[]{:S(2)}) collective-permute-start(bf16[384,512]{1,0:T(8,128)(2,1)S(1)} %constant_dynamic-update-slice_fusion.near), channel_id=1, source_target_pairs={{0,2},{1,3},{2,0},{3,1},{4,6},{5,7},{6,4},{7,5},{8,10},{9,11},{10,... | collective-permute-start | bytes 1179656 | tf_op jit(solution)/shard_map/ppermute | solution.py:99
  12.5 4.3 %collective-permute-start.7 = (bf16[128,512]{1,0:T(8,128)(2,1)S(1)}, bf16[128,512]{1,0:T(8,128)(2,1)S(1)}, u32[]{:S(2)}, u32[]{:S(2)}) collective-permute-start(bf16[128,512]{1,0:T(8,128)(2,1)S(1)} %copy-done.2), channel_id=1, source_target_pairs={{0,1},{1,0},{2,3},{3,2},{4,5},{5,4},{6,7},{7,6},{8,9},{9,8},{10,11... | collective-permute-start | bytes 393224 | tf_op jit(solution)/shard_map/ppermute | solution.py:99
  15.4 14.5 %collective-permute-start.11 = (bf16[256,512]{1,0:T(8,128)(2,1)S(1)}, bf16[256,512]{1,0:T(8,128)(2,1)S(1)}, u32[]{:S(2)}, u32[]{:S(2)}) collective-permute-start(bf16[256,512]{1,0:T(8,128)(2,1)S(1)} %shard_map.38.refs_4_), channel_id=1, source_target_pairs={{0,4},{1,5},{2,6},{3,7},{4,0},{5,1},{6,2},{7,3},{8,12},{9,13},{10,... | collective-permute-start | bytes 786440 | tf_op jit(solution)/shard_map/ppermute | solution.py:99
  15.9 15.5 %collective-permute-start.10 = (bf16[256,512]{1,0:T(8,128)(2,1)S(1)}, bf16[256,512]{1,0:T(8,128)(2,1)S(1)}, u32[]{:S(2)}, u32[]{:S(2)}) collective-permute-start(bf16[256,512]{1,0:T(8,128)(2,1)S(1)} %shard_map.38.refs_4_), channel_id=1, source_target_pairs={{0,8},{1,9},{2,10},{3,11},{4,12},{5,13},{6,14},{7,15},{8,0},{9,1},... | collective-permute-start | bytes 786440 | tf_op jit(solution)/shard_map/ppermute | solution.py:99
  16.8 14.6 %collective-permute-start.5 = (bf16[128,1024]{1,0:T(8,128)(2,1)S(1)}, bf16[128,1024]{1,0:T(8,128)(2,1)S(1)}, u32[]{:S(2)}, u32[]{:S(2)}) collective-permute-start(bf16[128,1024]{1,0:T(8,128)(2,1)S(1)} %get-tuple-element.25.refs_0_), channel_id=1, source_target_pairs={{0,2},{1,3},{2,0},{3,1},{4,6},{5,7},{6,4},{7,5},{8,10},{9,11},{10,... | collective-permute-start | bytes 786440 | tf_op jit(solution)/shard_map/ppermute | solution.py:99
  17.4 14.0 %collective-permute-start.9 = (bf16[128,1024]{1,0:T(8,128)(2,1)S(1)}, bf16[128,1024]{1,0:T(8,128)(2,1)S(1)}, u32[]{:S(2)}, u32[]{:S(2)}) collective-permute-start(bf16[128,1024]{1,0:T(8,128)(2,1)S(1)} %collective-permute-done.3.y_ref.b2), channel_id=1, source_target_pairs={{0,1},{1,0},{2,3},{3,2},{4,5},{5,4},{6,7},{7,6},{8,9},{9,8},{10,11... | collective-permute-start | bytes 786440 | tf_op jit(solution)/shard_map/ppermute | solution.py:99
  23.4 8.5 %collective-permute-start.2 = (bf16[128,512]{1,0:T(8,128)(2,1)S(1)}, bf16[128,512]{1,0:T(8,128)(2,1)S(1)}, u32[]{:S(2)}, u32[]{:S(2)}) collective-permute-start(bf16[128,512]{1,0:T(8,128)(2,1)S(1)} %collective-permute-done), channel_id=1, source_target_pairs={{0,4},{1,5},{2,6},{3,7},{4,0},{5,1},{6,2},{7,3},{8,12},{9,13},{10,... | collective-permute-start | bytes 393224 | tf_op jit(solution)/shard_map/ppermute | solution.py:99
  29.9 8.7 %collective-permute-start.14 = (bf16[128,1024]{1,0:T(8,128)(2,1)S(1)}, bf16[128,1024]{1,0:T(8,128)(2,1)S(1)}, u32[]{:S(2)}, u32[]{:S(2)}) collective-permute-start(bf16[128,1024]{1,0:T(8,128)(2,1)S(1)} %collective-permute-done.4.refs_1_), channel_id=1, source_target_pairs={{0,2},{1,3},{2,0},{3,1},{4,6},{5,7},{6,4},{7,5},{8,10},{9,11},{10,... | collective-permute-start | bytes 786440 | tf_op jit(solution)/shard_map/ppermute | solution.py:99
  31.4 7.1 %collective-permute-start.15 = (bf16[256,512]{1,0:T(8,128)(2,1)S(1)}, bf16[256,512]{1,0:T(8,128)(2,1)S(1)}, u32[]{:S(2)}, u32[]{:S(2)}) collective-permute-start(bf16[256,512]{1,0:T(8,128)(2,1)S(1)} %collective-permute-done.10.refs_5_), channel_id=1, source_target_pairs={{0,4},{1,5},{2,6},{3,7},{4,0},{5,1},{6,2},{7,3},{8,12},{9,13},{10,... | collective-permute-start | bytes 786440 | tf_op jit(solution)/shard_map/ppermute | solution.py:99
  31.9 6.6 %collective-permute-start.12 = (bf16[128,512]{1,0:T(8,128)(2,1)S(1)}, bf16[128,512]{1,0:T(8,128)(2,1)S(1)}, u32[]{:S(2)}, u32[]{:S(2)}) collective-permute-start(bf16[128,512]{1,0:T(8,128)(2,1)S(1)} %collective-permute-done.2.far), channel_id=1, source_target_pairs={{0,2},{1,3},{2,0},{3,1},{4,6},{5,7},{6,4},{7,5},{8,10},{9,11},{10,... | collective-permute-start | bytes 393224 | tf_op jit(solution)/shard_map/ppermute | solution.py:99
  33.4 5.1 %collective-permute-start.13 = (bf16[128,512]{1,0:T(8,128)(2,1)S(1)}, bf16[128,512]{1,0:T(8,128)(2,1)S(1)}, u32[]{:S(2)}, u32[]{:S(2)}) collective-permute-start(bf16[128,512]{1,0:T(8,128)(2,1)S(1)} %slice.3), channel_id=1, source_target_pairs={{0,1},{1,0},{2,3},{3,2},{4,5},{5,4},{6,7},{7,6},{8,9},{9,8},{10,11... | collective-permute-start | bytes 393224 | tf_op jit(solution)/shard_map/ppermute | solution.py:99
  40.1 1.6 %collective-permute-start.16 = (bf16[512,256]{1,0:T(8,128)(2,1)S(1)}, bf16[512,256]{1,0:T(8,128)(2,1)S(1)}, u32[]{:S(2)}, u32[]{:S(2)}) collective-permute-start(bf16[512,256]{1,0:T(8,128)(2,1)S(1)} %get-tuple-element.34), channel_id=1, source_target_pairs={{0,1},{1,0},{2,3},{3,2},{4,5},{5,4},{6,7},{7,6},{8,9},{9,8},{10,11... | collective-permute-start | bytes 786440 | tf_op jit(solution)/shard_map/ppermute | solution.py:99
  42.3 8.3 %collective-permute-start.17 = (bf16[64,1024]{1,0:T(8,128)(2,1)S(1)}, bf16[64,1024]{1,0:T(8,128)(2,1)S(1)}, u32[]{:S(2)}, u32[]{:S(2)}) collective-permute-start(bf16[64,1024]{1,0:T(8,128)(2,1)S(1)} %get-tuple-element.38), channel_id=1, source_target_pairs={{0,12},{1,13},{2,14},{3,15},{4,8},{5,9},{6,10},{7,11},{8,4},{9,5},... | collective-permute-start | bytes 393224 | tf_op jit(solution)/shard_map/ppermute | solution.py:99
  44.7 10.9 %collective-permute-start.18 = (bf16[64,1024]{1,0:T(8,128)(2,1)S(1)}, bf16[64,1024]{1,0:T(8,128)(2,1)S(1)}, u32[]{:S(2)}, u32[]{:S(2)}) collective-permute-start(bf16[64,1024]{1,0:T(8,128)(2,1)S(1)} %get-tuple-element.39), channel_id=1, source_target_pairs={{0,8},{1,9},{2,10},{3,11},{4,12},{5,13},{6,14},{7,15},{8,0},{9,1},... | collective-permute-start | bytes 393224 | tf_op jit(solution)/shard_map/ppermute | solution.py:99
  44.7 10.9 %collective-permute-start.19 = (bf16[64,1024]{1,0:T(8,128)(2,1)S(1)}, bf16[64,1024]{1,0:T(8,128)(2,1)S(1)}, u32[]{:S(2)}, u32[]{:S(2)}) collective-permute-start(bf16[64,1024]{1,0:T(8,128)(2,1)S(1)} %get-tuple-element.40), channel_id=1, source_target_pairs={{0,4},{1,5},{2,6},{3,7},{4,0},{5,1},{6,2},{7,3},{8,12},{9,13},{10,... | collective-permute-start | bytes 393224 | tf_op jit(solution)/shard_map/ppermute | solution.py:99

commit v4 on v3

--- a/solution.py
+++ b/solution.py
@@ -51,34 +51,52 @@
             x_ref[s * rows : (s + 1) * rows, c * share : (c + 1) * share] = dot(b[...], picker, 1, 0).astype(BF16)
 
 
-def apply_kernel(order, me_ref, near, far, near_y, far_y, oc_ref, oyc_ref, *refs):
-    nz = len(order)
+def weigh(o_rows, o_cols, ks, me, m):
+    rows = o_cols[0].shape[0]
+    density = dot(o_rows, jnp.concatenate(o_cols, axis=0), 1, 1)
+    at = [pl.multiple_of((2 * (me // QUAD ^ m) + (me // 2 % 2 ^ s)) * rows, rows) for s in (0, 1)]
+    k_block = jnp.concatenate(
+        [jnp.concatenate([kr[:, pl.ds(a, rows)] for a in at], axis=1) for kr in ks], axis=0
+    )
+    return (density * k_block.astype(F32)).astype(BF16)
+
+
+def early_kernel(planes, me_ref, near, near_y, oc_ref, k_keep, k_c, k_y, *refs):
+    rows = oc_ref.shape[0]
+    o_rows = jnp.concatenate([near[0:rows, :], oc_ref[...], near_y[0:rows, :]], axis=0)
+    acc = None
+    for i, m in enumerate(planes):
+        o_cols = [r[i * rows : (i + 1) * rows, :] for r in (near, near_y)]
+        term = dot(weigh(o_rows, o_cols, (k_keep, k_c, k_y), me_ref[0], m), refs[i][...], 1, 0)
+        acc = term if acc is None else acc + term
+    refs[-1][...] = acc
+
+
+def apply_kernel(planes, me_ref, early, near, far, near_y, far_y, oc_ref, oyc_ref, *refs):
+    nz = len(planes)
     k, x, (keep_ref, send_ref) = refs[0:4], refs[4 : 4 + nz], refs[4 + nz :]
-    rows = k[0].shape[0]
-    zi, y = me_ref[0] // QUAD, (me_ref[0] // 2) % 2
-    o_rows = jnp.concatenate([r[0:rows, :] for r in (near, oc_ref, near_y, oyc_ref)], axis=0)
-    acc = None
-    for i, m in enumerate(order):
-        held, at = ((near, near_y), i * rows) if i * rows < near.shape[0] else ((far, far_y), i * rows - near.shape[0])
-        o_cols = jnp.concatenate([r[at : at + rows, :] for r in held], axis=0)
-        density = dot(o_rows, o_cols, 1, 1)
-        at = [pl.multiple_of((2 * (zi ^ m) + (y ^ s)) * rows, rows) for s in (0, 1)]
-        k_block = jnp.concatenate(
-            [jnp.concatenate([kr[:, pl.ds(a, rows)] for a in at], axis=1) for kr in k], axis=0
-        )
-        weighted = (density * k_block.astype(F32)).astype(BF16)
-        term = dot(weighted, x[i][...], 1, 0)
-        acc = term if acc is None else acc + term
-    share = acc.shape[1] // 2
-    keep_ref[...] = acc[:, :share]
+    rows = oc_ref.shape[0]
+    o_rows = jnp.concatenate([near[0:rows, :], oc_ref[...], near_y[0:rows, :]], axis=0)
+    top, last = early[...], None
+    for i, m in enumerate(planes):
+        late = i * rows >= near.shape[0]
+        held, at = ((far, far_y), i * rows - near.shape[0]) if late else ((near, near_y), i * rows)
+        o_cols = [r[at : at + rows, :] for r in held]
+        if late:
+            top += dot(weigh(o_rows, o_cols, k[:3], me_ref[0], m), x[i][...], 1, 0)
+        term = dot(weigh(oyc_ref[...], o_cols, k[3:], me_ref[0], m), x[i][...], 1, 0)
+        last = term if last is None else last + term
+    share = top.shape[1] // 2
     for r in range(QUAD):
-        send_ref[(r ^ 1) * rows : ((r ^ 1) + 1) * rows, :] = acc[r * rows : (r + 1) * rows, share:].astype(BF16)
+        part = last if r == QUAD - 1 else top[r * rows : (r + 1) * rows, :]
+        keep_ref[r * rows : (r + 1) * rows, :] = part[:, :share]
+        send_ref[(r ^ 1) * rows : ((r ^ 1) + 1) * rows, :] = part[:, share:]
 
 
 def project_kernel(width, me_ref, keep_ref, came_ref, b0, b1, b2, b3, *refs):
     own_ref, outs, total = refs[0], refs[1:-1], refs[-1]
     zi = me_ref[0] // QUAD
-    applied = (keep_ref[...] + came_ref[...].astype(F32)).astype(BF16)
+    applied = (keep_ref[...] + came_ref[...]).astype(BF16)
     b_all = jnp.concatenate([r[...] for r in (b0, b1, b2, b3)], axis=0)
     total[...] = dot(applied, b_all, 0, 0)
     for m in range(len(outs) + 1):
@@ -141,14 +159,21 @@
     o_yc = swap(near_y[:rows], 1)
     places = [0, *o_hops, *(m for m in order if m and m not in o_hops)]
     xs = [xs[order.index(m)] for m in places]
-    kept = jax.ShapeDtypeStruct((QUAD * rows, share), F32)
-    sent = jax.ShapeDtypeStruct((QUAD * rows, share), BF16)
+    block = jax.ShapeDtypeStruct((QUAD * rows, share), F32)
+    n_near = 1 + len(o_hops)
+    (early,) = call(
+        functools.partial(early_kernel, tuple(places[:n_near])),
+        (jax.ShapeDtypeStruct((3 * rows, 2 * share), F32),),
+        where,
+        (near, near_y, o_c, k_keep, k_c, k_y, *xs[:n_near]),
+        12 * rows * n_near * rows * (orbitals.shape[1] + 2 * share),
+    )
     keep, send = call(
         functools.partial(apply_kernel, tuple(places)),
-        (kept, sent),
-        where,
-        (near, far, near_y, far_y, o_c, o_yc, k_keep, k_c, k_y, k_yc, *xs),
-        QUAD * rows * points * (orbitals.shape[1] + 2 * share),
+        (block, block),
+        where,
+        (early, near, far, near_y, far_y, o_c, o_yc, k_keep, k_c, k_y, k_yc, *xs),
+        QUAD * rows * points * (orbitals.shape[1] + 2 * share) // 2,
     )
     parts = call(
         functools.partial(project_kernel, width),

time: 56.6 us -> 56.7 us (level)
  Pallas kernels: 2.69 us -> 3.5 us
  waiting for transfers between devices: 31.4 us -> 30.7 us
    pallas_call x4 -> x5, Pallas kernels: 2.69 us -> 3.5 us  [call(): pl.pallas_call(body, out_shape=list(outs), in_specs=[pl.BlockSpec(memory_...]
    ppermute x20, waiting for transfers between devices: 31.4 us -> 30.7 us  [swap(): return lax.ppermute(a, 'row', [(i, i ^ bit) for i in range(n)])]
  transfers between devices with their start and end apart: 20 -> 20, of which waited for: 10 -> 10; matrix products, arithmetic and copies ran while one was open for 0% -> 0% of each run, Pallas kernels for 1% -> 3%
where the time goes in v4:
time: 56.7 us; the launch traced here: 56.5 us
  waiting for transfers between devices  30.7 us (54%)
  starting transfers between devices  19.9 us (35%)
  Pallas kernels  3.5 us (6%)
  local copies, waits for them, and re-layouts  1.55 us (3%)
  other arithmetic  0.76 us (1%)
    ppermute x20, waiting for transfers between devices, swap(): return lax.ppermute(a, 'row', [(i, i ^ bit) for i in range(n)])  30.7 us
    ppermute x20, starting transfers between devices, swap(): return lax.ppermute(a, 'row', [(i, i ^ bit) for i in range(n)])  19.9 us
    pallas_call x5, Pallas kernels, call(): pl.pallas_call(body, out_shape=list(outs), in_specs=[pl.BlockSpec(memory_...  3.5 us
    unnamed x8, local copies, waits for them, and re-layouts  1.53 us
  transfers between devices with their start and end apart: 20, of which 10 were waited for; matrix products, arithmetic and copies ran while one was open for 0% of the time, Pallas kernels for 3%

profile of v4, /device:TPU:0, one launch (start us, length us, event | category | flops | bytes accessed | tf_op | source)
XLA Modules:
  0.0 56.5 jit_solution(9090562358894664309)
XLA Ops:
  0.0 4.0 %collective-permute-start = (bf16[128,512]{1,0:T(8,128)(2,1)}, bf16[128,512]{1,0:T(8,128)(2,1)S(1)}, u32[]{:S(2)}, u32[]{:S(2)}) collective-permute-start(bf16[128,512]{1,0:T(8,128)(2,1)} %param.3), channel_id=1, source_target_pairs={{0,8},{1,9},{2,10},{3,11},{4,12},{5,13},{6,14},{7,15},{8,0},{9,1},... | collective-permute-start | bytes 393224 | tf_op jit(solution)/shard_map/ppermute | solution.py:117
  4.0 1.6 %collective-permute-start.1 = (bf16[128,512]{1,0:T(8,128)(2,1)}, bf16[128,512]{1,0:T(8,128)(2,1)S(1)}, u32[]{:S(2)}, u32[]{:S(2)}) collective-permute-start(bf16[128,512]{1,0:T(8,128)(2,1)} %param.3), channel_id=1, source_target_pairs={{0,4},{1,5},{2,6},{3,7},{4,0},{5,1},{6,2},{7,3},{8,12},{9,13},{10,... | collective-permute-start | bytes 393224 | tf_op jit(solution)/shard_map/ppermute | solution.py:117
  5.6 1.5 %collective-permute-start.2 = (bf16[128,1024]{1,0:T(8,128)(2,1)}, bf16[128,1024]{1,0:T(8,128)(2,1)S(1)}, u32[]{:S(2)}, u32[]{:S(2)}) collective-permute-start(bf16[128,1024]{1,0:T(8,128)(2,1)} %b0.1), channel_id=1, source_target_pairs={{0,2},{1,3},{2,0},{3,1},{4,6},{5,7},{6,4},{7,5},{8,10},{9,11},{10,... | collective-permute-start | bytes 786440 | tf_op jit(solution)/shard_map/ppermute | solution.py:117
  7.1 1.0 %copy-done = bf16[128,2048]{1,0:T(8,128)(2,1)S(1)} copy-done((bf16[128,2048]{1,0:T(8,128)(2,1)S(1)}, bf16[128,2048]{1,0:T(8,128)(2,1)}, u32[]{:S(2)}) %copy-start) | copy-done | bytes 524312
  9.1 1.5 %collective-permute-done = bf16[128,512]{1,0:T(8,128)(2,1)S(1)} collective-permute-done((bf16[128,512]{1,0:T(8,128)(2,1)}, bf16[128,512]{1,0:T(8,128)(2,1)S(1)}, u32[]{:S(2)}, u32[]{:S(2)}) %collective-permute-start) | collective-permute-done | bytes 131104 | tf_op jit(solution)/shard_map/ppermute | solution.py:117
  10.9 1.6 %collective-permute-start.5 = (bf16[384,512]{1,0:T(8,128)(2,1)S(1)}, bf16[384,512]{1,0:T(8,128)(2,1)S(1)}, u32[]{:S(2)}, u32[]{:S(2)}) collective-permute-start(bf16[384,512]{1,0:T(8,128)(2,1)S(1)} %constant_dynamic-update-slice_fusion.near), channel_id=1, source_target_pairs={{0,2},{1,3},{2,0},{3,1},{4,6},{5,7},{6,4},{7,5},{8,10},{9,11},{10,... | collective-permute-start | bytes 1179656 | tf_op jit(solution)/shard_map/ppermute | solution.py:117
  12.5 2.4 %collective-permute-done.2.y_ref.b2 = bf16[128,1024]{1,0:T(8,128)(2,1)S(1)} collective-permute-done((bf16[128,1024]{1,0:T(8,128)(2,1)}, bf16[128,1024]{1,0:T(8,128)(2,1)S(1)}, u32[]{:S(2)}, u32[]{:S(2)}) %collective-permute-start.2) | collective-permute-done | bytes 262176 | tf_op jit(solution)/shard_map/ppermute | solution.py:117
  15.9 0.9 %collective-permute-start.9 = (bf16[256,512]{1,0:T(8,128)(2,1)S(1)}, bf16[256,512]{1,0:T(8,128)(2,1)S(1)}, u32[]{:S(2)}, u32[]{:S(2)}) collective-permute-start(bf16[256,512]{1,0:T(8,128)(2,1)S(1)} %shard_map.38.refs_0_.refs_4_), channel_id=1, source_target_pairs={{0,8},{1,9},{2,10},{3,11},{4,12},{5,13},{6,14},{7,15},{8,0},{9,1},... | collective-permute-start | bytes 786440 | tf_op jit(solution)/shard_map/ppermute | solution.py:117
  16.8 0.6 %collective-permute-start.4 = (bf16[128,1024]{1,0:T(8,128)(2,1)S(1)}, bf16[128,1024]{1,0:T(8,128)(2,1)S(1)}, u32[]{:S(2)}, u32[]{:S(2)}) collective-permute-start(bf16[128,1024]{1,0:T(8,128)(2,1)S(1)} %get-tuple-element.25.k_keep.refs_0_), channel_id=1, source_target_pairs={{0,2},{1,3},{2,0},{3,1},{4,6},{5,7},{6,4},{7,5},{8,10},{9,11},{10,... | collective-permute-start | bytes 786440 | tf_op jit(solution)/shard_map/ppermute | solution.py:117
  17.4 5.9 %collective-permute-done.5.near_y = bf16[384,512]{1,0:T(8,128)(2,1)S(1)} collective-permute-done((bf16[384,512]{1,0:T(8,128)(2,1)S(1)}, bf16[384,512]{1,0:T(8,128)(2,1)S(1)}, u32[]{:S(2)}, u32[]{:S(2)}) %collective-permute-start.5) | collective-permute-done | bytes 393248 | tf_op jit(solution)/shard_map/ppermute | solution.py:117
  23.4 1.1 %collective-permute-start.11 = (bf16[128,512]{1,0:T(8,128)(2,1)S(1)}, bf16[128,512]{1,0:T(8,128)(2,1)S(1)}, u32[]{:S(2)}, u32[]{:S(2)}) collective-permute-start(bf16[128,512]{1,0:T(8,128)(2,1)S(1)} %collective-permute-done), channel_id=1, source_target_pairs={{0,4},{1,5},{2,6},{3,7},{4,0},{5,1},{6,2},{7,3},{8,12},{9,13},{10,... | collective-permute-start | bytes 393224 | tf_op jit(solution)/shard_map/ppermute | solution.py:117
  24.4 5.4 %collective-permute-done.10.refs_2_.refs_6_ = bf16[256,512]{1,0:T(8,128)(2,1)S(1)} collective-permute-done((bf16[256,512]{1,0:T(8,128)(2,1)S(1)}, bf16[256,512]{1,0:T(8,128)(2,1)S(1)}, u32[]{:S(2)}, u32[]{:S(2)}) %collective-permute-start.10) | collective-permute-done | bytes 262176 | tf_op jit(solution)/shard_map/ppermute | solution.py:117
  29.9 1.5 %collective-permute-start.14 = (bf16[128,1024]{1,0:T(8,128)(2,1)S(1)}, bf16[128,1024]{1,0:T(8,128)(2,1)S(1)}, u32[]{:S(2)}, u32[]{:S(2)}) collective-permute-start(bf16[128,1024]{1,0:T(8,128)(2,1)S(1)} %collective-permute-done.3.k_c.refs_1_), channel_id=1, source_target_pairs={{0,2},{1,3},{2,0},{3,1},{4,6},{5,7},{6,4},{7,5},{8,10},{9,11},{10,... | collective-permute-start | bytes 786440 | tf_op jit(solution)/shard_map/ppermute | solution.py:117
  31.9 1.5 %collective-permute-start.12 = (bf16[128,512]{1,0:T(8,128)(2,1)S(1)}, bf16[128,512]{1,0:T(8,128)(2,1)S(1)}, u32[]{:S(2)}, u32[]{:S(2)}) collective-permute-start(bf16[128,512]{1,0:T(8,128)(2,1)S(1)} %collective-permute-done.11.far), channel_id=1, source_target_pairs={{0,2},{1,3},{2,0},{3,1},{4,6},{5,7},{6,4},{7,5},{8,10},{9,11},{10,... | collective-permute-start | bytes 393224 | tf_op jit(solution)/shard_map/ppermute | solution.py:117
  33.5 1.1 %shard_map.39.early = f32[384,512]{1,0:T(8,128)S(1)} custom-call(s32[1]{0:T(128)} %bitcast.me_ref, bf16[384,512]{1,0:T(8,128)(2,1)S(1)} %constant_dynamic-update-slice_fusion.near, bf16[384,512]{1,0:T(8,128)(2,1)S(1)} %collective-permute-done.5.near_y, bf16[128,512]{1,0:T(8,128)(2,1)S(1)} %collective-permute-done.6.oc_ref, ...), custom_call_target="tpu_custom_call" | custom-call | flops 603979776 | bytes 3276800 | tf_op jit(solution)/shard_map/pallas_call | solution.py:22
  34.6 3.9 %collective-permute-done.12.far_y = bf16[128,512]{1,0:T(8,128)(2,1)S(1)} collective-permute-done((bf16[128,512]{1,0:T(8,128)(2,1)S(1)}, bf16[128,512]{1,0:T(8,128)(2,1)S(1)}, u32[]{:S(2)}, u32[]{:S(2)}) %collective-permute-start.12) | collective-permute-done | bytes 131104 | tf_op jit(solution)/shard_map/ppermute | solution.py:117
  38.5 1.3 %shard_map.40 = (f32[512,256]{1,0:T(8,128)S(1)}, f32[512,256]{1,0:T(8,128)S(1)}) custom-call(s32[1]{0:T(128)} %bitcast.me_ref, f32[384,512]{1,0:T(8,128)S(1)} %shard_map.39.early, bf16[384,512]{1,0:T(8,128)(2,1)S(1)} %constant_dynamic-update-slice_fusion.near, bf16[128,512]{1,0:T(8,128)(2,1)S(1)} %collective-permute-done.11.far, ...), custom_call_target="tpu_custom_call" | custom-call | flops 536870912 | bytes 5242880 | tf_op jit(solution)/shard_map/pallas_call | solution.py:22
  39.9 1.9 %collective-permute-done.16.came_ref = f32[512,256]{1,0:T(8,128)S(1)} collective-permute-done((f32[512,256]{1,0:T(8,128)S(1)}, f32[512,256]{1,0:T(8,128)S(1)}, u32[]{:S(2)}, u32[]{:S(2)}) %collective-permute-start.16) | collective-permute-done | bytes 524320 | tf_op jit(solution)/shard_map/ppermute | solution.py:117
  41.8 0.5 shard_map.41
  42.3 2.4 %collective-permute-start.17 = (bf16[64,1024]{1,0:T(8,128)(2,1)S(1)}, bf16[64,1024]{1,0:T(8,128)(2,1)S(1)}, u32[]{:S(2)}, u32[]{:S(2)}) collective-permute-start(bf16[64,1024]{1,0:T(8,128)(2,1)S(1)} %get-tuple-element.38), channel_id=1, source_target_pairs={{0,12},{1,13},{2,14},{3,15},{4,8},{5,9},{6,10},{7,11},{8,4},{9,5},... | collective-permute-start | bytes 393224 | tf_op jit(solution)/shard_map/ppermute | solution.py:117
  44.8 2.0 %collective-permute-start.19 = (bf16[64,1024]{1,0:T(8,128)(2,1)S(1)}, bf16[64,1024]{1,0:T(8,128)(2,1)S(1)}, u32[]{:S(2)}, u32[]{:S(2)}) collective-permute-start(bf16[64,1024]{1,0:T(8,128)(2,1)S(1)} %get-tuple-element.40), channel_id=1, source_target_pairs={{0,4},{1,5},{2,6},{3,7},{4,0},{5,1},{6,2},{7,3},{8,12},{9,13},{10,... | collective-permute-start | bytes 393224 | tf_op jit(solution)/shard_map/ppermute | solution.py:117
  46.8 3.9 %collective-permute-done.17 = bf16[64,1024]{1,0:T(8,128)(2,1)S(1)} collective-permute-done((bf16[64,1024]{1,0:T(8,128)(2,1)S(1)}, bf16[64,1024]{1,0:T(8,128)(2,1)S(1)}, u32[]{:S(2)}, u32[]{:S(2)}) %collective-permute-start.17) | collective-permute-done | bytes 131104 | tf_op jit(solution)/shard_map/ppermute | solution.py:117
  50.7 5.1 %collective-permute-done.18 = bf16[64,1024]{1,0:T(8,128)(2,1)S(1)} collective-permute-done((bf16[64,1024]{1,0:T(8,128)(2,1)S(1)}, bf16[64,1024]{1,0:T(8,128)(2,1)S(1)}, u32[]{:S(2)}, u32[]{:S(2)}) %collective-permute-start.18) | collective-permute-done | bytes 131104 | tf_op jit(solution)/shard_map/ppermute | solution.py:117
  55.7 0.8 %add_bitcast_fusion = f32[1024,64]{0,1:T(8,128)} fusion(bf16[64,1024]{1,0:T(8,128)(2,1)S(1)} %collective-permute-done.19, bf16[64,1024]{1,0:T(8,128)(2,1)S(1)} %collective-permute-done.18, f32[64,1024]{1,0:T(8,128)S(1)} %get-tuple-element.37, bf16[64,1024]{1,0:T(8,128)(2,1)S(1)} %collective-permute-done.17), kind=kLoop, calls=%fused_computation | loop fusion | flops 393216 | bytes 917504 | tf_op jit(solution)/shard_map/transpose | solution.py:189
  (32 shorter events, 2.8 us)
Async XLA Ops:
  0.0 10.7 %collective-permute-start = (bf16[128,512]{1,0:T(8,128)(2,1)}, bf16[128,512]{1,0:T(8,128)(2,1)S(1)}, u32[]{:S(2)}, u32[]{:S(2)}) collective-permute-start(bf16[128,512]{1,0:T(8,128)(2,1)} %param.3), channel_id=1, source_target_pairs={{0,8},{1,9},{2,10},{3,11},{4,12},{5,13},{6,14},{7,15},{8,0},{9,1},... | collective-permute-start | bytes 393224 | tf_op jit(solution)/shard_map/ppermute | solution.py:117
  4.0 6.8 %collective-permute-start.1 = (bf16[128,512]{1,0:T(8,128)(2,1)}, bf16[128,512]{1,0:T(8,128)(2,1)S(1)}, u32[]{:S(2)}, u32[]{:S(2)}) collective-permute-start(bf16[128,512]{1,0:T(8,128)(2,1)} %param.3), channel_id=1, source_target_pairs={{0,4},{1,5},{2,6},{3,7},{4,0},{5,1},{6,2},{7,3},{8,12},{9,13},{10,... | collective-permute-start | bytes 393224 | tf_op jit(solution)/shard_map/ppermute | solution.py:117
  5.6 11.8 %collective-permute-start.7 = (bf16[128,1024]{1,0:T(8,128)(2,1)}, bf16[128,1024]{1,0:T(8,128)(2,1)S(1)}, u32[]{:S(2)}, u32[]{:S(2)}) collective-permute-start(bf16[128,1024]{1,0:T(8,128)(2,1)} %b0.1), channel_id=1, source_target_pairs={{0,1},{1,0},{2,3},{3,2},{4,5},{5,4},{6,7},{7,6},{8,9},{9,8},{10,11... | collective-permute-start | bytes 786440 | tf_op jit(solution)/shard_map/ppermute | solution.py:117
  5.6 9.3 %collective-permute-start.2 = (bf16[128,1024]{1,0:T(8,128)(2,1)}, bf16[128,1024]{1,0:T(8,128)(2,1)S(1)}, u32[]{:S(2)}, u32[]{:S(2)}) collective-permute-start(bf16[128,1024]{1,0:T(8,128)(2,1)} %b0.1), channel_id=1, source_target_pairs={{0,2},{1,3},{2,0},{3,1},{4,6},{5,7},{6,4},{7,5},{8,10},{9,11},{10,... | collective-permute-start | bytes 786440 | tf_op jit(solution)/shard_map/ppermute | solution.py:117
  7.1 1.0 %copy-start = (bf16[128,2048]{1,0:T(8,128)(2,1)S(1)}, bf16[128,2048]{1,0:T(8,128)(2,1)}, u32[]{:S(2)}) copy-start(bf16[128,2048]{1,0:T(8,128)(2,1)} %k_ref.1) | copy-start | bytes 1572868
  8.2 0.9 %copy-start.2 = (bf16[128,512]{1,0:T(8,128)(2,1)S(1)}, bf16[128,512]{1,0:T(8,128)(2,1)}, u32[]{:S(2)}) copy-start(bf16[128,512]{1,0:T(8,128)(2,1)} %param.3) | copy-start | bytes 393220
  8.3 6.6 %collective-permute-start.3 = (bf16[128,1024]{1,0:T(8,128)(2,1)S(1)}, bf16[128,1024]{1,0:T(8,128)(2,1)S(1)}, u32[]{:S(2)}, u32[]{:S(2)}) collective-permute-start(bf16[128,1024]{1,0:T(8,128)(2,1)S(1)} %get-tuple-element.23), channel_id=1, source_target_pairs={{0,1},{1,0},{2,3},{3,2},{4,5},{5,4},{6,7},{7,6},{8,9},{9,8},{10,11... | collective-permute-start | bytes 786440 | tf_op jit(solution)/shard_map/ppermute | solution.py:117
  9.1 5.8 %copy-start.1 = (bf16[128,1024]{1,0:T(8,128)(2,1)S(1)}, bf16[128,1024]{1,0:T(8,128)(2,1)}, u32[]{:S(2)}) copy-start(bf16[128,1024]{1,0:T(8,128)(2,1)} %b0.1) | copy-start | bytes 786436
  10.9 12.5 %collective-permute-start.5 = (bf16[384,512]{1,0:T(8,128)(2,1)S(1)}, bf16[384,512]{1,0:T(8,128)(2,1)S(1)}, u32[]{:S(2)}, u32[]{:S(2)}) collective-permute-start(bf16[384,512]{1,0:T(8,128)(2,1)S(1)} %constant_dynamic-update-slice_fusion.near), channel_id=1, source_target_pairs={{0,2},{1,3},{2,0},{3,1},{4,6},{5,7},{6,4},{7,5},{8,10},{9,11},{10,... | collective-permute-start | bytes 1179656 | tf_op jit(solution)/shard_map/ppermute | solution.py:117
  12.5 4.3 %collective-permute-start.6 = (bf16[128,512]{1,0:T(8,128)(2,1)S(1)}, bf16[128,512]{1,0:T(8,128)(2,1)S(1)}, u32[]{:S(2)}, u32[]{:S(2)}) collective-permute-start(bf16[128,512]{1,0:T(8,128)(2,1)S(1)} %copy-done.2), channel_id=1, source_target_pairs={{0,1},{1,0},{2,3},{3,2},{4,5},{5,4},{6,7},{7,6},{8,9},{9,8},{10,11... | collective-permute-start | bytes 393224 | tf_op jit(solution)/shard_map/ppermute | solution.py:117
  15.4 14.5 %collective-permute-start.10 = (bf16[256,512]{1,0:T(8,128)(2,1)S(1)}, bf16[256,512]{1,0:T(8,128)(2,1)S(1)}, u32[]{:S(2)}, u32[]{:S(2)}) collective-permute-start(bf16[256,512]{1,0:T(8,128)(2,1)S(1)} %shard_map.38.refs_0_.refs_4_), channel_id=1, source_target_pairs={{0,4},{1,5},{2,6},{3,7},{4,0},{5,1},{6,2},{7,3},{8,12},{9,13},{10,... | collective-permute-start | bytes 786440 | tf_op jit(solution)/shard_map/ppermute | solution.py:117
  15.9 15.5 %collective-permute-start.9 = (bf16[256,512]{1,0:T(8,128)(2,1)S(1)}, bf16[256,512]{1,0:T(8,128)(2,1)S(1)}, u32[]{:S(2)}, u32[]{:S(2)}) collective-permute-start(bf16[256,512]{1,0:T(8,128)(2,1)S(1)} %shard_map.38.refs_0_.refs_4_), channel_id=1, source_target_pairs={{0,8},{1,9},{2,10},{3,11},{4,12},{5,13},{6,14},{7,15},{8,0},{9,1},... | collective-permute-start | bytes 786440 | tf_op jit(solution)/shard_map/ppermute | solution.py:117
  16.8 14.6 %collective-permute-start.4 = (bf16[128,1024]{1,0:T(8,128)(2,1)S(1)}, bf16[128,1024]{1,0:T(8,128)(2,1)S(1)}, u32[]{:S(2)}, u32[]{:S(2)}) collective-permute-start(bf16[128,1024]{1,0:T(8,128)(2,1)S(1)} %get-tuple-element.25.k_keep.refs_0_), channel_id=1, source_target_pairs={{0,2},{1,3},{2,0},{3,1},{4,6},{5,7},{6,4},{7,5},{8,10},{9,11},{10,... | collective-permute-start | bytes 786440 | tf_op jit(solution)/shard_map/ppermute | solution.py:117
  17.4 14.0 %collective-permute-start.8 = (bf16[128,1024]{1,0:T(8,128)(2,1)S(1)}, bf16[128,1024]{1,0:T(8,128)(2,1)S(1)}, u32[]{:S(2)}, u32[]{:S(2)}) collective-permute-start(bf16[128,1024]{1,0:T(8,128)(2,1)S(1)} %collective-permute-done.2.y_ref.b2), channel_id=1, source_target_pairs={{0,1},{1,0},{2,3},{3,2},{4,5},{5,4},{6,7},{7,6},{8,9},{9,8},{10,11... | collective-permute-start | bytes 786440 | tf_op jit(solution)/shard_map/ppermute | solution.py:117
  23.4 8.5 %collective-permute-start.11 = (bf16[128,512]{1,0:T(8,128)(2,1)S(1)}, bf16[128,512]{1,0:T(8,128)(2,1)S(1)}, u32[]{:S(2)}, u32[]{:S(2)}) collective-permute-start(bf16[128,512]{1,0:T(8,128)(2,1)S(1)} %collective-permute-done), channel_id=1, source_target_pairs={{0,4},{1,5},{2,6},{3,7},{4,0},{5,1},{6,2},{7,3},{8,12},{9,13},{10,... | collective-permute-start | bytes 393224 | tf_op jit(solution)/shard_map/ppermute | solution.py:117
  29.9 8.7 %collective-permute-start.14 = (bf16[128,1024]{1,0:T(8,128)(2,1)S(1)}, bf16[128,1024]{1,0:T(8,128)(2,1)S(1)}, u32[]{:S(2)}, u32[]{:S(2)}) collective-permute-start(bf16[128,1024]{1,0:T(8,128)(2,1)S(1)} %collective-permute-done.3.k_c.refs_1_), channel_id=1, source_target_pairs={{0,2},{1,3},{2,0},{3,1},{4,6},{5,7},{6,4},{7,5},{8,10},{9,11},{10,... | collective-permute-start | bytes 786440 | tf_op jit(solution)/shard_map/ppermute | solution.py:117
  31.4 7.1 %collective-permute-start.15 = (bf16[256,512]{1,0:T(8,128)(2,1)S(1)}, bf16[256,512]{1,0:T(8,128)(2,1)S(1)}, u32[]{:S(2)}, u32[]{:S(2)}) collective-permute-start(bf16[256,512]{1,0:T(8,128)(2,1)S(1)} %collective-permute-done.9.refs_1_.refs_5_), channel_id=1, source_target_pairs={{0,4},{1,5},{2,6},{3,7},{4,0},{5,1},{6,2},{7,3},{8,12},{9,13},{10,... | collective-permute-start | bytes 786440 | tf_op jit(solution)/shard_map/ppermute | solution.py:117
  31.9 6.6 %collective-permute-start.12 = (bf16[128,512]{1,0:T(8,128)(2,1)S(1)}, bf16[128,512]{1,0:T(8,128)(2,1)S(1)}, u32[]{:S(2)}, u32[]{:S(2)}) collective-permute-start(bf16[128,512]{1,0:T(8,128)(2,1)S(1)} %collective-permute-done.11.far), channel_id=1, source_target_pairs={{0,2},{1,3},{2,0},{3,1},{4,6},{5,7},{6,4},{7,5},{8,10},{9,11},{10,... | collective-permute-start | bytes 393224 | tf_op jit(solution)/shard_map/ppermute | solution.py:117
  33.4 5.1 %collective-permute-start.13 = (bf16[128,512]{1,0:T(8,128)(2,1)S(1)}, bf16[128,512]{1,0:T(8,128)(2,1)S(1)}, u32[]{:S(2)}, u32[]{:S(2)}) collective-permute-start(bf16[128,512]{1,0:T(8,128)(2,1)S(1)} %slice.3), channel_id=1, source_target_pairs={{0,1},{1,0},{2,3},{3,2},{4,5},{5,4},{6,7},{7,6},{8,9},{9,8},{10,11... | collective-permute-start | bytes 393224 | tf_op jit(solution)/shard_map/ppermute | solution.py:117
  39.8 2.0 %collective-permute-start.16 = (f32[512,256]{1,0:T(8,128)S(1)}, f32[512,256]{1,0:T(8,128)S(1)}, u32[]{:S(2)}, u32[]{:S(2)}) collective-permute-start(f32[512,256]{1,0:T(8,128)S(1)} %get-tuple-element.34), channel_id=1, source_target_pairs={{0,1},{1,0},{2,3},{3,2},{4,5},{5,4},{6,7},{7,6},{8,9},{9,8},{10,11... | collective-permute-start | bytes 1572872 | tf_op jit(solution)/shard_map/ppermute | solution.py:117
  42.3 8.3 %collective-permute-start.17 = (bf16[64,1024]{1,0:T(8,128)(2,1)S(1)}, bf16[64,1024]{1,0:T(8,128)(2,1)S(1)}, u32[]{:S(2)}, u32[]{:S(2)}) collective-permute-start(bf16[64,1024]{1,0:T(8,128)(2,1)S(1)} %get-tuple-element.38), channel_id=1, source_target_pairs={{0,12},{1,13},{2,14},{3,15},{4,8},{5,9},{6,10},{7,11},{8,4},{9,5},... | collective-permute-start | bytes 393224 | tf_op jit(solution)/shard_map/ppermute | solution.py:117
  44.8 11.0 %collective-permute-start.18 = (bf16[64,1024]{1,0:T(8,128)(2,1)S(1)}, bf16[64,1024]{1,0:T(8,128)(2,1)S(1)}, u32[]{:S(2)}, u32[]{:S(2)}) collective-permute-start(bf16[64,1024]{1,0:T(8,128)(2,1)S(1)} %get-tuple-element.39), channel_id=1, source_target_pairs={{0,8},{1,9},{2,10},{3,11},{4,12},{5,13},{6,14},{7,15},{8,0},{9,1},... | collective-permute-start | bytes 393224 | tf_op jit(solution)/shard_map/ppermute | solution.py:117
  44.8 11.0 %collective-permute-start.19 = (bf16[64,1024]{1,0:T(8,128)(2,1)S(1)}, bf16[64,1024]{1,0:T(8,128)(2,1)S(1)}, u32[]{:S(2)}, u32[]{:S(2)}) collective-permute-start(bf16[64,1024]{1,0:T(8,128)(2,1)S(1)} %get-tuple-element.40), channel_id=1, source_target_pairs={{0,4},{1,5},{2,6},{3,7},{4,0},{5,1},{6,2},{7,3},{8,12},{9,13},{10,... | collective-permute-start | bytes 393224 | tf_op jit(solution)/shard_map/ppermute | solution.py:117

commit v5 on v4

--- a/solution.py
+++ b/solution.py
@@ -184,7 +184,7 @@
         scratch=(pltpu.VMEM((share, columns), F32),),
     )
     total = parts[0]
-    for m in range(nz - 1, 0, -1):
+    for m in range(1, nz):
         total = total + swap(parts[m], QUAD * m).astype(F32)
     return total.T
 

time: 56.7 us -> 56.3 us (level)
  no operation moved by 1% of the time
where the time goes in v5:
time: 56.3 us; the launch traced here: 56.1 us
  waiting for transfers between devices  30.3 us (54%)
  starting transfers between devices  19.9 us (35%)
  Pallas kernels  3.5 us (6%)
  local copies, waits for them, and re-layouts  1.55 us (3%)
  other arithmetic  0.76 us (1%)
    ppermute x20, waiting for transfers between devices, swap(): return lax.ppermute(a, 'row', [(i, i ^ bit) for i in range(n)])  30.3 us
    ppermute x20, starting transfers between devices, swap(): return lax.ppermute(a, 'row', [(i, i ^ bit) for i in range(n)])  19.9 us
    pallas_call x5, Pallas kernels, call(): pl.pallas_call(body, out_shape=list(outs), in_specs=[pl.BlockSpec(memory_...  3.5 us
    unnamed x8, local copies, waits for them, and re-layouts  1.53 us
  transfers between devices with their start and end apart: 20, of which 10 were waited for; matrix products, arithmetic and copies ran while one was open for 0% of the time, Pallas kernels for 3%

profile of v5, /device:TPU:0, one launch (start us, length us, event | category | flops | bytes accessed | tf_op | source)
XLA Modules:
  0.0 56.1 jit_solution(7995446889814392237)
XLA Ops:
  0.0 4.0 %collective-permute-start = (bf16[128,512]{1,0:T(8,128)(2,1)}, bf16[128,512]{1,0:T(8,128)(2,1)S(1)}, u32[]{:S(2)}, u32[]{:S(2)}) collective-permute-start(bf16[128,512]{1,0:T(8,128)(2,1)} %param.3), channel_id=1, source_target_pairs={{0,8},{1,9},{2,10},{3,11},{4,12},{5,13},{6,14},{7,15},{8,0},{9,1},... | collective-permute-start | bytes 393224 | tf_op jit(solution)/shard_map/ppermute | solution.py:117
  4.0 1.6 %collective-permute-start.1 = (bf16[128,512]{1,0:T(8,128)(2,1)}, bf16[128,512]{1,0:T(8,128)(2,1)S(1)}, u32[]{:S(2)}, u32[]{:S(2)}) collective-permute-start(bf16[128,512]{1,0:T(8,128)(2,1)} %param.3), channel_id=1, source_target_pairs={{0,4},{1,5},{2,6},{3,7},{4,0},{5,1},{6,2},{7,3},{8,12},{9,13},{10,... | collective-permute-start | bytes 393224 | tf_op jit(solution)/shard_map/ppermute | solution.py:117
  5.6 1.5 %collective-permute-start.2 = (bf16[128,1024]{1,0:T(8,128)(2,1)}, bf16[128,1024]{1,0:T(8,128)(2,1)S(1)}, u32[]{:S(2)}, u32[]{:S(2)}) collective-permute-start(bf16[128,1024]{1,0:T(8,128)(2,1)} %b0.1), channel_id=1, source_target_pairs={{0,2},{1,3},{2,0},{3,1},{4,6},{5,7},{6,4},{7,5},{8,10},{9,11},{10,... | collective-permute-start | bytes 786440 | tf_op jit(solution)/shard_map/ppermute | solution.py:117
  7.1 1.0 %copy-done = bf16[128,2048]{1,0:T(8,128)(2,1)S(1)} copy-done((bf16[128,2048]{1,0:T(8,128)(2,1)S(1)}, bf16[128,2048]{1,0:T(8,128)(2,1)}, u32[]{:S(2)}) %copy-start) | copy-done | bytes 524312
  9.1 1.5 %collective-permute-done = bf16[128,512]{1,0:T(8,128)(2,1)S(1)} collective-permute-done((bf16[128,512]{1,0:T(8,128)(2,1)}, bf16[128,512]{1,0:T(8,128)(2,1)S(1)}, u32[]{:S(2)}, u32[]{:S(2)}) %collective-permute-start) | collective-permute-done | bytes 131104 | tf_op jit(solution)/shard_map/ppermute | solution.py:117
  10.9 1.6 %collective-permute-start.5 = (bf16[384,512]{1,0:T(8,128)(2,1)S(1)}, bf16[384,512]{1,0:T(8,128)(2,1)S(1)}, u32[]{:S(2)}, u32[]{:S(2)}) collective-permute-start(bf16[384,512]{1,0:T(8,128)(2,1)S(1)} %constant_dynamic-update-slice_fusion.near), channel_id=1, source_target_pairs={{0,2},{1,3},{2,0},{3,1},{4,6},{5,7},{6,4},{7,5},{8,10},{9,11},{10,... | collective-permute-start | bytes 1179656 | tf_op jit(solution)/shard_map/ppermute | solution.py:117
  12.5 2.4 %collective-permute-done.2.y_ref.b2 = bf16[128,1024]{1,0:T(8,128)(2,1)S(1)} collective-permute-done((bf16[128,1024]{1,0:T(8,128)(2,1)}, bf16[128,1024]{1,0:T(8,128)(2,1)S(1)}, u32[]{:S(2)}, u32[]{:S(2)}) %collective-permute-start.2) | collective-permute-done | bytes 262176 | tf_op jit(solution)/shard_map/ppermute | solution.py:117
  15.9 0.9 %collective-permute-start.9 = (bf16[256,512]{1,0:T(8,128)(2,1)S(1)}, bf16[256,512]{1,0:T(8,128)(2,1)S(1)}, u32[]{:S(2)}, u32[]{:S(2)}) collective-permute-start(bf16[256,512]{1,0:T(8,128)(2,1)S(1)} %shard_map.38.refs_0_.refs_4_), channel_id=1, source_target_pairs={{0,8},{1,9},{2,10},{3,11},{4,12},{5,13},{6,14},{7,15},{8,0},{9,1},... | collective-permute-start | bytes 786440 | tf_op jit(solution)/shard_map/ppermute | solution.py:117
  16.8 0.6 %collective-permute-start.4 = (bf16[128,1024]{1,0:T(8,128)(2,1)S(1)}, bf16[128,1024]{1,0:T(8,128)(2,1)S(1)}, u32[]{:S(2)}, u32[]{:S(2)}) collective-permute-start(bf16[128,1024]{1,0:T(8,128)(2,1)S(1)} %get-tuple-element.25.k_keep.refs_0_), channel_id=1, source_target_pairs={{0,2},{1,3},{2,0},{3,1},{4,6},{5,7},{6,4},{7,5},{8,10},{9,11},{10,... | collective-permute-start | bytes 786440 | tf_op jit(solution)/shard_map/ppermute | solution.py:117
  17.4 5.9 %collective-permute-done.5.near_y = bf16[384,512]{1,0:T(8,128)(2,1)S(1)} collective-permute-done((bf16[384,512]{1,0:T(8,128)(2,1)S(1)}, bf16[384,512]{1,0:T(8,128)(2,1)S(1)}, u32[]{:S(2)}, u32[]{:S(2)}) %collective-permute-start.5) | collective-permute-done | bytes 393248 | tf_op jit(solution)/shard_map/ppermute | solution.py:117
  23.4 1.1 %collective-permute-start.11 = (bf16[128,512]{1,0:T(8,128)(2,1)S(1)}, bf16[128,512]{1,0:T(8,128)(2,1)S(1)}, u32[]{:S(2)}, u32[]{:S(2)}) collective-permute-start(bf16[128,512]{1,0:T(8,128)(2,1)S(1)} %collective-permute-done), channel_id=1, source_target_pairs={{0,4},{1,5},{2,6},{3,7},{4,0},{5,1},{6,2},{7,3},{8,12},{9,13},{10,... | collective-permute-start | bytes 393224 | tf_op jit(solution)/shard_map/ppermute | solution.py:117
  24.4 5.4 %collective-permute-done.10.refs_2_.refs_6_ = bf16[256,512]{1,0:T(8,128)(2,1)S(1)} collective-permute-done((bf16[256,512]{1,0:T(8,128)(2,1)S(1)}, bf16[256,512]{1,0:T(8,128)(2,1)S(1)}, u32[]{:S(2)}, u32[]{:S(2)}) %collective-permute-start.10) | collective-permute-done | bytes 262176 | tf_op jit(solution)/shard_map/ppermute | solution.py:117
  29.9 1.5 %collective-permute-start.14 = (bf16[128,1024]{1,0:T(8,128)(2,1)S(1)}, bf16[128,1024]{1,0:T(8,128)(2,1)S(1)}, u32[]{:S(2)}, u32[]{:S(2)}) collective-permute-start(bf16[128,1024]{1,0:T(8,128)(2,1)S(1)} %collective-permute-done.3.k_c.refs_1_), channel_id=1, source_target_pairs={{0,2},{1,3},{2,0},{3,1},{4,6},{5,7},{6,4},{7,5},{8,10},{9,11},{10,... | collective-permute-start | bytes 786440 | tf_op jit(solution)/shard_map/ppermute | solution.py:117
  31.9 1.5 %collective-permute-start.12 = (bf16[128,512]{1,0:T(8,128)(2,1)S(1)}, bf16[128,512]{1,0:T(8,128)(2,1)S(1)}, u32[]{:S(2)}, u32[]{:S(2)}) collective-permute-start(bf16[128,512]{1,0:T(8,128)(2,1)S(1)} %collective-permute-done.11.far), channel_id=1, source_target_pairs={{0,2},{1,3},{2,0},{3,1},{4,6},{5,7},{6,4},{7,5},{8,10},{9,11},{10,... | collective-permute-start | bytes 393224 | tf_op jit(solution)/shard_map/ppermute | solution.py:117
  33.5 1.1 %shard_map.39.early = f32[384,512]{1,0:T(8,128)S(1)} custom-call(s32[1]{0:T(128)} %bitcast.me_ref, bf16[384,512]{1,0:T(8,128)(2,1)S(1)} %constant_dynamic-update-slice_fusion.near, bf16[384,512]{1,0:T(8,128)(2,1)S(1)} %collective-permute-done.5.near_y, bf16[128,512]{1,0:T(8,128)(2,1)S(1)} %collective-permute-done.6.oc_ref, ...), custom_call_target="tpu_custom_call" | custom-call | flops 603979776 | bytes 3276800 | tf_op jit(solution)/shard_map/pallas_call | solution.py:22
  34.6 3.9 %collective-permute-done.12.far_y = bf16[128,512]{1,0:T(8,128)(2,1)S(1)} collective-permute-done((bf16[128,512]{1,0:T(8,128)(2,1)S(1)}, bf16[128,512]{1,0:T(8,128)(2,1)S(1)}, u32[]{:S(2)}, u32[]{:S(2)}) %collective-permute-start.12) | collective-permute-done | bytes 131104 | tf_op jit(solution)/shard_map/ppermute | solution.py:117
  38.5 1.3 %shard_map.40 = (f32[512,256]{1,0:T(8,128)S(1)}, f32[512,256]{1,0:T(8,128)S(1)}) custom-call(s32[1]{0:T(128)} %bitcast.me_ref, f32[384,512]{1,0:T(8,128)S(1)} %shard_map.39.early, bf16[384,512]{1,0:T(8,128)(2,1)S(1)} %constant_dynamic-update-slice_fusion.near, bf16[128,512]{1,0:T(8,128)(2,1)S(1)} %collective-permute-done.11.far, ...), custom_call_target="tpu_custom_call" | custom-call | flops 536870912 | bytes 5242880 | tf_op jit(solution)/shard_map/pallas_call | solution.py:22
  39.9 1.9 %collective-permute-done.16.came_ref = f32[512,256]{1,0:T(8,128)S(1)} collective-permute-done((f32[512,256]{1,0:T(8,128)S(1)}, f32[512,256]{1,0:T(8,128)S(1)}, u32[]{:S(2)}, u32[]{:S(2)}) %collective-permute-start.16) | collective-permute-done | bytes 524320 | tf_op jit(solution)/shard_map/ppermute | solution.py:117
  41.8 0.5 shard_map.41
  42.4 2.9 %collective-permute-start.18 = (bf16[64,1024]{1,0:T(8,128)(2,1)S(1)}, bf16[64,1024]{1,0:T(8,128)(2,1)S(1)}, u32[]{:S(2)}, u32[]{:S(2)}) collective-permute-start(bf16[64,1024]{1,0:T(8,128)(2,1)S(1)} %get-tuple-element.39), channel_id=1, source_target_pairs={{0,8},{1,9},{2,10},{3,11},{4,12},{5,13},{6,14},{7,15},{8,0},{9,1},... | collective-permute-start | bytes 393224 | tf_op jit(solution)/shard_map/ppermute | solution.py:117
  45.3 1.4 %collective-permute-start.19 = (bf16[64,1024]{1,0:T(8,128)(2,1)S(1)}, bf16[64,1024]{1,0:T(8,128)(2,1)S(1)}, u32[]{:S(2)}, u32[]{:S(2)}) collective-permute-start(bf16[64,1024]{1,0:T(8,128)(2,1)S(1)} %get-tuple-element.40), channel_id=1, source_target_pairs={{0,12},{1,13},{2,14},{3,15},{4,8},{5,9},{6,10},{7,11},{8,4},{9,5},... | collective-permute-start | bytes 393224 | tf_op jit(solution)/shard_map/ppermute | solution.py:117
  46.8 3.4 %collective-permute-done.17 = bf16[64,1024]{1,0:T(8,128)(2,1)S(1)} collective-permute-done((bf16[64,1024]{1,0:T(8,128)(2,1)S(1)}, bf16[64,1024]{1,0:T(8,128)(2,1)S(1)}, u32[]{:S(2)}, u32[]{:S(2)}) %collective-permute-start.17) | collective-permute-done | bytes 131104 | tf_op jit(solution)/shard_map/ppermute | solution.py:117
  50.2 5.2 %collective-permute-done.18 = bf16[64,1024]{1,0:T(8,128)(2,1)S(1)} collective-permute-done((bf16[64,1024]{1,0:T(8,128)(2,1)S(1)}, bf16[64,1024]{1,0:T(8,128)(2,1)S(1)}, u32[]{:S(2)}, u32[]{:S(2)}) %collective-permute-start.18) | collective-permute-done | bytes 131104 | tf_op jit(solution)/shard_map/ppermute | solution.py:117
  55.4 0.8 %add_bitcast_fusion = f32[1024,64]{0,1:T(8,128)} fusion(bf16[64,1024]{1,0:T(8,128)(2,1)S(1)} %collective-permute-done.19, bf16[64,1024]{1,0:T(8,128)(2,1)S(1)} %collective-permute-done.18, f32[64,1024]{1,0:T(8,128)S(1)} %get-tuple-element.37, bf16[64,1024]{1,0:T(8,128)(2,1)S(1)} %collective-permute-done.17), kind=kLoop, calls=%fused_computation | loop fusion | flops 393216 | bytes 917504 | tf_op jit(solution)/shard_map/transpose | solution.py:189
  (32 shorter events, 2.8 us)
Async XLA Ops:
  0.0 10.7 %collective-permute-start = (bf16[128,512]{1,0:T(8,128)(2,1)}, bf16[128,512]{1,0:T(8,128)(2,1)S(1)}, u32[]{:S(2)}, u32[]{:S(2)}) collective-permute-start(bf16[128,512]{1,0:T(8,128)(2,1)} %param.3), channel_id=1, source_target_pairs={{0,8},{1,9},{2,10},{3,11},{4,12},{5,13},{6,14},{7,15},{8,0},{9,1},... | collective-permute-start | bytes 393224 | tf_op jit(solution)/shard_map/ppermute | solution.py:117
  4.0 6.8 %collective-permute-start.1 = (bf16[128,512]{1,0:T(8,128)(2,1)}, bf16[128,512]{1,0:T(8,128)(2,1)S(1)}, u32[]{:S(2)}, u32[]{:S(2)}) collective-permute-start(bf16[128,512]{1,0:T(8,128)(2,1)} %param.3), channel_id=1, source_target_pairs={{0,4},{1,5},{2,6},{3,7},{4,0},{5,1},{6,2},{7,3},{8,12},{9,13},{10,... | collective-permute-start | bytes 393224 | tf_op jit(solution)/shard_map/ppermute | solution.py:117
  5.6 11.8 %collective-permute-start.7 = (bf16[128,1024]{1,0:T(8,128)(2,1)}, bf16[128,1024]{1,0:T(8,128)(2,1)S(1)}, u32[]{:S(2)}, u32[]{:S(2)}) collective-permute-start(bf16[128,1024]{1,0:T(8,128)(2,1)} %b0.1), channel_id=1, source_target_pairs={{0,1},{1,0},{2,3},{3,2},{4,5},{5,4},{6,7},{7,6},{8,9},{9,8},{10,11... | collective-permute-start | bytes 786440 | tf_op jit(solution)/shard_map/ppermute | solution.py:117
  5.6 9.3 %collective-permute-start.2 = (bf16[128,1024]{1,0:T(8,128)(2,1)}, bf16[128,1024]{1,0:T(8,128)(2,1)S(1)}, u32[]{:S(2)}, u32[]{:S(2)}) collective-permute-start(bf16[128,1024]{1,0:T(8,128)(2,1)} %b0.1), channel_id=1, source_target_pairs={{0,2},{1,3},{2,0},{3,1},{4,6},{5,7},{6,4},{7,5},{8,10},{9,11},{10,... | collective-permute-start | bytes 786440 | tf_op jit(solution)/shard_map/ppermute | solution.py:117
  7.1 1.0 %copy-start = (bf16[128,2048]{1,0:T(8,128)(2,1)S(1)}, bf16[128,2048]{1,0:T(8,128)(2,1)}, u32[]{:S(2)}) copy-start(bf16[128,2048]{1,0:T(8,128)(2,1)} %k_ref.1) | copy-start | bytes 1572868
  8.2 0.9 %copy-start.2 = (bf16[128,512]{1,0:T(8,128)(2,1)S(1)}, bf16[128,512]{1,0:T(8,128)(2,1)}, u32[]{:S(2)}) copy-start(bf16[128,512]{1,0:T(8,128)(2,1)} %param.3) | copy-start | bytes 393220
  8.3 6.6 %collective-permute-start.3 = (bf16[128,1024]{1,0:T(8,128)(2,1)S(1)}, bf16[128,1024]{1,0:T(8,128)(2,1)S(1)}, u32[]{:S(2)}, u32[]{:S(2)}) collective-permute-start(bf16[128,1024]{1,0:T(8,128)(2,1)S(1)} %get-tuple-element.23), channel_id=1, source_target_pairs={{0,1},{1,0},{2,3},{3,2},{4,5},{5,4},{6,7},{7,6},{8,9},{9,8},{10,11... | collective-permute-start | bytes 786440 | tf_op jit(solution)/shard_map/ppermute | solution.py:117
  9.1 5.8 %copy-start.1 = (bf16[128,1024]{1,0:T(8,128)(2,1)S(1)}, bf16[128,1024]{1,0:T(8,128)(2,1)}, u32[]{:S(2)}) copy-start(bf16[128,1024]{1,0:T(8,128)(2,1)} %b0.1) | copy-start | bytes 786436
  10.9 12.5 %collective-permute-start.5 = (bf16[384,512]{1,0:T(8,128)(2,1)S(1)}, bf16[384,512]{1,0:T(8,128)(2,1)S(1)}, u32[]{:S(2)}, u32[]{:S(2)}) collective-permute-start(bf16[384,512]{1,0:T(8,128)(2,1)S(1)} %constant_dynamic-update-slice_fusion.near), channel_id=1, source_target_pairs={{0,2},{1,3},{2,0},{3,1},{4,6},{5,7},{6,4},{7,5},{8,10},{9,11},{10,... | collective-permute-start | bytes 1179656 | tf_op jit(solution)/shard_map/ppermute | solution.py:117
  12.5 4.3 %collective-permute-start.6 = (bf16[128,512]{1,0:T(8,128)(2,1)S(1)}, bf16[128,512]{1,0:T(8,128)(2,1)S(1)}, u32[]{:S(2)}, u32[]{:S(2)}) collective-permute-start(bf16[128,512]{1,0:T(8,128)(2,1)S(1)} %copy-done.2), channel_id=1, source_target_pairs={{0,1},{1,0},{2,3},{3,2},{4,5},{5,4},{6,7},{7,6},{8,9},{9,8},{10,11... | collective-permute-start | bytes 393224 | tf_op jit(solution)/shard_map/ppermute | solution.py:117
  15.4 14.5 %collective-permute-start.10 = (bf16[256,512]{1,0:T(8,128)(2,1)S(1)}, bf16[256,512]{1,0:T(8,128)(2,1)S(1)}, u32[]{:S(2)}, u32[]{:S(2)}) collective-permute-start(bf16[256,512]{1,0:T(8,128)(2,1)S(1)} %shard_map.38.refs_0_.refs_4_), channel_id=1, source_target_pairs={{0,4},{1,5},{2,6},{3,7},{4,0},{5,1},{6,2},{7,3},{8,12},{9,13},{10,... | collective-permute-start | bytes 786440 | tf_op jit(solution)/shard_map/ppermute | solution.py:117
  15.9 15.5 %collective-permute-start.9 = (bf16[256,512]{1,0:T(8,128)(2,1)S(1)}, bf16[256,512]{1,0:T(8,128)(2,1)S(1)}, u32[]{:S(2)}, u32[]{:S(2)}) collective-permute-start(bf16[256,512]{1,0:T(8,128)(2,1)S(1)} %shard_map.38.refs_0_.refs_4_), channel_id=1, source_target_pairs={{0,8},{1,9},{2,10},{3,11},{4,12},{5,13},{6,14},{7,15},{8,0},{9,1},... | collective-permute-start | bytes 786440 | tf_op jit(solution)/shard_map/ppermute | solution.py:117
  16.8 14.6 %collective-permute-start.4 = (bf16[128,1024]{1,0:T(8,128)(2,1)S(1)}, bf16[128,1024]{1,0:T(8,128)(2,1)S(1)}, u32[]{:S(2)}, u32[]{:S(2)}) collective-permute-start(bf16[128,1024]{1,0:T(8,128)(2,1)S(1)} %get-tuple-element.25.k_keep.refs_0_), channel_id=1, source_target_pairs={{0,2},{1,3},{2,0},{3,1},{4,6},{5,7},{6,4},{7,5},{8,10},{9,11},{10,... | collective-permute-start | bytes 786440 | tf_op jit(solution)/shard_map/ppermute | solution.py:117
  17.4 14.0 %collective-permute-start.8 = (bf16[128,1024]{1,0:T(8,128)(2,1)S(1)}, bf16[128,1024]{1,0:T(8,128)(2,1)S(1)}, u32[]{:S(2)}, u32[]{:S(2)}) collective-permute-start(bf16[128,1024]{1,0:T(8,128)(2,1)S(1)} %collective-permute-done.2.y_ref.b2), channel_id=1, source_target_pairs={{0,1},{1,0},{2,3},{3,2},{4,5},{5,4},{6,7},{7,6},{8,9},{9,8},{10,11... | collective-permute-start | bytes 786440 | tf_op jit(solution)/shard_map/ppermute | solution.py:117
  23.4 8.5 %collective-permute-start.11 = (bf16[128,512]{1,0:T(8,128)(2,1)S(1)}, bf16[128,512]{1,0:T(8,128)(2,1)S(1)}, u32[]{:S(2)}, u32[]{:S(2)}) collective-permute-start(bf16[128,512]{1,0:T(8,128)(2,1)S(1)} %collective-permute-done), channel_id=1, source_target_pairs={{0,4},{1,5},{2,6},{3,7},{4,0},{5,1},{6,2},{7,3},{8,12},{9,13},{10,... | collective-permute-start | bytes 393224 | tf_op jit(solution)/shard_map/ppermute | solution.py:117
  29.9 8.7 %collective-permute-start.14 = (bf16[128,1024]{1,0:T(8,128)(2,1)S(1)}, bf16[128,1024]{1,0:T(8,128)(2,1)S(1)}, u32[]{:S(2)}, u32[]{:S(2)}) collective-permute-start(bf16[128,1024]{1,0:T(8,128)(2,1)S(1)} %collective-permute-done.3.k_c.refs_1_), channel_id=1, source_target_pairs={{0,2},{1,3},{2,0},{3,1},{4,6},{5,7},{6,4},{7,5},{8,10},{9,11},{10,... | collective-permute-start | bytes 786440 | tf_op jit(solution)/shard_map/ppermute | solution.py:117
  31.4 7.1 %collective-permute-start.15 = (bf16[256,512]{1,0:T(8,128)(2,1)S(1)}, bf16[256,512]{1,0:T(8,128)(2,1)S(1)}, u32[]{:S(2)}, u32[]{:S(2)}) collective-permute-start(bf16[256,512]{1,0:T(8,128)(2,1)S(1)} %collective-permute-done.9.refs_1_.refs_5_), channel_id=1, source_target_pairs={{0,4},{1,5},{2,6},{3,7},{4,0},{5,1},{6,2},{7,3},{8,12},{9,13},{10,... | collective-permute-start | bytes 786440 | tf_op jit(solution)/shard_map/ppermute | solution.py:117
  31.9 6.6 %collective-permute-start.12 = (bf16[128,512]{1,0:T(8,128)(2,1)S(1)}, bf16[128,512]{1,0:T(8,128)(2,1)S(1)}, u32[]{:S(2)}, u32[]{:S(2)}) collective-permute-start(bf16[128,512]{1,0:T(8,128)(2,1)S(1)} %collective-permute-done.11.far), channel_id=1, source_target_pairs={{0,2},{1,3},{2,0},{3,1},{4,6},{5,7},{6,4},{7,5},{8,10},{9,11},{10,... | collective-permute-start | bytes 393224 | tf_op jit(solution)/shard_map/ppermute | solution.py:117
  33.4 5.1 %collective-permute-start.13 = (bf16[128,512]{1,0:T(8,128)(2,1)S(1)}, bf16[128,512]{1,0:T(8,128)(2,1)S(1)}, u32[]{:S(2)}, u32[]{:S(2)}) collective-permute-start(bf16[128,512]{1,0:T(8,128)(2,1)S(1)} %slice.3), channel_id=1, source_target_pairs={{0,1},{1,0},{2,3},{3,2},{4,5},{5,4},{6,7},{7,6},{8,9},{9,8},{10,11... | collective-permute-start | bytes 393224 | tf_op jit(solution)/shard_map/ppermute | solution.py:117
  39.8 2.0 %collective-permute-start.16 = (f32[512,256]{1,0:T(8,128)S(1)}, f32[512,256]{1,0:T(8,128)S(1)}, u32[]{:S(2)}, u32[]{:S(2)}) collective-permute-start(f32[512,256]{1,0:T(8,128)S(1)} %get-tuple-element.34), channel_id=1, source_target_pairs={{0,1},{1,0},{2,3},{3,2},{4,5},{5,4},{6,7},{7,6},{8,9},{9,8},{10,11... | collective-permute-start | bytes 1572872 | tf_op jit(solution)/shard_map/ppermute | solution.py:117
  42.3 7.9 %collective-permute-start.17 = (bf16[64,1024]{1,0:T(8,128)(2,1)S(1)}, bf16[64,1024]{1,0:T(8,128)(2,1)S(1)}, u32[]{:S(2)}, u32[]{:S(2)}) collective-permute-start(bf16[64,1024]{1,0:T(8,128)(2,1)S(1)} %get-tuple-element.38), channel_id=1, source_target_pairs={{0,4},{1,5},{2,6},{3,7},{4,0},{5,1},{6,2},{7,3},{8,12},{9,13},{10,... | collective-permute-start | bytes 393224 | tf_op jit(solution)/shard_map/ppermute | solution.py:117
  42.4 13.0 %collective-permute-start.18 = (bf16[64,1024]{1,0:T(8,128)(2,1)S(1)}, bf16[64,1024]{1,0:T(8,128)(2,1)S(1)}, u32[]{:S(2)}, u32[]{:S(2)}) collective-permute-start(bf16[64,1024]{1,0:T(8,128)(2,1)S(1)} %get-tuple-element.39), channel_id=1, source_target_pairs={{0,8},{1,9},{2,10},{3,11},{4,12},{5,13},{6,14},{7,15},{8,0},{9,1},... | collective-permute-start | bytes 393224 | tf_op jit(solution)/shard_map/ppermute | solution.py:117
  45.3 10.0 %collective-permute-start.19 = (bf16[64,1024]{1,0:T(8,128)(2,1)S(1)}, bf16[64,1024]{1,0:T(8,128)(2,1)S(1)}, u32[]{:S(2)}, u32[]{:S(2)}) collective-permute-start(bf16[64,1024]{1,0:T(8,128)(2,1)S(1)} %get-tuple-element.40), channel_id=1, source_target_pairs={{0,12},{1,13},{2,14},{3,15},{4,8},{5,9},{6,10},{7,11},{8,4},{9,5},... | collective-permute-start | bytes 393224 | tf_op jit(solution)/shard_map/ppermute | solution.py:117

commit v6 on v5

--- a/solution.py
+++ b/solution.py
@@ -51,9 +51,10 @@
             x_ref[s * rows : (s + 1) * rows, c * share : (c + 1) * share] = dot(b[...], picker, 1, 0).astype(BF16)
 
 
-def weigh(o_rows, o_cols, ks, me, m):
+def weigh(o_rows, o_cols, ks, me, m, density=None):
     rows = o_cols[0].shape[0]
-    density = dot(o_rows, jnp.concatenate(o_cols, axis=0), 1, 1)
+    if density is None:
+        density = dot(o_rows, jnp.concatenate(o_cols, axis=0), 1, 1)
     at = [pl.multiple_of((2 * (me // QUAD ^ m) + (me // 2 % 2 ^ s)) * rows, rows) for s in (0, 1)]
     k_block = jnp.concatenate(
         [jnp.concatenate([kr[:, pl.ds(a, rows)] for a in at], axis=1) for kr in ks], axis=0
@@ -61,7 +62,7 @@
     return (density * k_block.astype(F32)).astype(BF16)
 
 
-def early_kernel(planes, me_ref, near, near_y, oc_ref, k_keep, k_c, k_y, *refs):
+def early_kernel(planes, me_ref, near, near_y, oc_ref, oyc_ref, k_keep, k_c, k_y, *refs):
     rows = oc_ref.shape[0]
     o_rows = jnp.concatenate([near[0:rows, :], oc_ref[...], near_y[0:rows, :]], axis=0)
     acc = None
@@ -69,10 +70,11 @@
         o_cols = [r[i * rows : (i + 1) * rows, :] for r in (near, near_y)]
         term = dot(weigh(o_rows, o_cols, (k_keep, k_c, k_y), me_ref[0], m), refs[i][...], 1, 0)
         acc = term if acc is None else acc + term
-    refs[-1][...] = acc
-
-
-def apply_kernel(planes, me_ref, early, near, far, near_y, far_y, oc_ref, oyc_ref, *refs):
+        refs[-1][:, 2 * i * rows : 2 * (i + 1) * rows] = dot(oyc_ref[...], jnp.concatenate(o_cols, axis=0), 1, 1)
+    refs[-2][...] = acc
+
+
+def apply_kernel(planes, me_ref, early, ready, near, far, near_y, far_y, oc_ref, oyc_ref, *refs):
     nz = len(planes)
     k, x, (keep_ref, send_ref) = refs[0:4], refs[4 : 4 + nz], refs[4 + nz :]
     rows = oc_ref.shape[0]
@@ -84,7 +86,8 @@
         o_cols = [r[at : at + rows, :] for r in held]
         if late:
             top += dot(weigh(o_rows, o_cols, k[:3], me_ref[0], m), x[i][...], 1, 0)
-        term = dot(weigh(oyc_ref[...], o_cols, k[3:], me_ref[0], m), x[i][...], 1, 0)
+        known = None if late else ready[:, 2 * i * rows : 2 * (i + 1) * rows]
+        term = dot(weigh(oyc_ref[...], o_cols, k[3:], me_ref[0], m, known), x[i][...], 1, 0)
         last = term if last is None else last + term
     share = top.shape[1] // 2
     for r in range(QUAD):
@@ -161,18 +164,21 @@
     xs = [xs[order.index(m)] for m in places]
     block = jax.ShapeDtypeStruct((QUAD * rows, share), F32)
     n_near = 1 + len(o_hops)
-    (early,) = call(
+    early, ready = call(
         functools.partial(early_kernel, tuple(places[:n_near])),
-        (jax.ShapeDtypeStruct((3 * rows, 2 * share), F32),),
-        where,
-        (near, near_y, o_c, k_keep, k_c, k_y, *xs[:n_near]),
+        (
+            jax.ShapeDtypeStruct((3 * rows, 2 * share), F32),
+            jax.ShapeDtypeStruct((rows, n_near * 2 * rows), F32),
+        ),
+        where,
+        (near, near_y, o_c, o_yc, k_keep, k_c, k_y, *xs[:n_near]),
         12 * rows * n_near * rows * (orbitals.shape[1] + 2 * share),
     )
     keep, send = call(
         functools.partial(apply_kernel, tuple(places)),
         (block, block),
         where,
-        (early, near, far, near_y, far_y, o_c, o_yc, k_keep, k_c, k_y, k_yc, *xs),
+        (early, ready, near, far, near_y, far_y, o_c, o_yc, k_keep, k_c, k_y, k_yc, *xs),
         QUAD * rows * points * (orbitals.shape[1] + 2 * share) // 2,
     )
     parts = call(

time: 56.3 us -> 56.9 us (1.011)
  waiting for transfers between devices: 30.3 us -> 31.1 us
    ppermute x20, waiting for transfers between devices: 30.3 us -> 31.1 us  [swap(): return lax.ppermute(a, 'row', [(i, i ^ bit) for i in range(n)])]
where the time goes in v6:
time: 56.9 us; the launch traced here: 56.8 us
  waiting for transfers between devices  31.1 us (55%)
  starting transfers between devices  19.9 us (35%)
  Pallas kernels  3.29 us (6%)
  local copies, waits for them, and re-layouts  1.55 us (3%)
  other arithmetic  0.76 us (1%)
    ppermute x20, waiting for transfers between devices, swap(): return lax.ppermute(a, 'row', [(i, i ^ bit) for i in range(n)])  31.1 us
    ppermute x20, starting transfers between devices, swap(): return lax.ppermute(a, 'row', [(i, i ^ bit) for i in range(n)])  19.9 us
    pallas_call x5, Pallas kernels, call(): pl.pallas_call(body, out_shape=list(outs), in_specs=[pl.BlockSpec(memory_...  3.29 us
    unnamed x8, local copies, waits for them, and re-layouts  1.53 us
  transfers between devices with their start and end apart: 20, of which 10 were waited for; matrix products, arithmetic and copies ran while one was open for 0% of the time, Pallas kernels for 3%

profile of v6, /device:TPU:0, one launch (start us, length us, event | category | flops | bytes accessed | tf_op | source)
XLA Modules:
  0.0 56.8 jit_solution(4821613608161010988)
XLA Ops:
  0.0 4.0 %collective-permute-start = (bf16[128,512]{1,0:T(8,128)(2,1)}, bf16[128,512]{1,0:T(8,128)(2,1)S(1)}, u32[]{:S(2)}, u32[]{:S(2)}) collective-permute-start(bf16[128,512]{1,0:T(8,128)(2,1)} %param.3), channel_id=1, source_target_pairs={{0,8},{1,9},{2,10},{3,11},{4,12},{5,13},{6,14},{7,15},{8,0},{9,1},... | collective-permute-start | bytes 393224 | tf_op jit(solution)/shard_map/ppermute | solution.py:120
  4.0 1.6 %collective-permute-start.1 = (bf16[128,512]{1,0:T(8,128)(2,1)}, bf16[128,512]{1,0:T(8,128)(2,1)S(1)}, u32[]{:S(2)}, u32[]{:S(2)}) collective-permute-start(bf16[128,512]{1,0:T(8,128)(2,1)} %param.3), channel_id=1, source_target_pairs={{0,4},{1,5},{2,6},{3,7},{4,0},{5,1},{6,2},{7,3},{8,12},{9,13},{10,... | collective-permute-start | bytes 393224 | tf_op jit(solution)/shard_map/ppermute | solution.py:120
  5.6 1.5 %collective-permute-start.2 = (bf16[128,1024]{1,0:T(8,128)(2,1)}, bf16[128,1024]{1,0:T(8,128)(2,1)S(1)}, u32[]{:S(2)}, u32[]{:S(2)}) collective-permute-start(bf16[128,1024]{1,0:T(8,128)(2,1)} %b0.1), channel_id=1, source_target_pairs={{0,2},{1,3},{2,0},{3,1},{4,6},{5,7},{6,4},{7,5},{8,10},{9,11},{10,... | collective-permute-start | bytes 786440 | tf_op jit(solution)/shard_map/ppermute | solution.py:120
  7.1 1.0 %copy-done = bf16[128,2048]{1,0:T(8,128)(2,1)S(1)} copy-done((bf16[128,2048]{1,0:T(8,128)(2,1)S(1)}, bf16[128,2048]{1,0:T(8,128)(2,1)}, u32[]{:S(2)}) %copy-start) | copy-done | bytes 524312
  9.1 1.5 %collective-permute-done = bf16[128,512]{1,0:T(8,128)(2,1)S(1)} collective-permute-done((bf16[128,512]{1,0:T(8,128)(2,1)}, bf16[128,512]{1,0:T(8,128)(2,1)S(1)}, u32[]{:S(2)}, u32[]{:S(2)}) %collective-permute-start) | collective-permute-done | bytes 131104 | tf_op jit(solution)/shard_map/ppermute | solution.py:120
  10.9 1.6 %collective-permute-start.5 = (bf16[384,512]{1,0:T(8,128)(2,1)S(1)}, bf16[384,512]{1,0:T(8,128)(2,1)S(1)}, u32[]{:S(2)}, u32[]{:S(2)}) collective-permute-start(bf16[384,512]{1,0:T(8,128)(2,1)S(1)} %constant_dynamic-update-slice_fusion.near), channel_id=1, source_target_pairs={{0,2},{1,3},{2,0},{3,1},{4,6},{5,7},{6,4},{7,5},{8,10},{9,11},{10,... | collective-permute-start | bytes 1179656 | tf_op jit(solution)/shard_map/ppermute | solution.py:120
  12.5 2.4 %collective-permute-done.2.y_ref.b2 = bf16[128,1024]{1,0:T(8,128)(2,1)S(1)} collective-permute-done((bf16[128,1024]{1,0:T(8,128)(2,1)}, bf16[128,1024]{1,0:T(8,128)(2,1)S(1)}, u32[]{:S(2)}, u32[]{:S(2)}) %collective-permute-start.2) | collective-permute-done | bytes 262176 | tf_op jit(solution)/shard_map/ppermute | solution.py:120
  15.9 0.9 %collective-permute-start.9 = (bf16[256,512]{1,0:T(8,128)(2,1)S(1)}, bf16[256,512]{1,0:T(8,128)(2,1)S(1)}, u32[]{:S(2)}, u32[]{:S(2)}) collective-permute-start(bf16[256,512]{1,0:T(8,128)(2,1)S(1)} %shard_map.38.refs_0_.refs_4_), channel_id=1, source_target_pairs={{0,8},{1,9},{2,10},{3,11},{4,12},{5,13},{6,14},{7,15},{8,0},{9,1},... | collective-permute-start | bytes 786440 | tf_op jit(solution)/shard_map/ppermute | solution.py:120
  16.8 0.6 %collective-permute-start.4 = (bf16[128,1024]{1,0:T(8,128)(2,1)S(1)}, bf16[128,1024]{1,0:T(8,128)(2,1)S(1)}, u32[]{:S(2)}, u32[]{:S(2)}) collective-permute-start(bf16[128,1024]{1,0:T(8,128)(2,1)S(1)} %get-tuple-element.27.k_keep.refs_0_), channel_id=1, source_target_pairs={{0,2},{1,3},{2,0},{3,1},{4,6},{5,7},{6,4},{7,5},{8,10},{9,11},{10,... | collective-permute-start | bytes 786440 | tf_op jit(solution)/shard_map/ppermute | solution.py:120
  17.4 5.9 %collective-permute-done.5.near_y = bf16[384,512]{1,0:T(8,128)(2,1)S(1)} collective-permute-done((bf16[384,512]{1,0:T(8,128)(2,1)S(1)}, bf16[384,512]{1,0:T(8,128)(2,1)S(1)}, u32[]{:S(2)}, u32[]{:S(2)}) %collective-permute-start.5) | collective-permute-done | bytes 393248 | tf_op jit(solution)/shard_map/ppermute | solution.py:120
  23.4 1.1 %collective-permute-start.12 = (bf16[128,512]{1,0:T(8,128)(2,1)S(1)}, bf16[128,512]{1,0:T(8,128)(2,1)S(1)}, u32[]{:S(2)}, u32[]{:S(2)}) collective-permute-start(bf16[128,512]{1,0:T(8,128)(2,1)S(1)} %collective-permute-done), channel_id=1, source_target_pairs={{0,4},{1,5},{2,6},{3,7},{4,0},{5,1},{6,2},{7,3},{8,12},{9,13},{10,... | collective-permute-start | bytes 393224 | tf_op jit(solution)/shard_map/ppermute | solution.py:120
  24.4 5.4 %collective-permute-done.10.refs_2_.refs_6_ = bf16[256,512]{1,0:T(8,128)(2,1)S(1)} collective-permute-done((bf16[256,512]{1,0:T(8,128)(2,1)S(1)}, bf16[256,512]{1,0:T(8,128)(2,1)S(1)}, u32[]{:S(2)}, u32[]{:S(2)}) %collective-permute-start.10) | collective-permute-done | bytes 262176 | tf_op jit(solution)/shard_map/ppermute | solution.py:120
  29.9 1.5 %collective-permute-start.14 = (bf16[128,1024]{1,0:T(8,128)(2,1)S(1)}, bf16[128,1024]{1,0:T(8,128)(2,1)S(1)}, u32[]{:S(2)}, u32[]{:S(2)}) collective-permute-start(bf16[128,1024]{1,0:T(8,128)(2,1)S(1)} %collective-permute-done.3.k_c.refs_1_), channel_id=1, source_target_pairs={{0,2},{1,3},{2,0},{3,1},{4,6},{5,7},{6,4},{7,5},{8,10},{9,11},{10,... | collective-permute-start | bytes 786440 | tf_op jit(solution)/shard_map/ppermute | solution.py:120
  31.9 1.5 %collective-permute-start.13 = (bf16[128,512]{1,0:T(8,128)(2,1)S(1)}, bf16[128,512]{1,0:T(8,128)(2,1)S(1)}, u32[]{:S(2)}, u32[]{:S(2)}) collective-permute-start(bf16[128,512]{1,0:T(8,128)(2,1)S(1)} %collective-permute-done.12.far), channel_id=1, source_target_pairs={{0,2},{1,3},{2,0},{3,1},{4,6},{5,7},{6,4},{7,5},{8,10},{9,11},{10,... | collective-permute-start | bytes 393224 | tf_op jit(solution)/shard_map/ppermute | solution.py:120
  33.4 1.2 %shard_map.39 = (f32[384,512]{1,0:T(8,128)S(1)}, f32[128,768]{1,0:T(8,128)S(1)}) custom-call(s32[1]{0:T(128)} %bitcast.me_ref, bf16[384,512]{1,0:T(8,128)(2,1)S(1)} %constant_dynamic-update-slice_fusion.near, bf16[384,512]{1,0:T(8,128)(2,1)S(1)} %collective-permute-done.5.near_y, bf16[128,512]{1,0:T(8,128)(2,1)S(1)} %collective-permute-done.6.oc_ref, ...), custom_call_target="tpu_custom_call" | custom-call | flops 603979776 | bytes 3801088 | tf_op jit(solution)/shard_map/pallas_call | solution.py:22
  34.6 4.4 %collective-permute-done.13.far_y = bf16[128,512]{1,0:T(8,128)(2,1)S(1)} collective-permute-done((bf16[128,512]{1,0:T(8,128)(2,1)S(1)}, bf16[128,512]{1,0:T(8,128)(2,1)S(1)}, u32[]{:S(2)}, u32[]{:S(2)}) %collective-permute-start.13) | collective-permute-done | bytes 131104 | tf_op jit(solution)/shard_map/ppermute | solution.py:120
  39.1 1.0 %shard_map.40 = (f32[512,256]{1,0:T(8,128)S(1)}, f32[512,256]{1,0:T(8,128)S(1)}) custom-call(s32[1]{0:T(128)} %bitcast.me_ref, f32[384,512]{1,0:T(8,128)S(1)} %get-tuple-element.35.early, f32[128,768]{1,0:T(8,128)S(1)} %get-tuple-element.36.ready, bf16[384,512]{1,0:T(8,128)(2,1)S(1)} %constant_dynamic-update-slice_fusion.near, ...), custom_call_target="tpu_custom_call" | custom-call | flops 536870912 | bytes 5636096 | tf_op jit(solution)/shard_map/pallas_call | solution.py:22
  40.1 1.9 %collective-permute-done.16.came_ref = f32[512,256]{1,0:T(8,128)S(1)} collective-permute-done((f32[512,256]{1,0:T(8,128)S(1)}, f32[512,256]{1,0:T(8,128)S(1)}, u32[]{:S(2)}, u32[]{:S(2)}) %collective-permute-start.16) | collective-permute-done | bytes 524320 | tf_op jit(solution)/shard_map/ppermute | solution.py:120
  42.0 0.5 shard_map.41
  43.1 2.0 %collective-permute-start.18 = (bf16[64,1024]{1,0:T(8,128)(2,1)S(1)}, bf16[64,1024]{1,0:T(8,128)(2,1)S(1)}, u32[]{:S(2)}, u32[]{:S(2)}) collective-permute-start(bf16[64,1024]{1,0:T(8,128)(2,1)S(1)} %get-tuple-element.43), channel_id=1, source_target_pairs={{0,8},{1,9},{2,10},{3,11},{4,12},{5,13},{6,14},{7,15},{8,0},{9,1},... | collective-permute-start | bytes 393224 | tf_op jit(solution)/shard_map/ppermute | solution.py:120
  45.1 2.0 %collective-permute-start.19 = (bf16[64,1024]{1,0:T(8,128)(2,1)S(1)}, bf16[64,1024]{1,0:T(8,128)(2,1)S(1)}, u32[]{:S(2)}, u32[]{:S(2)}) collective-permute-start(bf16[64,1024]{1,0:T(8,128)(2,1)S(1)} %get-tuple-element.44), channel_id=1, source_target_pairs={{0,12},{1,13},{2,14},{3,15},{4,8},{5,9},{6,10},{7,11},{8,4},{9,5},... | collective-permute-start | bytes 393224 | tf_op jit(solution)/shard_map/ppermute | solution.py:120
  47.0 3.0 %collective-permute-done.17 = bf16[64,1024]{1,0:T(8,128)(2,1)S(1)} collective-permute-done((bf16[64,1024]{1,0:T(8,128)(2,1)S(1)}, bf16[64,1024]{1,0:T(8,128)(2,1)S(1)}, u32[]{:S(2)}, u32[]{:S(2)}) %collective-permute-start.17) | collective-permute-done | bytes 131104 | tf_op jit(solution)/shard_map/ppermute | solution.py:120
  50.0 6.0 %collective-permute-done.18 = bf16[64,1024]{1,0:T(8,128)(2,1)S(1)} collective-permute-done((bf16[64,1024]{1,0:T(8,128)(2,1)S(1)}, bf16[64,1024]{1,0:T(8,128)(2,1)S(1)}, u32[]{:S(2)}, u32[]{:S(2)}) %collective-permute-start.18) | collective-permute-done | bytes 131104 | tf_op jit(solution)/shard_map/ppermute | solution.py:120
  56.0 0.8 %add_bitcast_fusion = f32[1024,64]{0,1:T(8,128)} fusion(bf16[64,1024]{1,0:T(8,128)(2,1)S(1)} %collective-permute-done.19, bf16[64,1024]{1,0:T(8,128)(2,1)S(1)} %collective-permute-done.18, f32[64,1024]{1,0:T(8,128)S(1)} %get-tuple-element.41, bf16[64,1024]{1,0:T(8,128)(2,1)S(1)} %collective-permute-done.17), kind=kLoop, calls=%fused_computation | loop fusion | flops 393216 | bytes 917504 | tf_op jit(solution)/shard_map/transpose | solution.py:195
  (32 shorter events, 3.2 us)
Async XLA Ops:
  0.0 10.7 %collective-permute-start = (bf16[128,512]{1,0:T(8,128)(2,1)}, bf16[128,512]{1,0:T(8,128)(2,1)S(1)}, u32[]{:S(2)}, u32[]{:S(2)}) collective-permute-start(bf16[128,512]{1,0:T(8,128)(2,1)} %param.3), channel_id=1, source_target_pairs={{0,8},{1,9},{2,10},{3,11},{4,12},{5,13},{6,14},{7,15},{8,0},{9,1},... | collective-permute-start | bytes 393224 | tf_op jit(solution)/shard_map/ppermute | solution.py:120
  4.0 6.8 %collective-permute-start.1 = (bf16[128,512]{1,0:T(8,128)(2,1)}, bf16[128,512]{1,0:T(8,128)(2,1)S(1)}, u32[]{:S(2)}, u32[]{:S(2)}) collective-permute-start(bf16[128,512]{1,0:T(8,128)(2,1)} %param.3), channel_id=1, source_target_pairs={{0,4},{1,5},{2,6},{3,7},{4,0},{5,1},{6,2},{7,3},{8,12},{9,13},{10,... | collective-permute-start | bytes 393224 | tf_op jit(solution)/shard_map/ppermute | solution.py:120
  5.6 11.8 %collective-permute-start.7 = (bf16[128,1024]{1,0:T(8,128)(2,1)}, bf16[128,1024]{1,0:T(8,128)(2,1)S(1)}, u32[]{:S(2)}, u32[]{:S(2)}) collective-permute-start(bf16[128,1024]{1,0:T(8,128)(2,1)} %b0.1), channel_id=1, source_target_pairs={{0,1},{1,0},{2,3},{3,2},{4,5},{5,4},{6,7},{7,6},{8,9},{9,8},{10,11... | collective-permute-start | bytes 786440 | tf_op jit(solution)/shard_map/ppermute | solution.py:120
  5.6 9.3 %collective-permute-start.2 = (bf16[128,1024]{1,0:T(8,128)(2,1)}, bf16[128,1024]{1,0:T(8,128)(2,1)S(1)}, u32[]{:S(2)}, u32[]{:S(2)}) collective-permute-start(bf16[128,1024]{1,0:T(8,128)(2,1)} %b0.1), channel_id=1, source_target_pairs={{0,2},{1,3},{2,0},{3,1},{4,6},{5,7},{6,4},{7,5},{8,10},{9,11},{10,... | collective-permute-start | bytes 786440 | tf_op jit(solution)/shard_map/ppermute | solution.py:120
  7.1 1.0 %copy-start = (bf16[128,2048]{1,0:T(8,128)(2,1)S(1)}, bf16[128,2048]{1,0:T(8,128)(2,1)}, u32[]{:S(2)}) copy-start(bf16[128,2048]{1,0:T(8,128)(2,1)} %k_ref.1) | copy-start | bytes 1572868
  8.2 0.9 %copy-start.2 = (bf16[128,512]{1,0:T(8,128)(2,1)S(1)}, bf16[128,512]{1,0:T(8,128)(2,1)}, u32[]{:S(2)}) copy-start(bf16[128,512]{1,0:T(8,128)(2,1)} %param.3) | copy-start | bytes 393220
  8.3 6.6 %collective-permute-start.3 = (bf16[128,1024]{1,0:T(8,128)(2,1)S(1)}, bf16[128,1024]{1,0:T(8,128)(2,1)S(1)}, u32[]{:S(2)}, u32[]{:S(2)}) collective-permute-start(bf16[128,1024]{1,0:T(8,128)(2,1)S(1)} %get-tuple-element.25), channel_id=1, source_target_pairs={{0,1},{1,0},{2,3},{3,2},{4,5},{5,4},{6,7},{7,6},{8,9},{9,8},{10,11... | collective-permute-start | bytes 786440 | tf_op jit(solution)/shard_map/ppermute | solution.py:120
  9.1 5.8 %copy-start.1 = (bf16[128,1024]{1,0:T(8,128)(2,1)S(1)}, bf16[128,1024]{1,0:T(8,128)(2,1)}, u32[]{:S(2)}) copy-start(bf16[128,1024]{1,0:T(8,128)(2,1)} %b0.1) | copy-start | bytes 786436
  10.9 12.5 %collective-permute-start.5 = (bf16[384,512]{1,0:T(8,128)(2,1)S(1)}, bf16[384,512]{1,0:T(8,128)(2,1)S(1)}, u32[]{:S(2)}, u32[]{:S(2)}) collective-permute-start(bf16[384,512]{1,0:T(8,128)(2,1)S(1)} %constant_dynamic-update-slice_fusion.near), channel_id=1, source_target_pairs={{0,2},{1,3},{2,0},{3,1},{4,6},{5,7},{6,4},{7,5},{8,10},{9,11},{10,... | collective-permute-start | bytes 1179656 | tf_op jit(solution)/shard_map/ppermute | solution.py:120
  12.5 4.3 %collective-permute-start.6 = (bf16[128,512]{1,0:T(8,128)(2,1)S(1)}, bf16[128,512]{1,0:T(8,128)(2,1)S(1)}, u32[]{:S(2)}, u32[]{:S(2)}) collective-permute-start(bf16[128,512]{1,0:T(8,128)(2,1)S(1)} %copy-done.2), channel_id=1, source_target_pairs={{0,1},{1,0},{2,3},{3,2},{4,5},{5,4},{6,7},{7,6},{8,9},{9,8},{10,11... | collective-permute-start | bytes 393224 | tf_op jit(solution)/shard_map/ppermute | solution.py:120
  15.4 14.5 %collective-permute-start.10 = (bf16[256,512]{1,0:T(8,128)(2,1)S(1)}, bf16[256,512]{1,0:T(8,128)(2,1)S(1)}, u32[]{:S(2)}, u32[]{:S(2)}) collective-permute-start(bf16[256,512]{1,0:T(8,128)(2,1)S(1)} %shard_map.38.refs_0_.refs_4_), channel_id=1, source_target_pairs={{0,4},{1,5},{2,6},{3,7},{4,0},{5,1},{6,2},{7,3},{8,12},{9,13},{10,... | collective-permute-start | bytes 786440 | tf_op jit(solution)/shard_map/ppermute | solution.py:120
  15.9 15.5 %collective-permute-start.9 = (bf16[256,512]{1,0:T(8,128)(2,1)S(1)}, bf16[256,512]{1,0:T(8,128)(2,1)S(1)}, u32[]{:S(2)}, u32[]{:S(2)}) collective-permute-start(bf16[256,512]{1,0:T(8,128)(2,1)S(1)} %shard_map.38.refs_0_.refs_4_), channel_id=1, source_target_pairs={{0,8},{1,9},{2,10},{3,11},{4,12},{5,13},{6,14},{7,15},{8,0},{9,1},... | collective-permute-start | bytes 786440 | tf_op jit(solution)/shard_map/ppermute | solution.py:120
  16.8 14.6 %collective-permute-start.4 = (bf16[128,1024]{1,0:T(8,128)(2,1)S(1)}, bf16[128,1024]{1,0:T(8,128)(2,1)S(1)}, u32[]{:S(2)}, u32[]{:S(2)}) collective-permute-start(bf16[128,1024]{1,0:T(8,128)(2,1)S(1)} %get-tuple-element.27.k_keep.refs_0_), channel_id=1, source_target_pairs={{0,2},{1,3},{2,0},{3,1},{4,6},{5,7},{6,4},{7,5},{8,10},{9,11},{10,... | collective-permute-start | bytes 786440 | tf_op jit(solution)/shard_map/ppermute | solution.py:120
  17.4 14.0 %collective-permute-start.8 = (bf16[128,1024]{1,0:T(8,128)(2,1)S(1)}, bf16[128,1024]{1,0:T(8,128)(2,1)S(1)}, u32[]{:S(2)}, u32[]{:S(2)}) collective-permute-start(bf16[128,1024]{1,0:T(8,128)(2,1)S(1)} %collective-permute-done.2.y_ref.b2), channel_id=1, source_target_pairs={{0,1},{1,0},{2,3},{3,2},{4,5},{5,4},{6,7},{7,6},{8,9},{9,8},{10,11... | collective-permute-start | bytes 786440 | tf_op jit(solution)/shard_map/ppermute | solution.py:120
  23.4 8.5 %collective-permute-start.12 = (bf16[128,512]{1,0:T(8,128)(2,1)S(1)}, bf16[128,512]{1,0:T(8,128)(2,1)S(1)}, u32[]{:S(2)}, u32[]{:S(2)}) collective-permute-start(bf16[128,512]{1,0:T(8,128)(2,1)S(1)} %collective-permute-done), channel_id=1, source_target_pairs={{0,4},{1,5},{2,6},{3,7},{4,0},{5,1},{6,2},{7,3},{8,12},{9,13},{10,... | collective-permute-start | bytes 393224 | tf_op jit(solution)/shard_map/ppermute | solution.py:120
  29.9 9.2 %collective-permute-start.14 = (bf16[128,1024]{1,0:T(8,128)(2,1)S(1)}, bf16[128,1024]{1,0:T(8,128)(2,1)S(1)}, u32[]{:S(2)}, u32[]{:S(2)}) collective-permute-start(bf16[128,1024]{1,0:T(8,128)(2,1)S(1)} %collective-permute-done.3.k_c.refs_1_), channel_id=1, source_target_pairs={{0,2},{1,3},{2,0},{3,1},{4,6},{5,7},{6,4},{7,5},{8,10},{9,11},{10,... | collective-permute-start | bytes 786440 | tf_op jit(solution)/shard_map/ppermute | solution.py:120
  31.4 7.7 %collective-permute-start.15 = (bf16[256,512]{1,0:T(8,128)(2,1)S(1)}, bf16[256,512]{1,0:T(8,128)(2,1)S(1)}, u32[]{:S(2)}, u32[]{:S(2)}) collective-permute-start(bf16[256,512]{1,0:T(8,128)(2,1)S(1)} %collective-permute-done.9.refs_1_.refs_5_), channel_id=1, source_target_pairs={{0,4},{1,5},{2,6},{3,7},{4,0},{5,1},{6,2},{7,3},{8,12},{9,13},{10,... | collective-permute-start | bytes 786440 | tf_op jit(solution)/shard_map/ppermute | solution.py:120
  31.5 1.9 %collective-permute-start.11 = (bf16[128,512]{1,0:T(8,128)(2,1)S(1)}, bf16[128,512]{1,0:T(8,128)(2,1)S(1)}, u32[]{:S(2)}, u32[]{:S(2)}) collective-permute-start(bf16[128,512]{1,0:T(8,128)(2,1)S(1)} %slice.3), channel_id=1, source_target_pairs={{0,1},{1,0},{2,3},{3,2},{4,5},{5,4},{6,7},{7,6},{8,9},{9,8},{10,11... | collective-permute-start | bytes 393224 | tf_op jit(solution)/shard_map/ppermute | solution.py:120
  31.9 7.1 %collective-permute-start.13 = (bf16[128,512]{1,0:T(8,128)(2,1)S(1)}, bf16[128,512]{1,0:T(8,128)(2,1)S(1)}, u32[]{:S(2)}, u32[]{:S(2)}) collective-permute-start(bf16[128,512]{1,0:T(8,128)(2,1)S(1)} %collective-permute-done.12.far), channel_id=1, source_target_pairs={{0,2},{1,3},{2,0},{3,1},{4,6},{5,7},{6,4},{7,5},{8,10},{9,11},{10,... | collective-permute-start | bytes 393224 | tf_op jit(solution)/shard_map/ppermute | solution.py:120
  40.1 2.0 %collective-permute-start.16 = (f32[512,256]{1,0:T(8,128)S(1)}, f32[512,256]{1,0:T(8,128)S(1)}, u32[]{:S(2)}, u32[]{:S(2)}) collective-permute-start(f32[512,256]{1,0:T(8,128)S(1)} %get-tuple-element.38), channel_id=1, source_target_pairs={{0,1},{1,0},{2,3},{3,2},{4,5},{5,4},{6,7},{7,6},{8,9},{9,8},{10,11... | collective-permute-start | bytes 1572872 | tf_op jit(solution)/shard_map/ppermute | solution.py:120
  42.6 7.4 %collective-permute-start.17 = (bf16[64,1024]{1,0:T(8,128)(2,1)S(1)}, bf16[64,1024]{1,0:T(8,128)(2,1)S(1)}, u32[]{:S(2)}, u32[]{:S(2)}) collective-permute-start(bf16[64,1024]{1,0:T(8,128)(2,1)S(1)} %get-tuple-element.42), channel_id=1, source_target_pairs={{0,4},{1,5},{2,6},{3,7},{4,0},{5,1},{6,2},{7,3},{8,12},{9,13},{10,... | collective-permute-start | bytes 393224 | tf_op jit(solution)/shard_map/ppermute | solution.py:120
  43.1 12.9 %collective-permute-start.18 = (bf16[64,1024]{1,0:T(8,128)(2,1)S(1)}, bf16[64,1024]{1,0:T(8,128)(2,1)S(1)}, u32[]{:S(2)}, u32[]{:S(2)}) collective-permute-start(bf16[64,1024]{1,0:T(8,128)(2,1)S(1)} %get-tuple-element.43), channel_id=1, source_target_pairs={{0,8},{1,9},{2,10},{3,11},{4,12},{5,13},{6,14},{7,15},{8,0},{9,1},... | collective-permute-start | bytes 393224 | tf_op jit(solution)/shard_map/ppermute | solution.py:120
  45.1 10.9 %collective-permute-start.19 = (bf16[64,1024]{1,0:T(8,128)(2,1)S(1)}, bf16[64,1024]{1,0:T(8,128)(2,1)S(1)}, u32[]{:S(2)}, u32[]{:S(2)}) collective-permute-start(bf16[64,1024]{1,0:T(8,128)(2,1)S(1)} %get-tuple-element.44), channel_id=1, source_target_pairs={{0,12},{1,13},{2,14},{3,15},{4,8},{5,9},{6,10},{7,11},{8,4},{9,5},... | collective-permute-start | bytes 393224 | tf_op jit(solution)/shard_map/ppermute | solution.py:120

commit v7 on v5

--- a/solution.py
+++ b/solution.py
@@ -139,7 +139,7 @@
     k_keep, k_send = call(part_kernel, (half, half), where, (kernel,), 0)
     b_y, k_c = swap(basis, 2), swap(k_send, 1)
     o_hops = first_hops(orbitals)
-    b_y, k_c, k_keep = barrier((b_y, k_c, k_keep))
+    b_y, k_keep = barrier((b_y, k_keep))
     (x,) = call(
         functools.partial(pick_kernel, width),
         (jax.ShapeDtypeStruct((2 * rows, 2 * share), BF16),),

time: 56.3 us -> 55.8 us (level)
  waiting for transfers between devices: 30.3 us -> 29.4 us
    ppermute x20, waiting for transfers between devices: 30.3 us -> 29.4 us  [swap(): return lax.ppermute(a, 'row', [(i, i ^ bit) for i in range(n)])]
    unnamed x8 -> x6, local copies, waits for them, and re-layouts: 1.53 us -> 1.96 us
  transfers between devices with their start and end apart: 20 -> 20, of which waited for: 10 -> 10; matrix products, arithmetic and copies ran while one was open for 0% -> 2% of each run, Pallas kernels for 3% -> 3%
where the time goes in v7:
time: 55.8 us; the launch traced here: 55.6 us
  waiting for transfers between devices  29.4 us (53%)
  starting transfers between devices  19.8 us (35%)
  Pallas kernels  3.51 us (6%)
  local copies, waits for them, and re-layouts  1.98 us (4%)
  other arithmetic  0.76 us (1%)
    ppermute x20, waiting for transfers between devices, swap(): return lax.ppermute(a, 'row', [(i, i ^ bit) for i in range(n)])  29.4 us
    ppermute x20, starting transfers between devices, swap(): return lax.ppermute(a, 'row', [(i, i ^ bit) for i in range(n)])  19.8 us
    pallas_call x5, Pallas kernels, call(): pl.pallas_call(body, out_shape=list(outs), in_specs=[pl.BlockSpec(memory_...  3.51 us
    unnamed x6, local copies, waits for them, and re-layouts  1.96 us
  transfers between devices with their start and end apart: 20, of which 10 were waited for; matrix products, arithmetic and copies ran while one was open for 2% of the time, Pallas kernels for 3%

profile of v7, /device:TPU:0, one launch (start us, length us, event | category | flops | bytes accessed | tf_op | source)
XLA Modules:
  0.0 55.6 jit_solution(17851752179118284230)
XLA Ops:
  0.0 4.0 %collective-permute-start = (bf16[128,512]{1,0:T(8,128)(2,1)}, bf16[128,512]{1,0:T(8,128)(2,1)S(1)}, u32[]{:S(2)}, u32[]{:S(2)}) collective-permute-start(bf16[128,512]{1,0:T(8,128)(2,1)} %param.3), channel_id=1, source_target_pairs={{0,8},{1,9},{2,10},{3,11},{4,12},{5,13},{6,14},{7,15},{8,0},{9,1},... | collective-permute-start | bytes 393224 | tf_op jit(solution)/shard_map/ppermute | solution.py:117
  4.0 1.6 %collective-permute-start.1 = (bf16[128,512]{1,0:T(8,128)(2,1)}, bf16[128,512]{1,0:T(8,128)(2,1)S(1)}, u32[]{:S(2)}, u32[]{:S(2)}) collective-permute-start(bf16[128,512]{1,0:T(8,128)(2,1)} %param.3), channel_id=1, source_target_pairs={{0,4},{1,5},{2,6},{3,7},{4,0},{5,1},{6,2},{7,3},{8,12},{9,13},{10,... | collective-permute-start | bytes 393224 | tf_op jit(solution)/shard_map/ppermute | solution.py:117
  6.1 1.5 %collective-permute-start.2 = (bf16[128,1024]{1,0:T(8,128)(2,1)}, bf16[128,1024]{1,0:T(8,128)(2,1)S(1)}, u32[]{:S(2)}, u32[]{:S(2)}) collective-permute-start(bf16[128,1024]{1,0:T(8,128)(2,1)} %b0.1), channel_id=1, source_target_pairs={{0,2},{1,3},{2,0},{3,1},{4,6},{5,7},{6,4},{7,5},{8,10},{9,11},{10,... | collective-permute-start | bytes 786440 | tf_op jit(solution)/shard_map/ppermute | solution.py:117
  7.6 0.9 %constant_dynamic-update-slice_fusion.2 = bf16[384,512]{1,0:T(8,128)(2,1)S(1)} fusion(bf16[128,512]{1,0:T(8,128)(2,1)} %param.3), kind=kLoop, calls=%fused_computation.3 | loop fusion | bytes 262144
  8.6 1.0 %copy-done = bf16[128,2048]{1,0:T(8,128)(2,1)S(1)} copy-done((bf16[128,2048]{1,0:T(8,128)(2,1)S(1)}, bf16[128,2048]{1,0:T(8,128)(2,1)}, u32[]{:S(2)}) %copy-start) | copy-done | bytes 524312
  9.8 0.9 %collective-permute-done = bf16[128,512]{1,0:T(8,128)(2,1)S(1)} collective-permute-done((bf16[128,512]{1,0:T(8,128)(2,1)}, bf16[128,512]{1,0:T(8,128)(2,1)S(1)}, u32[]{:S(2)}, u32[]{:S(2)}) %collective-permute-start) | collective-permute-done | bytes 131104 | tf_op jit(solution)/shard_map/ppermute | solution.py:117
  10.9 1.6 %collective-permute-start.4 = (bf16[384,512]{1,0:T(8,128)(2,1)S(1)}, bf16[384,512]{1,0:T(8,128)(2,1)S(1)}, u32[]{:S(2)}, u32[]{:S(2)}) collective-permute-start(bf16[384,512]{1,0:T(8,128)(2,1)S(1)} %constant_dynamic-update-slice_fusion.near), channel_id=1, source_target_pairs={{0,2},{1,3},{2,0},{3,1},{4,6},{5,7},{6,4},{7,5},{8,10},{9,11},{10,... | collective-permute-start | bytes 1179656 | tf_op jit(solution)/shard_map/ppermute | solution.py:117
  12.5 2.6 %collective-permute-done.2.y_ref.b2 = bf16[128,1024]{1,0:T(8,128)(2,1)S(1)} collective-permute-done((bf16[128,1024]{1,0:T(8,128)(2,1)}, bf16[128,1024]{1,0:T(8,128)(2,1)S(1)}, u32[]{:S(2)}, u32[]{:S(2)}) %collective-permute-start.2) | collective-permute-done | bytes 262176 | tf_op jit(solution)/shard_map/ppermute | solution.py:117
  15.9 1.0 %collective-permute-start.8 = (bf16[256,512]{1,0:T(8,128)(2,1)S(1)}, bf16[256,512]{1,0:T(8,128)(2,1)S(1)}, u32[]{:S(2)}, u32[]{:S(2)}) collective-permute-start(bf16[256,512]{1,0:T(8,128)(2,1)S(1)} %shard_map.38.refs_0_.refs_4_), channel_id=1, source_target_pairs={{0,8},{1,9},{2,10},{3,11},{4,12},{5,13},{6,14},{7,15},{8,0},{9,1},... | collective-permute-start | bytes 786440 | tf_op jit(solution)/shard_map/ppermute | solution.py:117
  16.8 0.8 %collective-permute-start.3 = (bf16[128,1024]{1,0:T(8,128)(2,1)S(1)}, bf16[128,1024]{1,0:T(8,128)(2,1)S(1)}, u32[]{:S(2)}, u32[]{:S(2)}) collective-permute-start(bf16[128,1024]{1,0:T(8,128)(2,1)S(1)} %get-tuple-element.23.k_keep.refs_0_), channel_id=1, source_target_pairs={{0,2},{1,3},{2,0},{3,1},{4,6},{5,7},{6,4},{7,5},{8,10},{9,11},{10,... | collective-permute-start | bytes 786440 | tf_op jit(solution)/shard_map/ppermute | solution.py:117
  17.7 5.9 %collective-permute-done.4.near_y = bf16[384,512]{1,0:T(8,128)(2,1)S(1)} collective-permute-done((bf16[384,512]{1,0:T(8,128)(2,1)S(1)}, bf16[384,512]{1,0:T(8,128)(2,1)S(1)}, u32[]{:S(2)}, u32[]{:S(2)}) %collective-permute-start.4) | collective-permute-done | bytes 393248 | tf_op jit(solution)/shard_map/ppermute | solution.py:117
  23.6 0.8 %collective-permute-start.11 = (bf16[128,512]{1,0:T(8,128)(2,1)S(1)}, bf16[128,512]{1,0:T(8,128)(2,1)S(1)}, u32[]{:S(2)}, u32[]{:S(2)}) collective-permute-start(bf16[128,512]{1,0:T(8,128)(2,1)S(1)} %collective-permute-done), channel_id=1, source_target_pairs={{0,4},{1,5},{2,6},{3,7},{4,0},{5,1},{6,2},{7,3},{8,12},{9,13},{10,... | collective-permute-start | bytes 393224 | tf_op jit(solution)/shard_map/ppermute | solution.py:117
  24.4 4.9 %collective-permute-done.9.refs_2_.refs_6_ = bf16[256,512]{1,0:T(8,128)(2,1)S(1)} collective-permute-done((bf16[256,512]{1,0:T(8,128)(2,1)S(1)}, bf16[256,512]{1,0:T(8,128)(2,1)S(1)}, u32[]{:S(2)}, u32[]{:S(2)}) %collective-permute-start.9) | collective-permute-done | bytes 262176 | tf_op jit(solution)/shard_map/ppermute | solution.py:117
  29.3 1.5 %collective-permute-start.14 = (bf16[128,1024]{1,0:T(8,128)(2,1)S(1)}, bf16[128,1024]{1,0:T(8,128)(2,1)S(1)}, u32[]{:S(2)}, u32[]{:S(2)}) collective-permute-start(bf16[128,1024]{1,0:T(8,128)(2,1)S(1)} %collective-permute-done.10.k_c.refs_1_), channel_id=1, source_target_pairs={{0,2},{1,3},{2,0},{3,1},{4,6},{5,7},{6,4},{7,5},{8,10},{9,11},{10,... | collective-permute-start | bytes 786440 | tf_op jit(solution)/shard_map/ppermute | solution.py:117
  31.0 1.5 %collective-permute-start.12 = (bf16[128,512]{1,0:T(8,128)(2,1)S(1)}, bf16[128,512]{1,0:T(8,128)(2,1)S(1)}, u32[]{:S(2)}, u32[]{:S(2)}) collective-permute-start(bf16[128,512]{1,0:T(8,128)(2,1)S(1)} %collective-permute-done.11.far), channel_id=1, source_target_pairs={{0,2},{1,3},{2,0},{3,1},{4,6},{5,7},{6,4},{7,5},{8,10},{9,11},{10,... | collective-permute-start | bytes 393224 | tf_op jit(solution)/shard_map/ppermute | solution.py:117
  32.5 1.1 %shard_map.39.early = f32[384,512]{1,0:T(8,128)S(1)} custom-call(s32[1]{0:T(128)} %bitcast.me_ref, bf16[384,512]{1,0:T(8,128)(2,1)S(1)} %constant_dynamic-update-slice_fusion.near, bf16[384,512]{1,0:T(8,128)(2,1)S(1)} %collective-permute-done.4.near_y, bf16[128,512]{1,0:T(8,128)(2,1)S(1)} %collective-permute-done.5.oc_ref, ...), custom_call_target="tpu_custom_call" | custom-call | flops 603979776 | bytes 3276800 | tf_op jit(solution)/shard_map/pallas_call | solution.py:22
  33.6 4.3 %collective-permute-done.12.far_y = bf16[128,512]{1,0:T(8,128)(2,1)S(1)} collective-permute-done((bf16[128,512]{1,0:T(8,128)(2,1)S(1)}, bf16[128,512]{1,0:T(8,128)(2,1)S(1)}, u32[]{:S(2)}, u32[]{:S(2)}) %collective-permute-start.12) | collective-permute-done | bytes 131104 | tf_op jit(solution)/shard_map/ppermute | solution.py:117
  38.0 1.3 %shard_map.40 = (f32[512,256]{1,0:T(8,128)S(1)}, f32[512,256]{1,0:T(8,128)S(1)}) custom-call(s32[1]{0:T(128)} %bitcast.me_ref, f32[384,512]{1,0:T(8,128)S(1)} %shard_map.39.early, bf16[384,512]{1,0:T(8,128)(2,1)S(1)} %constant_dynamic-update-slice_fusion.near, bf16[128,512]{1,0:T(8,128)(2,1)S(1)} %collective-permute-done.11.far, ...), custom_call_target="tpu_custom_call" | custom-call | flops 536870912 | bytes 5242880 | tf_op jit(solution)/shard_map/pallas_call | solution.py:22
  39.3 1.9 %collective-permute-done.16.came_ref = f32[512,256]{1,0:T(8,128)S(1)} collective-permute-done((f32[512,256]{1,0:T(8,128)S(1)}, f32[512,256]{1,0:T(8,128)S(1)}, u32[]{:S(2)}, u32[]{:S(2)}) %collective-permute-start.16) | collective-permute-done | bytes 524320 | tf_op jit(solution)/shard_map/ppermute | solution.py:117
  41.8 2.8 %collective-permute-start.18 = (bf16[64,1024]{1,0:T(8,128)(2,1)S(1)}, bf16[64,1024]{1,0:T(8,128)(2,1)S(1)}, u32[]{:S(2)}, u32[]{:S(2)}) collective-permute-start(bf16[64,1024]{1,0:T(8,128)(2,1)S(1)} %get-tuple-element.37), channel_id=1, source_target_pairs={{0,8},{1,9},{2,10},{3,11},{4,12},{5,13},{6,14},{7,15},{8,0},{9,1},... | collective-permute-start | bytes 393224 | tf_op jit(solution)/shard_map/ppermute | solution.py:117
  44.6 1.6 %collective-permute-start.19 = (bf16[64,1024]{1,0:T(8,128)(2,1)S(1)}, bf16[64,1024]{1,0:T(8,128)(2,1)S(1)}, u32[]{:S(2)}, u32[]{:S(2)}) collective-permute-start(bf16[64,1024]{1,0:T(8,128)(2,1)S(1)} %get-tuple-element.38), channel_id=1, source_target_pairs={{0,12},{1,13},{2,14},{3,15},{4,8},{5,9},{6,10},{7,11},{8,4},{9,5},... | collective-permute-start | bytes 393224 | tf_op jit(solution)/shard_map/ppermute | solution.py:117
  46.2 3.3 %collective-permute-done.17 = bf16[64,1024]{1,0:T(8,128)(2,1)S(1)} collective-permute-done((bf16[64,1024]{1,0:T(8,128)(2,1)S(1)}, bf16[64,1024]{1,0:T(8,128)(2,1)S(1)}, u32[]{:S(2)}, u32[]{:S(2)}) %collective-permute-start.17) | collective-permute-done | bytes 131104 | tf_op jit(solution)/shard_map/ppermute | solution.py:117
  49.6 5.2 %collective-permute-done.18 = bf16[64,1024]{1,0:T(8,128)(2,1)S(1)} collective-permute-done((bf16[64,1024]{1,0:T(8,128)(2,1)S(1)}, bf16[64,1024]{1,0:T(8,128)(2,1)S(1)}, u32[]{:S(2)}, u32[]{:S(2)}) %collective-permute-start.18) | collective-permute-done | bytes 131104 | tf_op jit(solution)/shard_map/ppermute | solution.py:117
  54.8 0.8 %add_bitcast_fusion = f32[1024,64]{0,1:T(8,128)} fusion(bf16[64,1024]{1,0:T(8,128)(2,1)S(1)} %collective-permute-done.19, bf16[64,1024]{1,0:T(8,128)(2,1)S(1)} %collective-permute-done.18, f32[64,1024]{1,0:T(8,128)S(1)} %get-tuple-element.35, bf16[64,1024]{1,0:T(8,128)(2,1)S(1)} %collective-permute-done.17), kind=kLoop, calls=%fused_computation | loop fusion | flops 393216 | bytes 917504 | tf_op jit(solution)/shard_map/transpose | solution.py:189
  (30 shorter events, 2.5 us)
Async XLA Ops:
  0.0 10.7 %collective-permute-start = (bf16[128,512]{1,0:T(8,128)(2,1)}, bf16[128,512]{1,0:T(8,128)(2,1)S(1)}, u32[]{:S(2)}, u32[]{:S(2)}) collective-permute-start(bf16[128,512]{1,0:T(8,128)(2,1)} %param.3), channel_id=1, source_target_pairs={{0,8},{1,9},{2,10},{3,11},{4,12},{5,13},{6,14},{7,15},{8,0},{9,1},... | collective-permute-start | bytes 393224 | tf_op jit(solution)/shard_map/ppermute | solution.py:117
  4.0 6.8 %collective-permute-start.1 = (bf16[128,512]{1,0:T(8,128)(2,1)}, bf16[128,512]{1,0:T(8,128)(2,1)S(1)}, u32[]{:S(2)}, u32[]{:S(2)}) collective-permute-start(bf16[128,512]{1,0:T(8,128)(2,1)} %param.3), channel_id=1, source_target_pairs={{0,4},{1,5},{2,6},{3,7},{4,0},{5,1},{6,2},{7,3},{8,12},{9,13},{10,... | collective-permute-start | bytes 393224 | tf_op jit(solution)/shard_map/ppermute | solution.py:117
  5.6 10.3 %collective-permute-start.5 = (bf16[128,512]{1,0:T(8,128)(2,1)}, bf16[128,512]{1,0:T(8,128)(2,1)S(1)}, u32[]{:S(2)}, u32[]{:S(2)}) collective-permute-start(bf16[128,512]{1,0:T(8,128)(2,1)} %param.3), channel_id=1, source_target_pairs={{0,1},{1,0},{2,3},{3,2},{4,5},{5,4},{6,7},{7,6},{8,9},{9,8},{10,11... | collective-permute-start | bytes 393224 | tf_op jit(solution)/shard_map/ppermute | solution.py:117
  5.6 11.2 %collective-permute-start.6 = (bf16[128,1024]{1,0:T(8,128)(2,1)}, bf16[128,1024]{1,0:T(8,128)(2,1)S(1)}, u32[]{:S(2)}, u32[]{:S(2)}) collective-permute-start(bf16[128,1024]{1,0:T(8,128)(2,1)} %b0.1), channel_id=1, source_target_pairs={{0,1},{1,0},{2,3},{3,2},{4,5},{5,4},{6,7},{7,6},{8,9},{9,8},{10,11... | collective-permute-start | bytes 786440 | tf_op jit(solution)/shard_map/ppermute | solution.py:117
  6.1 9.0 %collective-permute-start.2 = (bf16[128,1024]{1,0:T(8,128)(2,1)}, bf16[128,1024]{1,0:T(8,128)(2,1)S(1)}, u32[]{:S(2)}, u32[]{:S(2)}) collective-permute-start(bf16[128,1024]{1,0:T(8,128)(2,1)} %b0.1), channel_id=1, source_target_pairs={{0,2},{1,3},{2,0},{3,1},{4,6},{5,7},{6,4},{7,5},{8,10},{9,11},{10,... | collective-permute-start | bytes 786440 | tf_op jit(solution)/shard_map/ppermute | solution.py:117
  8.6 1.0 %copy-start = (bf16[128,2048]{1,0:T(8,128)(2,1)S(1)}, bf16[128,2048]{1,0:T(8,128)(2,1)}, u32[]{:S(2)}) copy-start(bf16[128,2048]{1,0:T(8,128)(2,1)} %k_ref.1) | copy-start | bytes 1572868
  10.7 4.5 %copy-start.1 = (bf16[128,1024]{1,0:T(8,128)(2,1)S(1)}, bf16[128,1024]{1,0:T(8,128)(2,1)}, u32[]{:S(2)}) copy-start(bf16[128,1024]{1,0:T(8,128)(2,1)} %b0.1) | copy-start | bytes 786436
  10.7 7.0 %collective-permute-start.10 = (bf16[128,1024]{1,0:T(8,128)(2,1)S(1)}, bf16[128,1024]{1,0:T(8,128)(2,1)S(1)}, u32[]{:S(2)}, u32[]{:S(2)}) collective-permute-start(bf16[128,1024]{1,0:T(8,128)(2,1)S(1)} %get-tuple-element.27), channel_id=1, source_target_pairs={{0,1},{1,0},{2,3},{3,2},{4,5},{5,4},{6,7},{7,6},{8,9},{9,8},{10,11... | collective-permute-start | bytes 786440 | tf_op jit(solution)/shard_map/ppermute | solution.py:117
  10.9 12.7 %collective-permute-start.4 = (bf16[384,512]{1,0:T(8,128)(2,1)S(1)}, bf16[384,512]{1,0:T(8,128)(2,1)S(1)}, u32[]{:S(2)}, u32[]{:S(2)}) collective-permute-start(bf16[384,512]{1,0:T(8,128)(2,1)S(1)} %constant_dynamic-update-slice_fusion.near), channel_id=1, source_target_pairs={{0,2},{1,3},{2,0},{3,1},{4,6},{5,7},{6,4},{7,5},{8,10},{9,11},{10,... | collective-permute-start | bytes 1179656 | tf_op jit(solution)/shard_map/ppermute | solution.py:117
  15.6 13.7 %collective-permute-start.9 = (bf16[256,512]{1,0:T(8,128)(2,1)S(1)}, bf16[256,512]{1,0:T(8,128)(2,1)S(1)}, u32[]{:S(2)}, u32[]{:S(2)}) collective-permute-start(bf16[256,512]{1,0:T(8,128)(2,1)S(1)} %shard_map.38.refs_0_.refs_4_), channel_id=1, source_target_pairs={{0,4},{1,5},{2,6},{3,7},{4,0},{5,1},{6,2},{7,3},{8,12},{9,13},{10,... | collective-permute-start | bytes 786440 | tf_op jit(solution)/shard_map/ppermute | solution.py:117
  15.9 15.0 %collective-permute-start.8 = (bf16[256,512]{1,0:T(8,128)(2,1)S(1)}, bf16[256,512]{1,0:T(8,128)(2,1)S(1)}, u32[]{:S(2)}, u32[]{:S(2)}) collective-permute-start(bf16[256,512]{1,0:T(8,128)(2,1)S(1)} %shard_map.38.refs_0_.refs_4_), channel_id=1, source_target_pairs={{0,8},{1,9},{2,10},{3,11},{4,12},{5,13},{6,14},{7,15},{8,0},{9,1},... | collective-permute-start | bytes 786440 | tf_op jit(solution)/shard_map/ppermute | solution.py:117
  16.8 14.0 %collective-permute-start.3 = (bf16[128,1024]{1,0:T(8,128)(2,1)S(1)}, bf16[128,1024]{1,0:T(8,128)(2,1)S(1)}, u32[]{:S(2)}, u32[]{:S(2)}) collective-permute-start(bf16[128,1024]{1,0:T(8,128)(2,1)S(1)} %get-tuple-element.23.k_keep.refs_0_), channel_id=1, source_target_pairs={{0,2},{1,3},{2,0},{3,1},{4,6},{5,7},{6,4},{7,5},{8,10},{9,11},{10,... | collective-permute-start | bytes 786440 | tf_op jit(solution)/shard_map/ppermute | solution.py:117
  17.7 13.2 %collective-permute-start.7 = (bf16[128,1024]{1,0:T(8,128)(2,1)S(1)}, bf16[128,1024]{1,0:T(8,128)(2,1)S(1)}, u32[]{:S(2)}, u32[]{:S(2)}) collective-permute-start(bf16[128,1024]{1,0:T(8,128)(2,1)S(1)} %collective-permute-done.2.y_ref.b2), channel_id=1, source_target_pairs={{0,1},{1,0},{2,3},{3,2},{4,5},{5,4},{6,7},{7,6},{8,9},{9,8},{10,11... | collective-permute-start | bytes 786440 | tf_op jit(solution)/shard_map/ppermute | solution.py:117
  23.6 7.4 %collective-permute-start.11 = (bf16[128,512]{1,0:T(8,128)(2,1)S(1)}, bf16[128,512]{1,0:T(8,128)(2,1)S(1)}, u32[]{:S(2)}, u32[]{:S(2)}) collective-permute-start(bf16[128,512]{1,0:T(8,128)(2,1)S(1)} %collective-permute-done), channel_id=1, source_target_pairs={{0,4},{1,5},{2,6},{3,7},{4,0},{5,1},{6,2},{7,3},{8,12},{9,13},{10,... | collective-permute-start | bytes 393224 | tf_op jit(solution)/shard_map/ppermute | solution.py:117
  29.3 8.7 %collective-permute-start.14 = (bf16[128,1024]{1,0:T(8,128)(2,1)S(1)}, bf16[128,1024]{1,0:T(8,128)(2,1)S(1)}, u32[]{:S(2)}, u32[]{:S(2)}) collective-permute-start(bf16[128,1024]{1,0:T(8,128)(2,1)S(1)} %collective-permute-done.10.k_c.refs_1_), channel_id=1, source_target_pairs={{0,2},{1,3},{2,0},{3,1},{4,6},{5,7},{6,4},{7,5},{8,10},{9,11},{10,... | collective-permute-start | bytes 786440 | tf_op jit(solution)/shard_map/ppermute | solution.py:117
  30.8 7.1 %collective-permute-start.15 = (bf16[256,512]{1,0:T(8,128)(2,1)S(1)}, bf16[256,512]{1,0:T(8,128)(2,1)S(1)}, u32[]{:S(2)}, u32[]{:S(2)}) collective-permute-start(bf16[256,512]{1,0:T(8,128)(2,1)S(1)} %collective-permute-done.8.refs_1_.refs_5_), channel_id=1, source_target_pairs={{0,4},{1,5},{2,6},{3,7},{4,0},{5,1},{6,2},{7,3},{8,12},{9,13},{10,... | collective-permute-start | bytes 786440 | tf_op jit(solution)/shard_map/ppermute | solution.py:117
  31.0 7.0 %collective-permute-start.12 = (bf16[128,512]{1,0:T(8,128)(2,1)S(1)}, bf16[128,512]{1,0:T(8,128)(2,1)S(1)}, u32[]{:S(2)}, u32[]{:S(2)}) collective-permute-start(bf16[128,512]{1,0:T(8,128)(2,1)S(1)} %collective-permute-done.11.far), channel_id=1, source_target_pairs={{0,2},{1,3},{2,0},{3,1},{4,6},{5,7},{6,4},{7,5},{8,10},{9,11},{10,... | collective-permute-start | bytes 393224 | tf_op jit(solution)/shard_map/ppermute | solution.py:117
  32.5 5.5 %collective-permute-start.13 = (bf16[128,512]{1,0:T(8,128)(2,1)S(1)}, bf16[128,512]{1,0:T(8,128)(2,1)S(1)}, u32[]{:S(2)}, u32[]{:S(2)}) collective-permute-start(bf16[128,512]{1,0:T(8,128)(2,1)S(1)} %slice.3), channel_id=1, source_target_pairs={{0,1},{1,0},{2,3},{3,2},{4,5},{5,4},{6,7},{7,6},{8,9},{9,8},{10,11... | collective-permute-start | bytes 393224 | tf_op jit(solution)/shard_map/ppermute | solution.py:117
  39.2 2.0 %collective-permute-start.16 = (f32[512,256]{1,0:T(8,128)S(1)}, f32[512,256]{1,0:T(8,128)S(1)}, u32[]{:S(2)}, u32[]{:S(2)}) collective-permute-start(f32[512,256]{1,0:T(8,128)S(1)} %get-tuple-element.32), channel_id=1, source_target_pairs={{0,1},{1,0},{2,3},{3,2},{4,5},{5,4},{6,7},{7,6},{8,9},{9,8},{10,11... | collective-permute-start | bytes 1572872 | tf_op jit(solution)/shard_map/ppermute | solution.py:117
  41.8 7.8 %collective-permute-start.17 = (bf16[64,1024]{1,0:T(8,128)(2,1)S(1)}, bf16[64,1024]{1,0:T(8,128)(2,1)S(1)}, u32[]{:S(2)}, u32[]{:S(2)}) collective-permute-start(bf16[64,1024]{1,0:T(8,128)(2,1)S(1)} %get-tuple-element.36), channel_id=1, source_target_pairs={{0,4},{1,5},{2,6},{3,7},{4,0},{5,1},{6,2},{7,3},{8,12},{9,13},{10,... | collective-permute-start | bytes 393224 | tf_op jit(solution)/shard_map/ppermute | solution.py:117
  41.8 13.0 %collective-permute-start.18 = (bf16[64,1024]{1,0:T(8,128)(2,1)S(1)}, bf16[64,1024]{1,0:T(8,128)(2,1)S(1)}, u32[]{:S(2)}, u32[]{:S(2)}) collective-permute-start(bf16[64,1024]{1,0:T(8,128)(2,1)S(1)} %get-tuple-element.37), channel_id=1, source_target_pairs={{0,8},{1,9},{2,10},{3,11},{4,12},{5,13},{6,14},{7,15},{8,0},{9,1},... | collective-permute-start | bytes 393224 | tf_op jit(solution)/shard_map/ppermute | solution.py:117
  44.6 10.2 %collective-permute-start.19 = (bf16[64,1024]{1,0:T(8,128)(2,1)S(1)}, bf16[64,1024]{1,0:T(8,128)(2,1)S(1)}, u32[]{:S(2)}, u32[]{:S(2)}) collective-permute-start(bf16[64,1024]{1,0:T(8,128)(2,1)S(1)} %get-tuple-element.38), channel_id=1, source_target_pairs={{0,12},{1,13},{2,14},{3,15},{4,8},{5,9},{6,10},{7,11},{8,4},{9,5},... | collective-permute-start | bytes 393224 | tf_op jit(solution)/shard_map/ppermute | solution.py:117
